TPU v7x, 256 devices: a whole 4x4x8 slice. The times are simulated.
256 devices in a mesh: dp: 32 (over z_lo, x, core), tensor: 8 (over y, z_hi).
Axes of the slice: x: 4, y: 4, z: 8 (z_hi: 2, z_lo: 4; z = z_hi * 4 + z_lo), core: 2. Of those that a mesh axis runs over, the one named last changes fastest.
Arguments:
- up_inputs: bfloat16 [32, 256, 8192], P('dp', None, 'tensor'), may hold values from -6 to 6
- up_grads: bfloat16 [32, 256, 28672], P('dp', None, 'tensor'), may hold values from -6 to 6
- down_inputs: bfloat16 [32, 256, 28672], P('dp', None, 'tensor'), may hold values from -6 to 6
- down_grads: bfloat16 [32, 256, 8192], P('dp', None, 'tensor'), may hold values from -6 to 6
- up_in_proj: bfloat16 [8192, 64], P('tensor'), may hold values from -0.0625 to 0.0625
- up_out_proj: bfloat16 [28672, 64], P('tensor'), may hold values from -0.03125 to 0.03125
- down_in_proj: bfloat16 [28672, 64], P('tensor'), may hold values from -0.03125 to 0.03125
- down_out_proj: bfloat16 [8192, 64], P('tensor'), may hold values from -0.0625 to 0.0625
- queries: bfloat16 [4096, 8192], P('dp', 'tensor'), may hold values from -0.015625 to 0.015625
Outputs:
- scores: float32 [32, 4096], P(None, 'dp')
All inputs are finite; a program needn't handle non-finite values.
Results may differ from a plain program's by a relative error of at most 0.0029.
Values may be sent and summed in bfloat16 or wider, within the bound.
No kernel may reach another device: no remote copies, remote signals or barrier semaphores. Data moves between devices by JAX's collectives and lax.ppermute only.
A program may use at most 64 MiB of HBM per device.

v0:
```python
import jax
import jax.numpy as jnp
from jax import lax
from jax.sharding import PartitionSpec as P


def project_rows(acts, proj):
    ex, seq, wid = acts.shape
    return jnp.dot(acts.reshape(ex * seq, wid), proj, preferred_element_type=jnp.float32).reshape(
        ex, seq, -1
    )


def outer_pair(stacked, rank_size):
    up_in = stacked[:, :, 0:rank_size]
    up_out = stacked[:, :, rank_size : 2 * rank_size]
    down_in = stacked[:, :, 2 * rank_size : 3 * rank_size]
    down_out = stacked[:, :, 3 * rank_size : 4 * rank_size]
    first = jnp.einsum("esr,esc->erc", up_out, up_in, precision=lax.Precision.HIGHEST)
    second = jnp.einsum("esr,esc->erc", down_out, down_in, precision=lax.Precision.HIGHEST)
    ex = stacked.shape[0]
    return jnp.concatenate([first.reshape(ex, -1), second.reshape(ex, -1)], axis=1)


def per_device(
    up_inputs,
    up_grads,
    down_inputs,
    down_grads,
    up_in_proj,
    up_out_proj,
    down_in_proj,
    down_out_proj,
    queries,
):
    rank_size = up_in_proj.shape[1]
    partial_proj = jnp.concatenate(
        [
            project_rows(up_inputs, up_in_proj),
            project_rows(up_grads, up_out_proj),
            project_rows(down_inputs, down_in_proj),
            project_rows(down_grads, down_out_proj),
        ],
        axis=2,
    )
    summed_proj = lax.psum(partial_proj, "tensor")
    full_grads = outer_pair(summed_proj, rank_size)
    col_width = full_grads.shape[1] // lax.axis_size("tensor")
    own_slice = lax.dynamic_slice_in_dim(
        full_grads, lax.axis_index("tensor") * col_width, col_width, 1
    )
    packed = own_slice.astype(jnp.bfloat16)
    partial_scores = lax.dot_general(
        packed,
        lax.all_gather(queries, "dp", axis=0, tiled=True),
        (((1,), (1,)), ((), ())),
        preferred_element_type=jnp.float32,
    )
    summed_scores = lax.psum(partial_scores, "tensor")
    return lax.all_to_all(summed_scores, "dp", split_axis=1, concat_axis=0, tiled=True)


def solution(mesh):
    placed = (
        P("dp", None, "tensor"),
        P("dp", None, "tensor"),
        P("dp", None, "tensor"),
        P("dp", None, "tensor"),
        P("tensor", None),
        P("tensor", None),
        P("tensor", None),
        P("tensor", None),
        P("dp", "tensor"),
    )
    return jax.shard_map(
        per_device, mesh=mesh, in_specs=placed, out_specs=P(None, "dp"), check_vma=False
    )
```

profile of v0, /device:TPU:1, one launch (start us, length us, event | category | flops | bytes accessed | tf_op | source)
XLA Modules:
  0.0 209.3 jit_solution(10517124487330967669)
XLA Ops:
  7.4 0.0 copy-start
  7.4 0.0 all-reduce.2.cloned.1.call-start
  7.4 0.0 copy-start.1
  7.4 0.0 copy-start.2
  7.4 1.5 convolution_bitcast_fusion
  8.9 1.4 convolution_bitcast_fusion.1
  10.2 0.0 copy-done
  10.2 1.7 fusion.4
  11.9 0.0 copy-done.1
  11.9 0.0 copy-done.2
  11.9 0.7 fusion.7
  12.6 0.7 pad_maximum_fusion
  13.3 0.0 all-reduce.2.cloned.1.call-update
  13.4 0.0 all-gather.2.cloned.1.call-start
  13.4 0.5 all-gather.2.cloned.1.call-update
  14.0 111.6 %all-reduce.2.cloned.1.call-done = f32[1,256,256]{1,2,0:T(8,128)} async-done(((f32[1,256,256]{1,2,0:T(8,128)}), f32[1,256,256]{1,2,0:T(8,128)}) %all-reduce.2.cloned.1.call-update) | async-done | bytes 262160 | tf_op jit(solution)/shard_map/psum | solution.py:46
  125.6 1.1 fusion.13
  126.6 0.1 reshape.66
  126.7 1.1 fusion.12
  127.8 0.1 reshape.69
  127.9 5.6 %convolution_bitcast_fusion.2 = f32[1,32,128]{2,0,1:T(1,128)S(1)} fusion(bf16[4096,1024]{1,0:T(8,128)(2,1)} %all-gather.2.cloned.1.call-done, s32[]{:T(128)S(6)} %select_n.3, bf16[1,4096]{1,0:T(2,128)(2,1)S(1)} %reshape.66, bf16[1,4096]{1,0:T(2,128)(2,1)S(1)} %reshape.69), kind=kOutput, calls=%fused_computation.8 | convolution fusion | flops 8392704 | bytes 8421380 | tf_op jit(solution)/shard_map/dot_general | solution.py:53
  133.5 41.1 %psum.15 = f32[1,32,128]{2,0,1:T(1,128)S(1)} all-reduce(f32[1,32,128]{2,0,1:T(1,128)S(1)} %convolution_bitcast_fusion.2), channel_id=1, replica_groups=mesh['dp'=32,'tensor'=8] {'tensor'}, use_global_device_ids=true, to_apply=%region_1.0 | all-reduce | flops 4096 | bytes 32768 | tf_op jit(solution)/shard_map/psum | solution.py:59
  174.6 26.6 %all_to_all.16 = f32[1,32,128]{2,0,1:T(1,128)S(1)} all-to-all(f32[1,32,128]{2,0,1:T(1,128)S(1)} %psum.15), channel_id=1, replica_groups=mesh['dp'=32,'tensor'=8] {'dp'}, dimensions={1} | all-to-all | bytes 32768 | tf_op jit(solution)/shard_map/all_to_all | solution.py:60
  201.2 0.6 copy.12
  (1 shorter events, 0.0 us)
Async XLA Ops:
  7.4 2.9 %copy-start = (bf16[1,256,3584]{2,1,0:T(8,128)(2,1)S(1)}, bf16[1,256,3584]{2,1,0:T(8,128)(2,1)}, u32[]{:S(2)}) copy-start(bf16[1,256,3584]{2,1,0:T(8,128)(2,1)} %param.10) | copy-start | bytes 5505028
  7.4 118.2 %all-reduce.2.cloned.1.call-start = ((), (), s32[]{:S(2)}) async-start(), calls=%async_computation.1 | async-start | bytes 524288 | tf_op jit(solution)/shard_map/psum | solution.py:46
  7.4 4.6 %copy-start.1 = (bf16[1,256,3584]{2,1,0:T(8,128)(2,1)S(1)}, bf16[1,256,3584]{2,1,0:T(8,128)(2,1)}, u32[]{:S(2)}) copy-start(bf16[1,256,3584]{2,1,0:T(8,128)(2,1)} %param.11) | copy-start | bytes 5505028
  7.4 4.6 %copy-start.2 = (bf16[3584,64]{0,1:T(8,128)(2,1)S(1)}, bf16[3584,64]{0,1:T(8,128)(2,1)}, u32[]{:S(2)}) copy-start(bf16[3584,64]{0,1:T(8,128)(2,1)} %param.15) | copy-start | bytes 1376260
  13.4 114.5 %all-gather.2.cloned.1.call-start = ((), (), s32[]{:S(2)}) async-start(), calls=%async_computation.2 | async-start | bytes 8650752 | tf_op jit(solution)/shard_map/all_gather | solution.py:55
Sparse Core Ops, SparseCore 0:
  13.5 112.0 all-reduce.1
Sparse Core Ops, SparseCore 1:
  15.7 76.8 all-gather.1
where the time goes:
time: 210 us; the launch traced here: 209 us
  waiting for transfers between devices  112 us (53%)
  blocking collectives  67.7 us (32%)
  between operations  14.9 us (7%)
  matrix products  13 us (6%)
    psum x1, waiting for transfers between devices, per_device(): summed_proj = lax.psum(partial_proj, 'tensor')  112 us
    psum x1, blocking collectives, per_device(): summed_scores = lax.psum(partial_scores, 'tensor')  41.1 us
    all_to_all x1, blocking collectives, per_device(): lax.all_to_all(summed_scores, 'dp', split_axis=1, concat_axis=0, tiled=True)  26.6 us
    dot_general x1, matrix products, per_device(): lax.dot_general(packed, lax.all_gather(queries, 'dp', axis=0, tiled=True)...  5.65 us
    dot_general x4, matrix products, project_rows(): jnp.dot(acts.reshape(ex * seq, wid), proj, preferred_element_type=jnp.flo...  5.2 us
  transfers between devices with their start and end apart: 2, of which 1 were waited for; matrix products, arithmetic and copies ran while one was open for 1% of the time, Pallas kernels for 0%

commit v1 on v0

v1 whole, which is shorter than its diff:
```python
import jax
import jax.numpy as jnp
from jax import lax
from jax.sharding import Mesh, PartitionSpec as P

SIZES = (4, 4, 2, 4, 2)
NAMES = ("zl", "x", "c", "y", "zh")
DP = ("zl", "x", "c")
TENSOR = ("y", "zh")


def project_columns(acts, proj):
    return lax.dot_general(
        proj, acts[0], (((0,), (1,)), ((), ())), preferred_element_type=jnp.float32
    )


def outer_rows(outs, ins):
    return lax.dot_general(
        outs, ins, (((1,), (1,)), ((), ())),
        precision=lax.Precision.HIGHEST, preferred_element_type=jnp.float32,
    )


def exchange(pieces, axes):
    return lax.all_to_all(pieces, axes, split_axis=0, concat_axis=0, tiled=True)


def swap(values, axis, mask):
    size = lax.axis_size(axis)
    return lax.ppermute(values, axis, [(k, k ^ mask) for k in range(size)])


def to_all(held, axes, size):
    return exchange(jnp.broadcast_to(held, (size,) + held.shape), axes)


def per_device(
    up_inputs,
    up_grads,
    down_inputs,
    down_grads,
    up_in_proj,
    up_out_proj,
    down_in_proj,
    down_out_proj,
    queries,
):
    zls, xs, cores, ys, zhs = SIZES
    rank = up_in_proj.shape[1]
    rows = 2 * rank // ys // zhs
    other = swap(queries, "zh", 1)
    up_in = project_columns(up_inputs, up_in_proj)
    down_out = project_columns(down_grads, down_out_proj)
    wide_proj = jnp.concatenate([up_out_proj, down_in_proj], axis=1)
    wide_proj, up_in, down_out = lax.optimization_barrier((wide_proj, up_in, down_out))
    up_out = project_columns(up_grads, wide_proj[:, :rank])
    down_in = project_columns(down_inputs, wide_proj[:, rank:])
    pieces = []
    for outs, ins in ((up_out, up_in), (down_out, down_in)):
        for k in range(rank // (zhs * rows)):
            pieces.append(jnp.concatenate([outs[k * zhs * rows : (k + 1) * zhs * rows], ins], axis=0))
    pieces = jnp.stack(pieces)
    y = lax.axis_index("y")
    piece = lambda k: lax.dynamic_index_in_dim(pieces, k, 0, keepdims=False)
    half = piece(y) + sum(swap(piece(y ^ mask), "y", mask) for mask in (1, 3, 2))
    sums = half + swap(half, "zh", 1)
    outer = zhs * rows
    outs, ins = sums[:outer], sums[outer:]
    own = jnp.concatenate([outer_rows(outs[0::2], ins), outer_rows(outs[1::2], ins)], axis=1)
    every = to_all(own.astype(jnp.bfloat16), DP, zls * xs * cores)
    first_half = lax.axis_index("zh") == 0
    low, high = jnp.where(first_half, queries, other), jnp.where(first_half, other, queries)
    scores = lax.dot_general(
        every.reshape(every.shape[0], -1), jnp.concatenate([low, high], axis=1), (((1,), (1,)), ((), ())),
        preferred_element_type=jnp.float32,
    )
    from_1, from_2, from_3 = (swap(scores, "y", mask) for mask in (1, 2, 3))
    return (from_2 + from_3) + (from_1 + scores)


def solution(mesh):
    split = Mesh(mesh.devices.reshape(SIZES), NAMES)
    placed = (
        P(DP, None, TENSOR),
        P(DP, None, TENSOR),
        P(DP, None, TENSOR),
        P(DP, None, TENSOR),
        P(TENSOR, None),
        P(TENSOR, None),
        P(TENSOR, None),
        P(TENSOR, None),
        P(DP, TENSOR),
    )
    return jax.shard_map(
        per_device, mesh=split, in_specs=placed, out_specs=P(None, DP), check_vma=False
    )
```

time: 210 us -> 50.8 us (0.24)
  waiting for transfers between devices: 112 us -> 17.4 us
  blocking collectives: 67.7 us -> 0 us
  starting transfers between devices: 0.05 us -> 26.8 us
  between operations: 14.9 us -> 0.21 us
  matrix products: 13 us -> 2.48 us
    psum x1 -> x0, waiting for transfers between devices: 112 us -> none  [per_device(): summed_proj = lax.psum(partial_proj, 'tensor')]
    psum x1 -> x0, blocking collectives: 41.1 us -> none  [per_device(): summed_scores = lax.psum(partial_scores, 'tensor')]
    all_to_all x1 -> x0, blocking collectives: 26.6 us -> none  [per_device(): lax.all_to_all(summed_scores, 'dp', split_axis=1, concat_axis=0, tiled=True)]
    ppermute x0 -> x8, starting transfers between devices: none -> 14.9 us  [swap(): return lax.ppermute(values, axis, [(k, k ^ mask) for k in range(size)])]
    all_to_all x0 -> x1, starting transfers between devices: none -> 11.9 us  [exchange(): return lax.all_to_all(pieces, axes, split_axis=0, concat_axis=0, tiled=True)]
    dot_general x7, matrix products: 13 us -> 2.48 us  [the longest x4 1.89 us: project_columns(): lax.dot_general(proj, acts[0], (((0,), (1,)), ((), ())), preferred_elemen...]
    ppermute x0 -> x8, waiting for transfers between devices: none -> 8.94 us  [swap(): return lax.ppermute(values, axis, [(k, k ^ mask) for k in range(size)])]
    all_to_all x0 -> x1, waiting for transfers between devices: none -> 8.49 us  [exchange(): return lax.all_to_all(pieces, axes, split_axis=0, concat_axis=0, tiled=True)]
  transfers between devices with their start and end apart: 2 -> 9, of which waited for: 1 -> 7; matrix products, arithmetic and copies ran while one was open for 1% -> 2% of each run, Pallas kernels for 0% -> 0%
where the time goes in v1:
time: 50.8 us; the launch traced here: 50.6 us
  starting transfers between devices  26.8 us (53%)
  waiting for transfers between devices  17.4 us (34%)
  matrix products  2.48 us (5%)
  other arithmetic  2.22 us (4%)
  local copies, waits for them, and re-layouts  1.47 us (3%)
    ppermute x8, starting transfers between devices, swap(): return lax.ppermute(values, axis, [(k, k ^ mask) for k in range(size)])  14.9 us
    all_to_all x1, starting transfers between devices, exchange(): return lax.all_to_all(pieces, axes, split_axis=0, concat_axis=0, tiled=True)  11.9 us
    ppermute x8, waiting for transfers between devices, swap(): return lax.ppermute(values, axis, [(k, k ^ mask) for k in range(size)])  8.94 us
    all_to_all x1, waiting for transfers between devices, exchange(): return lax.all_to_all(pieces, axes, split_axis=0, concat_axis=0, tiled=True)  8.49 us
    dot_general x4, matrix products, project_columns(): lax.dot_general(proj, acts[0], (((0,), (1,)), ((), ())), preferred_elemen...  1.89 us
    concatenate x1, other arithmetic, per_device(): wide_proj = jnp.concatenate([up_out_proj, down_in_proj], axis=1)  1.37 us
  transfers between devices with their start and end apart: 9, of which 7 were waited for; matrix products, arithmetic and copies ran while one was open for 2% of the time, Pallas kernels for 0%

profile of v1, /device:TPU:1, one launch (start us, length us, event | category | flops | bytes accessed | tf_op | source)
XLA Modules:
  0.0 50.6 jit_solution(1133583291860487251)
XLA Ops:
  0.0 1.4 %pad_maximum_fusion = bf16[3584,128]{0,1:T(8,128)(2,1)S(1)} fusion(bf16[3584,64]{0,1:T(8,128)(2,1)} %param.15, bf16[3584,64]{0,1:T(8,128)(2,1)} %param.14), kind=kLoop, calls=%fused_computation.6 | loop fusion | flops 1835008 | bytes 1835008 | tf_op jit(solution)/shard_map/concatenate | solution.py:55
  1.5 0.3 fusion.10
  1.8 0.3 fusion.8
  2.2 0.7 %fusion.2 = f32[64,256]{1,0:T(8,128)S(1)} fusion(bf16[1,256,3584]{2,1,0:T(8,128)(2,1)S(1)} %copy-done, bf16[3584,128]{0,1:T(8,128)(2,1)S(1)} %pad_maximum_fusion), kind=kOutput, calls=%fused_computation.2 | convolution fusion | flops 117440512 | bytes 2359296 | tf_op jit(solution)/shard_map/dot_general | solution.py:13
  2.9 0.5 %copy-done.1 = bf16[1,256,3584]{2,1,0:T(8,128)(2,1)S(1)} copy-done((bf16[1,256,3584]{2,1,0:T(8,128)(2,1)S(1)}, bf16[1,256,3584]{2,1,0:T(8,128)(2,1)}, u32[]{:S(2)}) %copy-start.1) | copy-done | bytes 1835032
  3.4 0.7 %fusion = f32[64,256]{1,0:T(8,128)S(1)} fusion(bf16[1,256,3584]{2,1,0:T(8,128)(2,1)S(1)} %copy-done.1, bf16[3584,128]{0,1:T(8,128)(2,1)S(1)} %pad_maximum_fusion), kind=kOutput, calls=%fused_computation | convolution fusion | flops 117440512 | bytes 2359296 | tf_op jit(solution)/shard_map/dot_general | solution.py:13
  4.2 2.2 %collective-permute-start = (f32[96,256]{1,0:T(8,128)S(1)}, f32[96,256]{1,0:T(8,128)S(1)}, u32[]{:S(2)}, u32[]{:S(2)}) collective-permute-start(f32[96,256]{1,0:T(8,128)S(1)} %get-tuple-element.15), channel_id=1, source_target_pairs={{0,2},{2,0},{4,6},{6,4},{1,3},{3,1},{5,7},{7,5},{8,10},{10,8},{12,... | collective-permute-start | bytes 294920 | tf_op jit(solution)/shard_map/ppermute | solution.py:31
  6.4 1.9 %collective-permute-start.1 = (f32[96,256]{1,0:T(8,128)S(1)}, f32[96,256]{1,0:T(8,128)S(1)}, u32[]{:S(2)}, u32[]{:S(2)}) collective-permute-start(f32[96,256]{1,0:T(8,128)S(1)} %get-tuple-element.13), channel_id=1, source_target_pairs={{0,6},{2,4},{4,2},{6,0},{1,7},{3,5},{5,3},{7,1},{8,14},{10,12},{12... | collective-permute-start | bytes 294920 | tf_op jit(solution)/shard_map/ppermute | solution.py:31
  8.3 0.7 %collective-permute-start.2 = (f32[96,256]{1,0:T(8,128)S(1)}, f32[96,256]{1,0:T(8,128)S(1)}, u32[]{:S(2)}, u32[]{:S(2)}) collective-permute-start(f32[96,256]{1,0:T(8,128)S(1)} %get-tuple-element.14), channel_id=1, source_target_pairs={{0,4},{2,6},{4,0},{6,2},{1,5},{3,7},{5,1},{7,3},{8,12},{10,14},{12... | collective-permute-start | bytes 294920 | tf_op jit(solution)/shard_map/ppermute | solution.py:31
  9.1 2.1 %collective-permute-done.1 = f32[96,256]{1,0:T(8,128)S(1)} collective-permute-done((f32[96,256]{1,0:T(8,128)S(1)}, f32[96,256]{1,0:T(8,128)S(1)}, u32[]{:S(2)}, u32[]{:S(2)}) %collective-permute-start.1) | collective-permute-done | bytes 98336 | tf_op jit(solution)/shard_map/ppermute | solution.py:31
  11.1 2.3 %collective-permute-done.2 = f32[96,256]{1,0:T(8,128)S(1)} collective-permute-done((f32[96,256]{1,0:T(8,128)S(1)}, f32[96,256]{1,0:T(8,128)S(1)}, u32[]{:S(2)}, u32[]{:S(2)}) %collective-permute-start.2) | collective-permute-done | bytes 98336 | tf_op jit(solution)/shard_map/ppermute | solution.py:31
  13.4 7.0 %collective-permute-start.3 = (f32[96,256]{1,0:T(8,128)S(1)}, f32[96,256]{1,0:T(8,128)S(1)}, u32[]{:S(2)}, u32[]{:S(2)}) collective-permute-start(f32[96,256]{1,0:T(8,128)S(1)} %bitcast_add_fusion), channel_id=1, source_target_pairs={{0,1},{1,0},{2,3},{3,2},{4,5},{5,4},{6,7},{7,6},{8,9},{9,8},{10,11... | collective-permute-start | bytes 294920 | tf_op jit(solution)/shard_map/ppermute | solution.py:31
  20.6 2.0 %collective-permute-done.3 = f32[96,256]{1,0:T(8,128)S(1)} collective-permute-done((f32[96,256]{1,0:T(8,128)S(1)}, f32[96,256]{1,0:T(8,128)S(1)}, u32[]{:S(2)}, u32[]{:S(2)}) %collective-permute-start.3) | collective-permute-done | bytes 98336 | tf_op jit(solution)/shard_map/ppermute | solution.py:31
  22.8 0.2 convolution_convert_fusion
  23.0 0.7 %broadcast_in_dim.3 = bf16[32,16,128]{2,1,0:T(8,128)(2,1)} broadcast(bf16[16,128]{1,0:T(8,128)(2,1)S(1)} %pad_maximum_fusion.6), dimensions={1,2} | broadcast | bytes 135168 | tf_op jit(solution)/shard_map/broadcast_in_dim | solution.py:35
  23.7 11.9 %all-to-all-start = ((bf16[32,16,128]{2,1,0:T(8,128)(2,1)}), bf16[32,16,128]{2,1,0:T(8,128)(2,1)S(1)}, u32[]{:S(2)}, u32[]{:S(2)}) async-start(bf16[32,16,128]{2,1,0:T(8,128)(2,1)} %broadcast_in_dim.3), calls=%async_computation | async-start | bytes 262144 | tf_op jit(solution)/shard_map/all_to_all | solution.py:26
  35.7 8.5 %all-to-all-done = bf16[32,16,128]{2,1,0:T(8,128)(2,1)S(1)} async-done(((bf16[32,16,128]{2,1,0:T(8,128)(2,1)}), bf16[32,16,128]{2,1,0:T(8,128)(2,1)S(1)}, u32[]{:S(2)}, u32[]{:S(2)}) %all-to-all-start) | async-done | bytes 131104 | tf_op jit(solution)/shard_map/all_to_all | solution.py:26
  44.2 0.3 fusion.4
  44.5 1.4 %collective-permute-start.5 = (f32[32,128]{1,0:T(8,128)S(1)}, f32[32,128]{1,0:T(8,128)S(1)}, u32[]{:S(2)}, u32[]{:S(2)}) collective-permute-start(f32[32,128]{1,0:T(8,128)S(1)} %fusion.4), channel_id=1, source_target_pairs={{0,4},{2,6},{4,0},{6,2},{1,5},{3,7},{5,1},{7,3},{8,12},{10,14},{12... | collective-permute-start | bytes 49160 | tf_op jit(solution)/shard_map/ppermute | solution.py:31
  45.8 1.6 %collective-permute-start.6 = (f32[32,128]{1,0:T(8,128)S(1)}, f32[32,128]{1,0:T(8,128)S(1)}, u32[]{:S(2)}, u32[]{:S(2)}) collective-permute-start(f32[32,128]{1,0:T(8,128)S(1)} %fusion.4), channel_id=1, source_target_pairs={{0,6},{2,4},{4,2},{6,0},{1,7},{3,5},{5,3},{7,1},{8,14},{10,12},{12... | collective-permute-start | bytes 49160 | tf_op jit(solution)/shard_map/ppermute | solution.py:31
  47.4 1.2 %collective-permute-done.5 = f32[32,128]{1,0:T(8,128)S(1)} collective-permute-done((f32[32,128]{1,0:T(8,128)S(1)}, f32[32,128]{1,0:T(8,128)S(1)}, u32[]{:S(2)}, u32[]{:S(2)}) %collective-permute-start.5) | collective-permute-done | bytes 16416 | tf_op jit(solution)/shard_map/ppermute | solution.py:31
  48.6 1.1 %collective-permute-done.6 = f32[32,128]{1,0:T(8,128)S(1)} collective-permute-done((f32[32,128]{1,0:T(8,128)S(1)}, f32[32,128]{1,0:T(8,128)S(1)}, u32[]{:S(2)}, u32[]{:S(2)}) %collective-permute-start.6) | collective-permute-done | bytes 16416 | tf_op jit(solution)/shard_map/ppermute | solution.py:31
  49.7 0.3 collective-permute-done.7
  50.0 0.6 %add_add_fusion = f32[32,128]{1,0:T(8,128)} fusion(f32[32,128]{1,0:T(8,128)S(1)} %collective-permute-done.7, f32[32,128]{1,0:T(8,128)S(1)} %fusion.4, f32[32,128]{1,0:T(8,128)S(1)} %collective-permute-done.5, f32[32,128]{1,0:T(8,128)S(1)} %collective-permute-done.6), kind=kLoop, calls=%fused_computation.36 | loop fusion | flops 12288 | bytes 81920 | tf_op jit(solution)/shard_map/add | solution.py:79
  (30 shorter events, 0.8 us)
Async XLA Ops:
  0.0 2.2 %copy-start = (bf16[1,256,3584]{2,1,0:T(8,128)(2,1)S(1)}, bf16[1,256,3584]{2,1,0:T(8,128)(2,1)}, u32[]{:S(2)}) copy-start(bf16[1,256,3584]{2,1,0:T(8,128)(2,1)} %param.10) | copy-start | bytes 5505028
  0.0 1.4 %copy-start.5 = (bf16[1024,64]{0,1:T(8,128)(2,1)S(1)}, bf16[1024,64]{0,1:T(8,128)(2,1)}, u32[]{:S(2)}) copy-start(bf16[1024,64]{0,1:T(8,128)(2,1)} %param.13) | copy-start | bytes 393220
  0.0 1.5 %copy-start.2 = (bf16[1,256,1024]{2,1,0:T(8,128)(2,1)S(1)}, bf16[1,256,1024]{2,1,0:T(8,128)(2,1)}, u32[]{:S(2)}) copy-start(bf16[1,256,1024]{2,1,0:T(8,128)(2,1)} %param.9) | copy-start | bytes 1572868
  0.0 1.8 %copy-start.3 = (bf16[1,256,1024]{2,1,0:T(8,128)(2,1)S(1)}, bf16[1,256,1024]{2,1,0:T(8,128)(2,1)}, u32[]{:S(2)}) copy-start(bf16[1,256,1024]{2,1,0:T(8,128)(2,1)} %param.12) | copy-start | bytes 1572868
  0.0 1.8 %copy-start.6 = (bf16[1024,64]{0,1:T(8,128)(2,1)S(1)}, bf16[1024,64]{0,1:T(8,128)(2,1)}, u32[]{:S(2)}) copy-start(bf16[1024,64]{0,1:T(8,128)(2,1)} %param.16) | copy-start | bytes 393220
  1.8 1.6 %copy-start.1 = (bf16[1,256,3584]{2,1,0:T(8,128)(2,1)S(1)}, bf16[1,256,3584]{2,1,0:T(8,128)(2,1)}, u32[]{:S(2)}) copy-start(bf16[1,256,3584]{2,1,0:T(8,128)(2,1)} %param.11) | copy-start | bytes 5505028
  4.1 16.4 %copy-start.4 = (bf16[128,1024]{1,0:T(8,128)(2,1)S(1)}, bf16[128,1024]{1,0:T(8,128)(2,1)}, u32[]{:S(2)}) copy-start(bf16[128,1024]{1,0:T(8,128)(2,1)} %param.17) | copy-start | bytes 786436
  4.2 4.8 %collective-permute-start = (f32[96,256]{1,0:T(8,128)S(1)}, f32[96,256]{1,0:T(8,128)S(1)}, u32[]{:S(2)}, u32[]{:S(2)}) collective-permute-start(f32[96,256]{1,0:T(8,128)S(1)} %get-tuple-element.15), channel_id=1, source_target_pairs={{0,2},{2,0},{4,6},{6,4},{1,3},{3,1},{5,7},{7,5},{8,10},{10,8},{12,... | collective-permute-start | bytes 294920 | tf_op jit(solution)/shard_map/ppermute | solution.py:31
  6.4 4.7 %collective-permute-start.1 = (f32[96,256]{1,0:T(8,128)S(1)}, f32[96,256]{1,0:T(8,128)S(1)}, u32[]{:S(2)}, u32[]{:S(2)}) collective-permute-start(f32[96,256]{1,0:T(8,128)S(1)} %get-tuple-element.13), channel_id=1, source_target_pairs={{0,6},{2,4},{4,2},{6,0},{1,7},{3,5},{5,3},{7,1},{8,14},{10,12},{12... | collective-permute-start | bytes 294920 | tf_op jit(solution)/shard_map/ppermute | solution.py:31
  8.3 5.1 %collective-permute-start.2 = (f32[96,256]{1,0:T(8,128)S(1)}, f32[96,256]{1,0:T(8,128)S(1)}, u32[]{:S(2)}, u32[]{:S(2)}) collective-permute-start(f32[96,256]{1,0:T(8,128)S(1)} %get-tuple-element.14), channel_id=1, source_target_pairs={{0,4},{2,6},{4,0},{6,2},{1,5},{3,7},{5,1},{7,3},{8,12},{10,14},{12... | collective-permute-start | bytes 294920 | tf_op jit(solution)/shard_map/ppermute | solution.py:31
  13.4 9.1 %collective-permute-start.3 = (f32[96,256]{1,0:T(8,128)S(1)}, f32[96,256]{1,0:T(8,128)S(1)}, u32[]{:S(2)}, u32[]{:S(2)}) collective-permute-start(f32[96,256]{1,0:T(8,128)S(1)} %bitcast_add_fusion), channel_id=1, source_target_pairs={{0,1},{1,0},{2,3},{3,2},{4,5},{5,4},{6,7},{7,6},{8,9},{9,8},{10,11... | collective-permute-start | bytes 294920 | tf_op jit(solution)/shard_map/ppermute | solution.py:31
  20.4 15.2 %collective-permute-start.4 = (bf16[128,1024]{1,0:T(8,128)(2,1)S(1)}, bf16[128,1024]{1,0:T(8,128)(2,1)S(1)}, u32[]{:S(2)}, u32[]{:S(2)}) collective-permute-start(bf16[128,1024]{1,0:T(8,128)(2,1)S(1)} %copy-done.4), channel_id=1, source_target_pairs={{0,1},{1,0},{2,3},{3,2},{4,5},{5,4},{6,7},{7,6},{8,9},{9,8},{10,11... | collective-permute-start | bytes 786440 | tf_op jit(solution)/shard_map/ppermute | solution.py:31
  23.7 20.5 %all-to-all-start = ((bf16[32,16,128]{2,1,0:T(8,128)(2,1)}), bf16[32,16,128]{2,1,0:T(8,128)(2,1)S(1)}, u32[]{:S(2)}, u32[]{:S(2)}) async-start(bf16[32,16,128]{2,1,0:T(8,128)(2,1)} %broadcast_in_dim.3), calls=%async_computation | async-start | bytes 262144 | tf_op jit(solution)/shard_map/all_to_all | solution.py:26
  44.5 4.1 %collective-permute-start.5 = (f32[32,128]{1,0:T(8,128)S(1)}, f32[32,128]{1,0:T(8,128)S(1)}, u32[]{:S(2)}, u32[]{:S(2)}) collective-permute-start(f32[32,128]{1,0:T(8,128)S(1)} %fusion.4), channel_id=1, source_target_pairs={{0,4},{2,6},{4,0},{6,2},{1,5},{3,7},{5,1},{7,3},{8,12},{10,14},{12... | collective-permute-start | bytes 49160 | tf_op jit(solution)/shard_map/ppermute | solution.py:31
  45.8 3.9 %collective-permute-start.6 = (f32[32,128]{1,0:T(8,128)S(1)}, f32[32,128]{1,0:T(8,128)S(1)}, u32[]{:S(2)}, u32[]{:S(2)}) collective-permute-start(f32[32,128]{1,0:T(8,128)S(1)} %fusion.4), channel_id=1, source_target_pairs={{0,6},{2,4},{4,2},{6,0},{1,7},{3,5},{5,3},{7,1},{8,14},{10,12},{12... | collective-permute-start | bytes 49160 | tf_op jit(solution)/shard_map/ppermute | solution.py:31
  47.4 2.6 %collective-permute-start.7 = (f32[32,128]{1,0:T(8,128)S(1)}, f32[32,128]{1,0:T(8,128)S(1)}, u32[]{:S(2)}, u32[]{:S(2)}) collective-permute-start(f32[32,128]{1,0:T(8,128)S(1)} %fusion.4), channel_id=1, source_target_pairs={{0,2},{2,0},{4,6},{6,4},{1,3},{3,1},{5,7},{7,5},{8,10},{10,8},{12,... | collective-permute-start | bytes 49160 | tf_op jit(solution)/shard_map/ppermute | solution.py:31

commit v2 on v1

--- a/solution.py
+++ b/solution.py
@@ -13,6 +13,19 @@
     return lax.dot_general(
         proj, acts[0], (((0,), (1,)), ((), ())), preferred_element_type=jnp.float32
     )
+
+
+def rounded(values):
+    return lax.reduce_precision(values, 8, 7)
+
+
+def in_16_bits(sums, outer):
+    high = rounded(sums[:outer])
+    return jnp.concatenate([high, rounded(sums[:outer] - high), rounded(sums[outer:])], axis=0)
+
+
+def sum_of_parts(parts, outer):
+    return parts[:outer] + parts[outer : 2 * outer], parts[2 * outer :]
 
 
 def outer_rows(outs, ins):
@@ -64,9 +77,11 @@
     y = lax.axis_index("y")
     piece = lambda k: lax.dynamic_index_in_dim(pieces, k, 0, keepdims=False)
     half = piece(y) + sum(swap(piece(y ^ mask), "y", mask) for mask in (1, 3, 2))
-    sums = half + swap(half, "zh", 1)
     outer = zhs * rows
-    outs, ins = sums[:outer], sums[outer:]
+    parts = in_16_bits(half, outer)
+    near = sum_of_parts(parts, outer)
+    far = sum_of_parts(swap(parts.astype(jnp.bfloat16), "zh", 1).astype(jnp.float32), outer)
+    outs, ins = near[0] + far[0], near[1] + far[1]
     own = jnp.concatenate([outer_rows(outs[0::2], ins), outer_rows(outs[1::2], ins)], axis=1)
     every = to_all(own.astype(jnp.bfloat16), DP, zls * xs * cores)
     first_half = lax.axis_index("zh") == 0

time: 50.8 us -> 50.4 us (level)
  no operation moved by 1% of the time
where the time goes in v2:
time: 50.4 us; the launch traced here: 50.2 us
  starting transfers between devices  26.4 us (52%)
  waiting for transfers between devices  17.4 us (35%)
  matrix products  2.49 us (5%)
  other arithmetic  2.25 us (4%)
  local copies, waits for them, and re-layouts  1.47 us (3%)
    ppermute x8, starting transfers between devices, swap(): return lax.ppermute(values, axis, [(k, k ^ mask) for k in range(size)])  14.8 us
    all_to_all x1, starting transfers between devices, exchange(): return lax.all_to_all(pieces, axes, split_axis=0, concat_axis=0, tiled=True)  11.6 us
    all_to_all x1, waiting for transfers between devices, exchange(): return lax.all_to_all(pieces, axes, split_axis=0, concat_axis=0, tiled=True)  8.81 us
    ppermute x8, waiting for transfers between devices, swap(): return lax.ppermute(values, axis, [(k, k ^ mask) for k in range(size)])  8.55 us
    dot_general x4, matrix products, project_columns(): lax.dot_general(proj, acts[0], (((0,), (1,)), ((), ())), preferred_elemen...  1.89 us
    concatenate x1, other arithmetic, per_device(): wide_proj = jnp.concatenate([up_out_proj, down_in_proj], axis=1)  1.37 us
  transfers between devices with their start and end apart: 9, of which 7 were waited for; matrix products, arithmetic and copies ran while one was open for 2% of the time, Pallas kernels for 0%

profile of v2, /device:TPU:1, one launch (start us, length us, event | category | flops | bytes accessed | tf_op | source)
XLA Modules:
  0.0 50.2 jit_solution(14709461078223510471)
XLA Ops:
  0.0 1.4 %pad_maximum_fusion = bf16[3584,128]{0,1:T(8,128)(2,1)S(1)} fusion(bf16[3584,64]{0,1:T(8,128)(2,1)} %param.15, bf16[3584,64]{0,1:T(8,128)(2,1)} %param.14), kind=kLoop, calls=%fused_computation.6 | loop fusion | flops 1835008 | bytes 1835008 | tf_op jit(solution)/shard_map/concatenate | solution.py:68
  1.5 0.3 fusion.10
  1.8 0.3 fusion.8
  2.2 0.7 %fusion.2 = f32[64,256]{1,0:T(8,128)S(1)} fusion(bf16[1,256,3584]{2,1,0:T(8,128)(2,1)S(1)} %copy-done, bf16[3584,128]{0,1:T(8,128)(2,1)S(1)} %pad_maximum_fusion), kind=kOutput, calls=%fused_computation.2 | convolution fusion | flops 117440512 | bytes 2359296 | tf_op jit(solution)/shard_map/dot_general | solution.py:13
  2.9 0.5 %copy-done.1 = bf16[1,256,3584]{2,1,0:T(8,128)(2,1)S(1)} copy-done((bf16[1,256,3584]{2,1,0:T(8,128)(2,1)S(1)}, bf16[1,256,3584]{2,1,0:T(8,128)(2,1)}, u32[]{:S(2)}) %copy-start.1) | copy-done | bytes 1835032
  3.4 0.7 %fusion = f32[64,256]{1,0:T(8,128)S(1)} fusion(bf16[1,256,3584]{2,1,0:T(8,128)(2,1)S(1)} %copy-done.1, bf16[3584,128]{0,1:T(8,128)(2,1)S(1)} %pad_maximum_fusion), kind=kOutput, calls=%fused_computation | convolution fusion | flops 117440512 | bytes 2359296 | tf_op jit(solution)/shard_map/dot_general | solution.py:13
  4.2 2.2 %collective-permute-start = (f32[96,256]{1,0:T(8,128)S(1)}, f32[96,256]{1,0:T(8,128)S(1)}, u32[]{:S(2)}, u32[]{:S(2)}) collective-permute-start(f32[96,256]{1,0:T(8,128)S(1)} %get-tuple-element.15), channel_id=1, source_target_pairs={{0,2},{2,0},{4,6},{6,4},{1,3},{3,1},{5,7},{7,5},{8,10},{10,8},{12,... | collective-permute-start | bytes 294920 | tf_op jit(solution)/shard_map/ppermute | solution.py:44
  6.4 1.9 %collective-permute-start.1 = (f32[96,256]{1,0:T(8,128)S(1)}, f32[96,256]{1,0:T(8,128)S(1)}, u32[]{:S(2)}, u32[]{:S(2)}) collective-permute-start(f32[96,256]{1,0:T(8,128)S(1)} %get-tuple-element.13), channel_id=1, source_target_pairs={{0,6},{2,4},{4,2},{6,0},{1,7},{3,5},{5,3},{7,1},{8,14},{10,12},{12... | collective-permute-start | bytes 294920 | tf_op jit(solution)/shard_map/ppermute | solution.py:44
  8.3 0.7 %collective-permute-start.2 = (f32[96,256]{1,0:T(8,128)S(1)}, f32[96,256]{1,0:T(8,128)S(1)}, u32[]{:S(2)}, u32[]{:S(2)}) collective-permute-start(f32[96,256]{1,0:T(8,128)S(1)} %get-tuple-element.14), channel_id=1, source_target_pairs={{0,4},{2,6},{4,0},{6,2},{1,5},{3,7},{5,1},{7,3},{8,12},{10,14},{12... | collective-permute-start | bytes 294920 | tf_op jit(solution)/shard_map/ppermute | solution.py:44
  9.1 2.1 %collective-permute-done.1 = f32[96,256]{1,0:T(8,128)S(1)} collective-permute-done((f32[96,256]{1,0:T(8,128)S(1)}, f32[96,256]{1,0:T(8,128)S(1)}, u32[]{:S(2)}, u32[]{:S(2)}) %collective-permute-start.1) | collective-permute-done | bytes 98336 | tf_op jit(solution)/shard_map/ppermute | solution.py:44
  11.1 2.3 %collective-permute-done.2 = f32[96,256]{1,0:T(8,128)S(1)} collective-permute-done((f32[96,256]{1,0:T(8,128)S(1)}, f32[96,256]{1,0:T(8,128)S(1)}, u32[]{:S(2)}, u32[]{:S(2)}) %collective-permute-start.2) | collective-permute-done | bytes 98336 | tf_op jit(solution)/shard_map/ppermute | solution.py:44
  13.5 7.0 %collective-permute-start.3 = (bf16[128,256]{1,0:T(8,128)(2,1)S(1)}, bf16[128,256]{1,0:T(8,128)(2,1)S(1)}, u32[]{:S(2)}, u32[]{:S(2)}) collective-permute-start(bf16[128,256]{1,0:T(8,128)(2,1)S(1)} %pad_maximum_fusion.6), channel_id=1, source_target_pairs={{0,1},{1,0},{2,3},{3,2},{4,5},{5,4},{6,7},{7,6},{8,9},{9,8},{10,11... | collective-permute-start | bytes 196616 | tf_op jit(solution)/shard_map/ppermute | solution.py:44
  20.6 1.6 %collective-permute-done.3 = bf16[128,256]{1,0:T(8,128)(2,1)S(1)} collective-permute-done((bf16[128,256]{1,0:T(8,128)(2,1)S(1)}, bf16[128,256]{1,0:T(8,128)(2,1)S(1)}, u32[]{:S(2)}, u32[]{:S(2)}) %collective-permute-start.3) | collective-permute-done | bytes 65568 | tf_op jit(solution)/shard_map/ppermute | solution.py:44
  22.4 0.2 convolution_convert_fusion
  22.7 0.7 %broadcast_in_dim.3 = bf16[32,16,128]{2,1,0:T(8,128)(2,1)} broadcast(bf16[16,128]{1,0:T(8,128)(2,1)S(1)} %pad_maximum_fusion.7), dimensions={1,2} | broadcast | bytes 135168 | tf_op jit(solution)/shard_map/broadcast_in_dim | solution.py:48
  23.4 11.6 %all-to-all-start = ((bf16[32,16,128]{2,1,0:T(8,128)(2,1)}), bf16[32,16,128]{2,1,0:T(8,128)(2,1)S(1)}, u32[]{:S(2)}, u32[]{:S(2)}) async-start(bf16[32,16,128]{2,1,0:T(8,128)(2,1)} %broadcast_in_dim.3), calls=%async_computation | async-start | bytes 262144 | tf_op jit(solution)/shard_map/all_to_all | solution.py:39
  35.1 8.8 %all-to-all-done = bf16[32,16,128]{2,1,0:T(8,128)(2,1)S(1)} async-done(((bf16[32,16,128]{2,1,0:T(8,128)(2,1)}), bf16[32,16,128]{2,1,0:T(8,128)(2,1)S(1)}, u32[]{:S(2)}, u32[]{:S(2)}) %all-to-all-start) | async-done | bytes 131104 | tf_op jit(solution)/shard_map/all_to_all | solution.py:39
  43.9 0.3 fusion.4
  44.1 1.3 %collective-permute-start.5 = (f32[32,128]{1,0:T(8,128)S(1)}, f32[32,128]{1,0:T(8,128)S(1)}, u32[]{:S(2)}, u32[]{:S(2)}) collective-permute-start(f32[32,128]{1,0:T(8,128)S(1)} %fusion.4), channel_id=1, source_target_pairs={{0,4},{2,6},{4,0},{6,2},{1,5},{3,7},{5,1},{7,3},{8,12},{10,14},{12... | collective-permute-start | bytes 49160 | tf_op jit(solution)/shard_map/ppermute | solution.py:44
  45.5 1.6 %collective-permute-start.6 = (f32[32,128]{1,0:T(8,128)S(1)}, f32[32,128]{1,0:T(8,128)S(1)}, u32[]{:S(2)}, u32[]{:S(2)}) collective-permute-start(f32[32,128]{1,0:T(8,128)S(1)} %fusion.4), channel_id=1, source_target_pairs={{0,6},{2,4},{4,2},{6,0},{1,7},{3,5},{5,3},{7,1},{8,14},{10,12},{12... | collective-permute-start | bytes 49160 | tf_op jit(solution)/shard_map/ppermute | solution.py:44
  47.0 1.2 %collective-permute-done.5 = f32[32,128]{1,0:T(8,128)S(1)} collective-permute-done((f32[32,128]{1,0:T(8,128)S(1)}, f32[32,128]{1,0:T(8,128)S(1)}, u32[]{:S(2)}, u32[]{:S(2)}) %collective-permute-start.5) | collective-permute-done | bytes 16416 | tf_op jit(solution)/shard_map/ppermute | solution.py:44
  48.3 1.0 %collective-permute-done.6 = f32[32,128]{1,0:T(8,128)S(1)} collective-permute-done((f32[32,128]{1,0:T(8,128)S(1)}, f32[32,128]{1,0:T(8,128)S(1)}, u32[]{:S(2)}, u32[]{:S(2)}) %collective-permute-start.6) | collective-permute-done | bytes 16416 | tf_op jit(solution)/shard_map/ppermute | solution.py:44
  49.3 0.3 collective-permute-done.7
  49.6 0.6 %add_add_fusion = f32[32,128]{1,0:T(8,128)} fusion(f32[32,128]{1,0:T(8,128)S(1)} %collective-permute-done.7, f32[32,128]{1,0:T(8,128)S(1)} %fusion.4, f32[32,128]{1,0:T(8,128)S(1)} %collective-permute-done.5, f32[32,128]{1,0:T(8,128)S(1)} %collective-permute-done.6), kind=kLoop, calls=%fused_computation.45 | loop fusion | flops 12288 | bytes 81920 | tf_op jit(solution)/shard_map/add | solution.py:94
  (33 shorter events, 0.8 us)
Async XLA Ops:
  0.0 2.2 %copy-start = (bf16[1,256,3584]{2,1,0:T(8,128)(2,1)S(1)}, bf16[1,256,3584]{2,1,0:T(8,128)(2,1)}, u32[]{:S(2)}) copy-start(bf16[1,256,3584]{2,1,0:T(8,128)(2,1)} %param.10) | copy-start | bytes 5505028
  0.0 1.4 %copy-start.5 = (bf16[1024,64]{0,1:T(8,128)(2,1)S(1)}, bf16[1024,64]{0,1:T(8,128)(2,1)}, u32[]{:S(2)}) copy-start(bf16[1024,64]{0,1:T(8,128)(2,1)} %param.13) | copy-start | bytes 393220
  0.0 1.5 %copy-start.2 = (bf16[1,256,1024]{2,1,0:T(8,128)(2,1)S(1)}, bf16[1,256,1024]{2,1,0:T(8,128)(2,1)}, u32[]{:S(2)}) copy-start(bf16[1,256,1024]{2,1,0:T(8,128)(2,1)} %param.9) | copy-start | bytes 1572868
  0.0 1.8 %copy-start.3 = (bf16[1,256,1024]{2,1,0:T(8,128)(2,1)S(1)}, bf16[1,256,1024]{2,1,0:T(8,128)(2,1)}, u32[]{:S(2)}) copy-start(bf16[1,256,1024]{2,1,0:T(8,128)(2,1)} %param.12) | copy-start | bytes 1572868
  0.0 1.8 %copy-start.6 = (bf16[1024,64]{0,1:T(8,128)(2,1)S(1)}, bf16[1024,64]{0,1:T(8,128)(2,1)}, u32[]{:S(2)}) copy-start(bf16[1024,64]{0,1:T(8,128)(2,1)} %param.16) | copy-start | bytes 393220
  1.8 1.6 %copy-start.1 = (bf16[1,256,3584]{2,1,0:T(8,128)(2,1)S(1)}, bf16[1,256,3584]{2,1,0:T(8,128)(2,1)}, u32[]{:S(2)}) copy-start(bf16[1,256,3584]{2,1,0:T(8,128)(2,1)} %param.11) | copy-start | bytes 5505028
  4.1 16.4 %copy-start.4 = (bf16[128,1024]{1,0:T(8,128)(2,1)S(1)}, bf16[128,1024]{1,0:T(8,128)(2,1)}, u32[]{:S(2)}) copy-start(bf16[128,1024]{1,0:T(8,128)(2,1)} %param.17) | copy-start | bytes 786436
  4.2 4.8 %collective-permute-start = (f32[96,256]{1,0:T(8,128)S(1)}, f32[96,256]{1,0:T(8,128)S(1)}, u32[]{:S(2)}, u32[]{:S(2)}) collective-permute-start(f32[96,256]{1,0:T(8,128)S(1)} %get-tuple-element.15), channel_id=1, source_target_pairs={{0,2},{2,0},{4,6},{6,4},{1,3},{3,1},{5,7},{7,5},{8,10},{10,8},{12,... | collective-permute-start | bytes 294920 | tf_op jit(solution)/shard_map/ppermute | solution.py:44
  6.4 4.7 %collective-permute-start.1 = (f32[96,256]{1,0:T(8,128)S(1)}, f32[96,256]{1,0:T(8,128)S(1)}, u32[]{:S(2)}, u32[]{:S(2)}) collective-permute-start(f32[96,256]{1,0:T(8,128)S(1)} %get-tuple-element.13), channel_id=1, source_target_pairs={{0,6},{2,4},{4,2},{6,0},{1,7},{3,5},{5,3},{7,1},{8,14},{10,12},{12... | collective-permute-start | bytes 294920 | tf_op jit(solution)/shard_map/ppermute | solution.py:44
  8.3 5.1 %collective-permute-start.2 = (f32[96,256]{1,0:T(8,128)S(1)}, f32[96,256]{1,0:T(8,128)S(1)}, u32[]{:S(2)}, u32[]{:S(2)}) collective-permute-start(f32[96,256]{1,0:T(8,128)S(1)} %get-tuple-element.14), channel_id=1, source_target_pairs={{0,4},{2,6},{4,0},{6,2},{1,5},{3,7},{5,1},{7,3},{8,12},{10,14},{12... | collective-permute-start | bytes 294920 | tf_op jit(solution)/shard_map/ppermute | solution.py:44
  13.5 8.7 %collective-permute-start.3 = (bf16[128,256]{1,0:T(8,128)(2,1)S(1)}, bf16[128,256]{1,0:T(8,128)(2,1)S(1)}, u32[]{:S(2)}, u32[]{:S(2)}) collective-permute-start(bf16[128,256]{1,0:T(8,128)(2,1)S(1)} %pad_maximum_fusion.6), channel_id=1, source_target_pairs={{0,1},{1,0},{2,3},{3,2},{4,5},{5,4},{6,7},{7,6},{8,9},{9,8},{10,11... | collective-permute-start | bytes 196616 | tf_op jit(solution)/shard_map/ppermute | solution.py:44
  20.5 14.5 %collective-permute-start.4 = (bf16[128,1024]{1,0:T(8,128)(2,1)S(1)}, bf16[128,1024]{1,0:T(8,128)(2,1)S(1)}, u32[]{:S(2)}, u32[]{:S(2)}) collective-permute-start(bf16[128,1024]{1,0:T(8,128)(2,1)S(1)} %copy-done.4), channel_id=1, source_target_pairs={{0,1},{1,0},{2,3},{3,2},{4,5},{5,4},{6,7},{7,6},{8,9},{9,8},{10,11... | collective-permute-start | bytes 786440 | tf_op jit(solution)/shard_map/ppermute | solution.py:44
  23.4 20.5 %all-to-all-start = ((bf16[32,16,128]{2,1,0:T(8,128)(2,1)}), bf16[32,16,128]{2,1,0:T(8,128)(2,1)S(1)}, u32[]{:S(2)}, u32[]{:S(2)}) async-start(bf16[32,16,128]{2,1,0:T(8,128)(2,1)} %broadcast_in_dim.3), calls=%async_computation | async-start | bytes 262144 | tf_op jit(solution)/shard_map/all_to_all | solution.py:39
  44.1 4.1 %collective-permute-start.5 = (f32[32,128]{1,0:T(8,128)S(1)}, f32[32,128]{1,0:T(8,128)S(1)}, u32[]{:S(2)}, u32[]{:S(2)}) collective-permute-start(f32[32,128]{1,0:T(8,128)S(1)} %fusion.4), channel_id=1, source_target_pairs={{0,4},{2,6},{4,0},{6,2},{1,5},{3,7},{5,1},{7,3},{8,12},{10,14},{12... | collective-permute-start | bytes 49160 | tf_op jit(solution)/shard_map/ppermute | solution.py:44
  45.5 3.8 %collective-permute-start.6 = (f32[32,128]{1,0:T(8,128)S(1)}, f32[32,128]{1,0:T(8,128)S(1)}, u32[]{:S(2)}, u32[]{:S(2)}) collective-permute-start(f32[32,128]{1,0:T(8,128)S(1)} %fusion.4), channel_id=1, source_target_pairs={{0,6},{2,4},{4,2},{6,0},{1,7},{3,5},{5,3},{7,1},{8,14},{10,12},{12... | collective-permute-start | bytes 49160 | tf_op jit(solution)/shard_map/ppermute | solution.py:44
  47.0 2.6 %collective-permute-start.7 = (f32[32,128]{1,0:T(8,128)S(1)}, f32[32,128]{1,0:T(8,128)S(1)}, u32[]{:S(2)}, u32[]{:S(2)}) collective-permute-start(f32[32,128]{1,0:T(8,128)S(1)} %fusion.4), channel_id=1, source_target_pairs={{0,2},{2,0},{4,6},{6,4},{1,3},{3,1},{5,7},{7,5},{8,10},{10,8},{12,... | collective-permute-start | bytes 49160 | tf_op jit(solution)/shard_map/ppermute | solution.py:44

commit v3 on v1

--- a/solution.py
+++ b/solution.py
@@ -29,6 +29,12 @@
 def swap(values, axis, mask):
     size = lax.axis_size(axis)
     return lax.ppermute(values, axis, [(k, k ^ mask) for k in range(size)])
+
+
+def swap_by_core(values, masks):
+    ys = lax.axis_size("y")
+    pairs = [(c * ys + y, c * ys + (y ^ mask)) for c, mask in enumerate(masks) for y in range(ys)]
+    return lax.ppermute(values, ("c", "y"), pairs)
 
 
 def to_all(held, axes, size):
@@ -63,12 +69,16 @@
     pieces = jnp.stack(pieces)
     y = lax.axis_index("y")
     piece = lambda k: lax.dynamic_index_in_dim(pieces, k, 0, keepdims=False)
-    half = piece(y) + sum(swap(piece(y ^ mask), "y", mask) for mask in (1, 3, 2))
+    turns = ((2, 2), (3, 1), (1, 3))
+    half = piece(y)
+    for masks in turns:
+        half = half + swap_by_core(piece(y ^ jnp.where(lax.axis_index("c") == 0, *masks)), masks)
     sums = half + swap(half, "zh", 1)
     outer = zhs * rows
     outs, ins = sums[:outer], sums[outer:]
     own = jnp.concatenate([outer_rows(outs[0::2], ins), outer_rows(outs[1::2], ins)], axis=1)
     every = to_all(own.astype(jnp.bfloat16), DP, zls * xs * cores)
+    other, every = lax.optimization_barrier((other, every))
     first_half = lax.axis_index("zh") == 0
     low, high = jnp.where(first_half, queries, other), jnp.where(first_half, other, queries)
     scores = lax.dot_general(

time: 50.8 us -> 51.5 us (1.014)
  waiting for transfers between devices: 17.4 us -> 20.6 us
  starting transfers between devices: 26.8 us -> 24.3 us
    ppermute x0 -> x3, waiting for transfers between devices: none -> 6.51 us  [swap_by_core(): return lax.ppermute(values, ('c', 'y'), pairs)]
    ppermute x8 -> x5, starting transfers between devices: 14.9 us -> 9.42 us  [swap(): return lax.ppermute(values, axis, [(k, k ^ mask) for k in range(size)])]
    ppermute x0 -> x3, starting transfers between devices: none -> 4.61 us  [swap_by_core(): return lax.ppermute(values, ('c', 'y'), pairs)]
    ppermute x8 -> x5, waiting for transfers between devices: 8.94 us -> 4.98 us  [swap(): return lax.ppermute(values, axis, [(k, k ^ mask) for k in range(size)])]
    all_to_all x1, starting transfers between devices: 11.9 us -> 10.3 us  [exchange(): return lax.all_to_all(pieces, axes, split_axis=0, concat_axis=0, tiled=True)]
    all_to_all x1, waiting for transfers between devices: 8.49 us -> 9.12 us  [exchange(): return lax.all_to_all(pieces, axes, split_axis=0, concat_axis=0, tiled=True)]
where the time goes in v3:
time: 51.5 us; the launch traced here: 51.3 us
  starting transfers between devices  24.3 us (47%)
  waiting for transfers between devices  20.6 us (40%)
  matrix products  2.48 us (5%)
  other arithmetic  2.22 us (4%)
  local copies, waits for them, and re-layouts  1.46 us (3%)
    all_to_all x1, starting transfers between devices, exchange(): return lax.all_to_all(pieces, axes, split_axis=0, concat_axis=0, tiled=True)  10.3 us
    ppermute x5, starting transfers between devices, swap(): return lax.ppermute(values, axis, [(k, k ^ mask) for k in range(size)])  9.42 us
    all_to_all x1, waiting for transfers between devices, exchange(): return lax.all_to_all(pieces, axes, split_axis=0, concat_axis=0, tiled=True)  9.12 us
    ppermute x3, waiting for transfers between devices, swap_by_core(): return lax.ppermute(values, ('c', 'y'), pairs)  6.51 us
    ppermute x5, waiting for transfers between devices, swap(): return lax.ppermute(values, axis, [(k, k ^ mask) for k in range(size)])  4.98 us
    ppermute x3, starting transfers between devices, swap_by_core(): return lax.ppermute(values, ('c', 'y'), pairs)  4.61 us
    dot_general x4, matrix products, project_columns(): lax.dot_general(proj, acts[0], (((0,), (1,)), ((), ())), preferred_elemen...  1.89 us
    concatenate x1, other arithmetic, per_device(): wide_proj = jnp.concatenate([up_out_proj, down_in_proj], axis=1)  1.37 us
  transfers between devices with their start and end apart: 9, of which 7 were waited for; matrix products, arithmetic and copies ran while one was open for 2% of the time, Pallas kernels for 0%

profile of v3, /device:TPU:1, one launch (start us, length us, event | category | flops | bytes accessed | tf_op | source)
XLA Modules:
  0.0 51.3 jit_solution(11214151515271904305)
XLA Ops:
  0.1 1.4 %pad_maximum_fusion = bf16[3584,128]{0,1:T(8,128)(2,1)S(1)} fusion(bf16[3584,64]{0,1:T(8,128)(2,1)} %param.15, bf16[3584,64]{0,1:T(8,128)(2,1)} %param.14), kind=kLoop, calls=%fused_computation.6 | loop fusion | flops 1835008 | bytes 1835008 | tf_op jit(solution)/shard_map/concatenate | solution.py:61
  1.5 0.3 fusion.10
  1.8 0.3 fusion.8
  2.2 0.7 %fusion.2 = f32[64,256]{1,0:T(8,128)S(1)} fusion(bf16[1,256,3584]{2,1,0:T(8,128)(2,1)S(1)} %copy-done, bf16[3584,128]{0,1:T(8,128)(2,1)S(1)} %pad_maximum_fusion), kind=kOutput, calls=%fused_computation.2 | convolution fusion | flops 117440512 | bytes 2359296 | tf_op jit(solution)/shard_map/dot_general | solution.py:13
  2.9 0.5 %copy-done.1 = bf16[1,256,3584]{2,1,0:T(8,128)(2,1)S(1)} copy-done((bf16[1,256,3584]{2,1,0:T(8,128)(2,1)S(1)}, bf16[1,256,3584]{2,1,0:T(8,128)(2,1)}, u32[]{:S(2)}) %copy-start.1) | copy-done | bytes 1835032
  3.4 0.7 %fusion = f32[64,256]{1,0:T(8,128)S(1)} fusion(bf16[1,256,3584]{2,1,0:T(8,128)(2,1)S(1)} %copy-done.1, bf16[3584,128]{0,1:T(8,128)(2,1)S(1)} %pad_maximum_fusion), kind=kOutput, calls=%fused_computation | convolution fusion | flops 117440512 | bytes 2359296 | tf_op jit(solution)/shard_map/dot_general | solution.py:13
  4.2 3.8 %collective-permute-start.1 = (f32[96,256]{1,0:T(8,128)S(1)}, f32[96,256]{1,0:T(8,128)S(1)}, u32[]{:S(2)}, u32[]{:S(2)}) collective-permute-start(f32[96,256]{1,0:T(8,128)S(1)} %get-tuple-element.17), channel_id=1, source_target_pairs={{0,4},{2,6},{4,0},{6,2},{8,12},{10,14},{12,8},{14,10},{1,5},{3,7},... | collective-permute-start | bytes 294920 | tf_op jit(solution)/shard_map/ppermute | solution.py:37
  8.1 0.4 collective-permute-start.2
  8.5 0.4 collective-permute-start.3
  8.8 1.2 %collective-permute-done.1 = f32[96,256]{1,0:T(8,128)S(1)} collective-permute-done((f32[96,256]{1,0:T(8,128)S(1)}, f32[96,256]{1,0:T(8,128)S(1)}, u32[]{:S(2)}, u32[]{:S(2)}) %collective-permute-start.1) | collective-permute-done | bytes 98336 | tf_op jit(solution)/shard_map/ppermute | solution.py:37
  10.1 2.7 %collective-permute-done.2 = f32[96,256]{1,0:T(8,128)S(1)} collective-permute-done((f32[96,256]{1,0:T(8,128)S(1)}, f32[96,256]{1,0:T(8,128)S(1)}, u32[]{:S(2)}, u32[]{:S(2)}) %collective-permute-start.2) | collective-permute-done | bytes 98336 | tf_op jit(solution)/shard_map/ppermute | solution.py:37
  12.8 2.5 %collective-permute-done.3 = f32[96,256]{1,0:T(8,128)S(1)} collective-permute-done((f32[96,256]{1,0:T(8,128)S(1)}, f32[96,256]{1,0:T(8,128)S(1)}, u32[]{:S(2)}, u32[]{:S(2)}) %collective-permute-start.3) | collective-permute-done | bytes 98336 | tf_op jit(solution)/shard_map/ppermute | solution.py:37
  15.4 5.1 %collective-permute-start.4 = (f32[96,256]{1,0:T(8,128)S(1)}, f32[96,256]{1,0:T(8,128)S(1)}, u32[]{:S(2)}, u32[]{:S(2)}) collective-permute-start(f32[96,256]{1,0:T(8,128)S(1)} %fusion.21), channel_id=1, source_target_pairs={{0,1},{1,0},{2,3},{3,2},{4,5},{5,4},{6,7},{7,6},{8,9},{9,8},{10,11... | collective-permute-start | bytes 294920 | tf_op jit(solution)/shard_map/ppermute | solution.py:31
  20.5 0.3 collective-permute-start
  20.8 2.1 %collective-permute-done.4 = f32[96,256]{1,0:T(8,128)S(1)} collective-permute-done((f32[96,256]{1,0:T(8,128)S(1)}, f32[96,256]{1,0:T(8,128)S(1)}, u32[]{:S(2)}, u32[]{:S(2)}) %collective-permute-start.4) | collective-permute-done | bytes 98336 | tf_op jit(solution)/shard_map/ppermute | solution.py:31
  23.4 0.7 %broadcast_in_dim.3 = bf16[32,16,128]{2,1,0:T(8,128)(2,1)} broadcast(bf16[16,128]{1,0:T(8,128)(2,1)S(1)} %pad_maximum_fusion.6), dimensions={1,2} | broadcast | bytes 135168 | tf_op jit(solution)/shard_map/broadcast_in_dim | solution.py:41
  24.1 10.3 %all-to-all-start = ((bf16[32,16,128]{2,1,0:T(8,128)(2,1)}), bf16[32,16,128]{2,1,0:T(8,128)(2,1)S(1)}, u32[]{:S(2)}, u32[]{:S(2)}) async-start(bf16[32,16,128]{2,1,0:T(8,128)(2,1)} %broadcast_in_dim.3), calls=%async_computation | async-start | bytes 262144 | tf_op jit(solution)/shard_map/all_to_all | solution.py:26
  34.4 9.1 %all-to-all-done = bf16[32,16,128]{2,1,0:T(8,128)(2,1)S(1)} async-done(((bf16[32,16,128]{2,1,0:T(8,128)(2,1)}), bf16[32,16,128]{2,1,0:T(8,128)(2,1)S(1)}, u32[]{:S(2)}, u32[]{:S(2)}) %all-to-all-start) | async-done | bytes 131104 | tf_op jit(solution)/shard_map/all_to_all | solution.py:26
  43.6 0.3 fusion.4
  43.9 3.0 %collective-permute-start.5 = (f32[32,128]{1,0:T(8,128)S(1)}, f32[32,128]{1,0:T(8,128)S(1)}, u32[]{:S(2)}, u32[]{:S(2)}) collective-permute-start(f32[32,128]{1,0:T(8,128)S(1)} %fusion.4), channel_id=1, source_target_pairs={{0,4},{2,6},{4,0},{6,2},{1,5},{3,7},{5,1},{7,3},{8,12},{10,14},{12... | collective-permute-start | bytes 49160 | tf_op jit(solution)/shard_map/ppermute | solution.py:31
  46.9 0.9 %collective-permute-start.6 = (f32[32,128]{1,0:T(8,128)S(1)}, f32[32,128]{1,0:T(8,128)S(1)}, u32[]{:S(2)}, u32[]{:S(2)}) collective-permute-start(f32[32,128]{1,0:T(8,128)S(1)} %fusion.4), channel_id=1, source_target_pairs={{0,6},{2,4},{4,2},{6,0},{1,7},{3,5},{5,3},{7,1},{8,14},{10,12},{12... | collective-permute-start | bytes 49160 | tf_op jit(solution)/shard_map/ppermute | solution.py:31
  47.8 0.2 collective-permute-done.5
  48.0 2.7 %collective-permute-done.6 = f32[32,128]{1,0:T(8,128)S(1)} collective-permute-done((f32[32,128]{1,0:T(8,128)S(1)}, f32[32,128]{1,0:T(8,128)S(1)}, u32[]{:S(2)}, u32[]{:S(2)}) %collective-permute-start.6) | collective-permute-done | bytes 16416 | tf_op jit(solution)/shard_map/ppermute | solution.py:31
  50.7 0.6 %add_add_fusion = f32[32,128]{1,0:T(8,128)} fusion(f32[32,128]{1,0:T(8,128)S(1)} %collective-permute-done.7, f32[32,128]{1,0:T(8,128)S(1)} %fusion.4, f32[32,128]{1,0:T(8,128)S(1)} %collective-permute-done.5, f32[32,128]{1,0:T(8,128)S(1)} %collective-permute-done.6), kind=kLoop, calls=%fused_computation.38 | loop fusion | flops 12288 | bytes 81920 | tf_op jit(solution)/shard_map/add | solution.py:89
  (30 shorter events, 0.8 us)
Async XLA Ops:
  0.0 2.2 %copy-start = (bf16[1,256,3584]{2,1,0:T(8,128)(2,1)S(1)}, bf16[1,256,3584]{2,1,0:T(8,128)(2,1)}, u32[]{:S(2)}) copy-start(bf16[1,256,3584]{2,1,0:T(8,128)(2,1)} %param.10) | copy-start | bytes 5505028
  0.0 1.4 %copy-start.5 = (bf16[1024,64]{0,1:T(8,128)(2,1)S(1)}, bf16[1024,64]{0,1:T(8,128)(2,1)}, u32[]{:S(2)}) copy-start(bf16[1024,64]{0,1:T(8,128)(2,1)} %param.13) | copy-start | bytes 393220
  0.0 1.5 %copy-start.2 = (bf16[1,256,1024]{2,1,0:T(8,128)(2,1)S(1)}, bf16[1,256,1024]{2,1,0:T(8,128)(2,1)}, u32[]{:S(2)}) copy-start(bf16[1,256,1024]{2,1,0:T(8,128)(2,1)} %param.9) | copy-start | bytes 1572868
  0.0 1.8 %copy-start.3 = (bf16[1,256,1024]{2,1,0:T(8,128)(2,1)S(1)}, bf16[1,256,1024]{2,1,0:T(8,128)(2,1)}, u32[]{:S(2)}) copy-start(bf16[1,256,1024]{2,1,0:T(8,128)(2,1)} %param.12) | copy-start | bytes 1572868
  0.0 1.8 %copy-start.6 = (bf16[1024,64]{0,1:T(8,128)(2,1)S(1)}, bf16[1024,64]{0,1:T(8,128)(2,1)}, u32[]{:S(2)}) copy-start(bf16[1024,64]{0,1:T(8,128)(2,1)} %param.16) | copy-start | bytes 393220
  1.8 1.6 %copy-start.1 = (bf16[1,256,3584]{2,1,0:T(8,128)(2,1)S(1)}, bf16[1,256,3584]{2,1,0:T(8,128)(2,1)}, u32[]{:S(2)}) copy-start(bf16[1,256,3584]{2,1,0:T(8,128)(2,1)} %param.11) | copy-start | bytes 5505028
  4.1 16.4 %copy-start.4 = (bf16[128,1024]{1,0:T(8,128)(2,1)S(1)}, bf16[128,1024]{1,0:T(8,128)(2,1)}, u32[]{:S(2)}) copy-start(bf16[128,1024]{1,0:T(8,128)(2,1)} %param.17) | copy-start | bytes 786436
  4.2 5.8 %collective-permute-start.1 = (f32[96,256]{1,0:T(8,128)S(1)}, f32[96,256]{1,0:T(8,128)S(1)}, u32[]{:S(2)}, u32[]{:S(2)}) collective-permute-start(f32[96,256]{1,0:T(8,128)S(1)} %get-tuple-element.17), channel_id=1, source_target_pairs={{0,4},{2,6},{4,0},{6,2},{8,12},{10,14},{12,8},{14,10},{1,5},{3,7},... | collective-permute-start | bytes 294920 | tf_op jit(solution)/shard_map/ppermute | solution.py:37
  8.1 4.7 %collective-permute-start.2 = (f32[96,256]{1,0:T(8,128)S(1)}, f32[96,256]{1,0:T(8,128)S(1)}, u32[]{:S(2)}, u32[]{:S(2)}) collective-permute-start(f32[96,256]{1,0:T(8,128)S(1)} %get-tuple-element.19), channel_id=1, source_target_pairs={{0,6},{2,4},{4,2},{6,0},{8,10},{10,8},{12,14},{14,12},{1,7},{3,5},... | collective-permute-start | bytes 294920 | tf_op jit(solution)/shard_map/ppermute | solution.py:37
  8.5 6.9 %collective-permute-start.3 = (f32[96,256]{1,0:T(8,128)S(1)}, f32[96,256]{1,0:T(8,128)S(1)}, u32[]{:S(2)}, u32[]{:S(2)}) collective-permute-start(f32[96,256]{1,0:T(8,128)S(1)} %get-tuple-element.18), channel_id=1, source_target_pairs={{0,2},{2,0},{4,6},{6,4},{8,14},{10,12},{12,10},{14,8},{1,3},{3,1},... | collective-permute-start | bytes 294920 | tf_op jit(solution)/shard_map/ppermute | solution.py:37
  15.4 7.6 %collective-permute-start.4 = (f32[96,256]{1,0:T(8,128)S(1)}, f32[96,256]{1,0:T(8,128)S(1)}, u32[]{:S(2)}, u32[]{:S(2)}) collective-permute-start(f32[96,256]{1,0:T(8,128)S(1)} %fusion.21), channel_id=1, source_target_pairs={{0,1},{1,0},{2,3},{3,2},{4,5},{5,4},{6,7},{7,6},{8,9},{9,8},{10,11... | collective-permute-start | bytes 294920 | tf_op jit(solution)/shard_map/ppermute | solution.py:31
  20.5 13.9 %collective-permute-start = (bf16[128,1024]{1,0:T(8,128)(2,1)S(1)}, bf16[128,1024]{1,0:T(8,128)(2,1)S(1)}, u32[]{:S(2)}, u32[]{:S(2)}) collective-permute-start(bf16[128,1024]{1,0:T(8,128)(2,1)S(1)} %copy-done.4), channel_id=1, source_target_pairs={{0,1},{1,0},{2,3},{3,2},{4,5},{5,4},{6,7},{7,6},{8,9},{9,8},{10,11... | collective-permute-start | bytes 786440 | tf_op jit(solution)/shard_map/ppermute | solution.py:31
  24.1 19.5 %all-to-all-start = ((bf16[32,16,128]{2,1,0:T(8,128)(2,1)}), bf16[32,16,128]{2,1,0:T(8,128)(2,1)S(1)}, u32[]{:S(2)}, u32[]{:S(2)}) async-start(bf16[32,16,128]{2,1,0:T(8,128)(2,1)} %broadcast_in_dim.3), calls=%async_computation | async-start | bytes 262144 | tf_op jit(solution)/shard_map/all_to_all | solution.py:26
  43.9 4.2 %collective-permute-start.5 = (f32[32,128]{1,0:T(8,128)S(1)}, f32[32,128]{1,0:T(8,128)S(1)}, u32[]{:S(2)}, u32[]{:S(2)}) collective-permute-start(f32[32,128]{1,0:T(8,128)S(1)} %fusion.4), channel_id=1, source_target_pairs={{0,4},{2,6},{4,0},{6,2},{1,5},{3,7},{5,1},{7,3},{8,12},{10,14},{12... | collective-permute-start | bytes 49160 | tf_op jit(solution)/shard_map/ppermute | solution.py:31
  46.9 3.8 %collective-permute-start.6 = (f32[32,128]{1,0:T(8,128)S(1)}, f32[32,128]{1,0:T(8,128)S(1)}, u32[]{:S(2)}, u32[]{:S(2)}) collective-permute-start(f32[32,128]{1,0:T(8,128)S(1)} %fusion.4), channel_id=1, source_target_pairs={{0,6},{2,4},{4,2},{6,0},{1,7},{3,5},{5,3},{7,1},{8,14},{10,12},{12... | collective-permute-start | bytes 49160 | tf_op jit(solution)/shard_map/ppermute | solution.py:31
  47.8 2.9 %collective-permute-start.7 = (f32[32,128]{1,0:T(8,128)S(1)}, f32[32,128]{1,0:T(8,128)S(1)}, u32[]{:S(2)}, u32[]{:S(2)}) collective-permute-start(f32[32,128]{1,0:T(8,128)S(1)} %fusion.4), channel_id=1, source_target_pairs={{0,2},{2,0},{4,6},{6,4},{1,3},{3,1},{5,7},{7,5},{8,10},{10,8},{12,... | collective-permute-start | bytes 49160 | tf_op jit(solution)/shard_map/ppermute | solution.py:31

commit v4 on v1

--- a/solution.py
+++ b/solution.py
@@ -46,7 +46,7 @@
     down_out_proj,
     queries,
 ):
-    zls, xs, cores, ys, zhs = SIZES
+    zls, xs, _, ys, zhs = SIZES
     rank = up_in_proj.shape[1]
     rows = 2 * rank // ys // zhs
     other = swap(queries, "zh", 1)
@@ -68,7 +68,11 @@
     outer = zhs * rows
     outs, ins = sums[:outer], sums[outer:]
     own = jnp.concatenate([outer_rows(outs[0::2], ins), outer_rows(outs[1::2], ins)], axis=1)
-    every = to_all(own.astype(jnp.bfloat16), DP, zls * xs * cores)
+    near = to_all(own.astype(jnp.bfloat16), ("zl", "x"), zls * xs)
+    far = swap(near, "c", 1)
+    second = lax.axis_index("c") == 1
+    every = jnp.stack([jnp.where(second, far, near), jnp.where(second, near, far)], axis=1)
+    every = every.reshape((-1,) + own.shape)
     first_half = lax.axis_index("zh") == 0
     low, high = jnp.where(first_half, queries, other), jnp.where(first_half, other, queries)
     scores = lax.dot_general(

time: 50.8 us -> 51.5 us (1.014)
  waiting for transfers between devices: 17.4 us -> 18.8 us
  starting transfers between devices: 26.8 us -> 26.1 us
    all_to_all x1, starting transfers between devices: 11.9 us -> 6.62 us  [exchange(): return lax.all_to_all(pieces, axes, split_axis=0, concat_axis=0, tiled=True)]
    ppermute x8 -> x9, starting transfers between devices: 14.9 us -> 19.5 us  [swap(): return lax.ppermute(values, axis, [(k, k ^ mask) for k in range(size)])]
    ppermute x8 -> x9, waiting for transfers between devices: 8.94 us -> 9.79 us  [swap(): return lax.ppermute(values, axis, [(k, k ^ mask) for k in range(size)])]
    all_to_all x1, waiting for transfers between devices: 8.49 us -> 9.03 us  [exchange(): return lax.all_to_all(pieces, axes, split_axis=0, concat_axis=0, tiled=True)]
  transfers between devices with their start and end apart: 9 -> 10, of which waited for: 7 -> 8; matrix products, arithmetic and copies ran while one was open for 2% -> 2% of each run, Pallas kernels for 0% -> 0%
where the time goes in v4:
time: 51.5 us; the launch traced here: 51.3 us
  starting transfers between devices  26.1 us (51%)
  waiting for transfers between devices  18.8 us (37%)
  matrix products  2.48 us (5%)
  other arithmetic  2.25 us (4%)
  local copies, waits for them, and re-layouts  1.43 us (3%)
    ppermute x9, starting transfers between devices, swap(): return lax.ppermute(values, axis, [(k, k ^ mask) for k in range(size)])  19.5 us
    ppermute x9, waiting for transfers between devices, swap(): return lax.ppermute(values, axis, [(k, k ^ mask) for k in range(size)])  9.79 us
    all_to_all x1, waiting for transfers between devices, exchange(): return lax.all_to_all(pieces, axes, split_axis=0, concat_axis=0, tiled=True)  9.03 us
    all_to_all x1, starting transfers between devices, exchange(): return lax.all_to_all(pieces, axes, split_axis=0, concat_axis=0, tiled=True)  6.62 us
    dot_general x4, matrix products, project_columns(): lax.dot_general(proj, acts[0], (((0,), (1,)), ((), ())), preferred_elemen...  1.89 us
    concatenate x1, other arithmetic, per_device(): wide_proj = jnp.concatenate([up_out_proj, down_in_proj], axis=1)  1.37 us
  transfers between devices with their start and end apart: 10, of which 8 were waited for; matrix products, arithmetic and copies ran while one was open for 2% of the time, Pallas kernels for 0%

profile of v4, /device:TPU:1, one launch (start us, length us, event | category | flops | bytes accessed | tf_op | source)
XLA Modules:
  0.0 51.3 jit_solution(17507457859700657562)
XLA Ops:
  0.0 1.4 %pad_maximum_fusion = bf16[3584,128]{0,1:T(8,128)(2,1)S(1)} fusion(bf16[3584,64]{0,1:T(8,128)(2,1)} %param.15, bf16[3584,64]{0,1:T(8,128)(2,1)} %param.14), kind=kLoop, calls=%fused_computation.6 | loop fusion | flops 1835008 | bytes 1835008 | tf_op jit(solution)/shard_map/concatenate | solution.py:55
  1.5 0.3 fusion.10
  1.8 0.3 fusion.8
  2.2 0.7 %fusion.2 = f32[64,256]{1,0:T(8,128)S(1)} fusion(bf16[1,256,3584]{2,1,0:T(8,128)(2,1)S(1)} %copy-done, bf16[3584,128]{0,1:T(8,128)(2,1)S(1)} %pad_maximum_fusion), kind=kOutput, calls=%fused_computation.2 | convolution fusion | flops 117440512 | bytes 2359296 | tf_op jit(solution)/shard_map/dot_general | solution.py:13
  2.9 0.5 %copy-done.1 = bf16[1,256,3584]{2,1,0:T(8,128)(2,1)S(1)} copy-done((bf16[1,256,3584]{2,1,0:T(8,128)(2,1)S(1)}, bf16[1,256,3584]{2,1,0:T(8,128)(2,1)}, u32[]{:S(2)}) %copy-start.1) | copy-done | bytes 1835032
  3.4 0.7 %fusion = f32[64,256]{1,0:T(8,128)S(1)} fusion(bf16[1,256,3584]{2,1,0:T(8,128)(2,1)S(1)} %copy-done.1, bf16[3584,128]{0,1:T(8,128)(2,1)S(1)} %pad_maximum_fusion), kind=kOutput, calls=%fused_computation | convolution fusion | flops 117440512 | bytes 2359296 | tf_op jit(solution)/shard_map/dot_general | solution.py:13
  4.2 2.2 %collective-permute-start = (f32[96,256]{1,0:T(8,128)S(1)}, f32[96,256]{1,0:T(8,128)S(1)}, u32[]{:S(2)}, u32[]{:S(2)}) collective-permute-start(f32[96,256]{1,0:T(8,128)S(1)} %get-tuple-element.15), channel_id=1, source_target_pairs={{0,2},{2,0},{4,6},{6,4},{1,3},{3,1},{5,7},{7,5},{8,10},{10,8},{12,... | collective-permute-start | bytes 294920 | tf_op jit(solution)/shard_map/ppermute | solution.py:31
  6.4 1.9 %collective-permute-start.1 = (f32[96,256]{1,0:T(8,128)S(1)}, f32[96,256]{1,0:T(8,128)S(1)}, u32[]{:S(2)}, u32[]{:S(2)}) collective-permute-start(f32[96,256]{1,0:T(8,128)S(1)} %get-tuple-element.13), channel_id=1, source_target_pairs={{0,6},{2,4},{4,2},{6,0},{1,7},{3,5},{5,3},{7,1},{8,14},{10,12},{12... | collective-permute-start | bytes 294920 | tf_op jit(solution)/shard_map/ppermute | solution.py:31
  8.3 0.7 %collective-permute-start.2 = (f32[96,256]{1,0:T(8,128)S(1)}, f32[96,256]{1,0:T(8,128)S(1)}, u32[]{:S(2)}, u32[]{:S(2)}) collective-permute-start(f32[96,256]{1,0:T(8,128)S(1)} %get-tuple-element.14), channel_id=1, source_target_pairs={{0,4},{2,6},{4,0},{6,2},{1,5},{3,7},{5,1},{7,3},{8,12},{10,14},{12... | collective-permute-start | bytes 294920 | tf_op jit(solution)/shard_map/ppermute | solution.py:31
  9.1 2.1 %collective-permute-done.1 = f32[96,256]{1,0:T(8,128)S(1)} collective-permute-done((f32[96,256]{1,0:T(8,128)S(1)}, f32[96,256]{1,0:T(8,128)S(1)}, u32[]{:S(2)}, u32[]{:S(2)}) %collective-permute-start.1) | collective-permute-done | bytes 98336 | tf_op jit(solution)/shard_map/ppermute | solution.py:31
  11.1 2.3 %collective-permute-done.2 = f32[96,256]{1,0:T(8,128)S(1)} collective-permute-done((f32[96,256]{1,0:T(8,128)S(1)}, f32[96,256]{1,0:T(8,128)S(1)}, u32[]{:S(2)}, u32[]{:S(2)}) %collective-permute-start.2) | collective-permute-done | bytes 98336 | tf_op jit(solution)/shard_map/ppermute | solution.py:31
  13.4 7.0 %collective-permute-start.3 = (f32[96,256]{1,0:T(8,128)S(1)}, f32[96,256]{1,0:T(8,128)S(1)}, u32[]{:S(2)}, u32[]{:S(2)}) collective-permute-start(f32[96,256]{1,0:T(8,128)S(1)} %bitcast_add_fusion), channel_id=1, source_target_pairs={{0,1},{1,0},{2,3},{3,2},{4,5},{5,4},{6,7},{7,6},{8,9},{9,8},{10,11... | collective-permute-start | bytes 294920 | tf_op jit(solution)/shard_map/ppermute | solution.py:31
  20.6 2.0 %collective-permute-done.3 = f32[96,256]{1,0:T(8,128)S(1)} collective-permute-done((f32[96,256]{1,0:T(8,128)S(1)}, f32[96,256]{1,0:T(8,128)S(1)}, u32[]{:S(2)}, u32[]{:S(2)}) %collective-permute-start.3) | collective-permute-done | bytes 98336 | tf_op jit(solution)/shard_map/ppermute | solution.py:31
  23.0 0.6 %broadcast_in_dim.3 = bf16[16,16,128]{2,1,0:T(8,128)(2,1)} broadcast(bf16[16,128]{1,0:T(8,128)(2,1)S(1)} %pad_maximum_fusion.7), dimensions={1,2} | broadcast | bytes 69632 | tf_op jit(solution)/shard_map/broadcast_in_dim | solution.py:35
  23.7 6.6 %all-to-all-start = ((bf16[16,16,128]{2,1,0:T(8,128)(2,1)}), bf16[16,16,128]{2,1,0:T(8,128)(2,1)S(1)}, u32[]{:S(2)}, u32[]{:S(2)}) async-start(bf16[16,16,128]{2,1,0:T(8,128)(2,1)} %broadcast_in_dim.3), calls=%async_computation | async-start | bytes 131072 | tf_op jit(solution)/shard_map/all_to_all | solution.py:26
  30.3 9.0 %all-to-all-done = bf16[16,16,128]{2,1,0:T(8,128)(2,1)S(1)} async-done(((bf16[16,16,128]{2,1,0:T(8,128)(2,1)}), bf16[16,16,128]{2,1,0:T(8,128)(2,1)S(1)}, u32[]{:S(2)}, u32[]{:S(2)}) %all-to-all-start) | async-done | bytes 65568 | tf_op jit(solution)/shard_map/all_to_all | solution.py:26
  39.3 4.6 %collective-permute-start.4 = (bf16[16,16,128]{2,1,0:T(8,128)(2,1)S(1)}, bf16[16,16,128]{2,1,0:T(8,128)(2,1)S(1)}, u32[]{:S(2)}, u32[]{:S(2)}) collective-permute-start(bf16[16,16,128]{2,1,0:T(8,128)(2,1)S(1)} %all-to-all-done), channel_id=1, source_target_pairs={{0,8},{8,0},{1,9},{9,1},{2,10},{10,2},{3,11},{11,3},{4,12},{12,4},... | collective-permute-start | bytes 196616 | tf_op jit(solution)/shard_map/ppermute | solution.py:31
  44.0 0.9 %collective-permute-done.4 = bf16[16,16,128]{2,1,0:T(8,128)(2,1)S(1)} collective-permute-done((bf16[16,16,128]{2,1,0:T(8,128)(2,1)S(1)}, bf16[16,16,128]{2,1,0:T(8,128)(2,1)S(1)}, u32[]{:S(2)}, u32[]{:S(2)}) %collective-permute-start.4) | collective-permute-done | bytes 65568 | tf_op jit(solution)/shard_map/ppermute | solution.py:31
  45.2 1.4 %collective-permute-start.6 = (f32[32,128]{1,0:T(8,128)S(1)}, f32[32,128]{1,0:T(8,128)S(1)}, u32[]{:S(2)}, u32[]{:S(2)}) collective-permute-start(f32[32,128]{1,0:T(8,128)S(1)} %fusion.4), channel_id=1, source_target_pairs={{0,4},{2,6},{4,0},{6,2},{1,5},{3,7},{5,1},{7,3},{8,12},{10,14},{12... | collective-permute-start | bytes 49160 | tf_op jit(solution)/shard_map/ppermute | solution.py:31
  46.5 1.6 %collective-permute-start.7 = (f32[32,128]{1,0:T(8,128)S(1)}, f32[32,128]{1,0:T(8,128)S(1)}, u32[]{:S(2)}, u32[]{:S(2)}) collective-permute-start(f32[32,128]{1,0:T(8,128)S(1)} %fusion.4), channel_id=1, source_target_pairs={{0,6},{2,4},{4,2},{6,0},{1,7},{3,5},{5,3},{7,1},{8,14},{10,12},{12... | collective-permute-start | bytes 49160 | tf_op jit(solution)/shard_map/ppermute | solution.py:31
  48.1 1.2 %collective-permute-done.6 = f32[32,128]{1,0:T(8,128)S(1)} collective-permute-done((f32[32,128]{1,0:T(8,128)S(1)}, f32[32,128]{1,0:T(8,128)S(1)}, u32[]{:S(2)}, u32[]{:S(2)}) %collective-permute-start.6) | collective-permute-done | bytes 16416 | tf_op jit(solution)/shard_map/ppermute | solution.py:31
  49.3 1.1 %collective-permute-done.7 = f32[32,128]{1,0:T(8,128)S(1)} collective-permute-done((f32[32,128]{1,0:T(8,128)S(1)}, f32[32,128]{1,0:T(8,128)S(1)}, u32[]{:S(2)}, u32[]{:S(2)}) %collective-permute-start.7) | collective-permute-done | bytes 16416 | tf_op jit(solution)/shard_map/ppermute | solution.py:31
  50.4 0.3 collective-permute-done.8
  50.7 0.6 %add_add_fusion = f32[32,128]{1,0:T(8,128)} fusion(f32[32,128]{1,0:T(8,128)S(1)} %collective-permute-done.8, f32[32,128]{1,0:T(8,128)S(1)} %fusion.4, f32[32,128]{1,0:T(8,128)S(1)} %collective-permute-done.6, f32[32,128]{1,0:T(8,128)S(1)} %collective-permute-done.7), kind=kLoop, calls=%fused_computation.39 | loop fusion | flops 12288 | bytes 81920 | tf_op jit(solution)/shard_map/add | solution.py:83
  (34 shorter events, 1.2 us)
Async XLA Ops:
  0.0 2.2 %copy-start = (bf16[1,256,3584]{2,1,0:T(8,128)(2,1)S(1)}, bf16[1,256,3584]{2,1,0:T(8,128)(2,1)}, u32[]{:S(2)}) copy-start(bf16[1,256,3584]{2,1,0:T(8,128)(2,1)} %param.10) | copy-start | bytes 5505028
  0.0 1.4 %copy-start.5 = (bf16[1024,64]{0,1:T(8,128)(2,1)S(1)}, bf16[1024,64]{0,1:T(8,128)(2,1)}, u32[]{:S(2)}) copy-start(bf16[1024,64]{0,1:T(8,128)(2,1)} %param.13) | copy-start | bytes 393220
  0.0 1.5 %copy-start.2 = (bf16[1,256,1024]{2,1,0:T(8,128)(2,1)S(1)}, bf16[1,256,1024]{2,1,0:T(8,128)(2,1)}, u32[]{:S(2)}) copy-start(bf16[1,256,1024]{2,1,0:T(8,128)(2,1)} %param.9) | copy-start | bytes 1572868
  0.0 1.8 %copy-start.3 = (bf16[1,256,1024]{2,1,0:T(8,128)(2,1)S(1)}, bf16[1,256,1024]{2,1,0:T(8,128)(2,1)}, u32[]{:S(2)}) copy-start(bf16[1,256,1024]{2,1,0:T(8,128)(2,1)} %param.12) | copy-start | bytes 1572868
  0.0 1.8 %copy-start.6 = (bf16[1024,64]{0,1:T(8,128)(2,1)S(1)}, bf16[1024,64]{0,1:T(8,128)(2,1)}, u32[]{:S(2)}) copy-start(bf16[1024,64]{0,1:T(8,128)(2,1)} %param.16) | copy-start | bytes 393220
  1.8 1.6 %copy-start.1 = (bf16[1,256,3584]{2,1,0:T(8,128)(2,1)S(1)}, bf16[1,256,3584]{2,1,0:T(8,128)(2,1)}, u32[]{:S(2)}) copy-start(bf16[1,256,3584]{2,1,0:T(8,128)(2,1)} %param.11) | copy-start | bytes 5505028
  4.1 16.4 %copy-start.4 = (bf16[128,1024]{1,0:T(8,128)(2,1)S(1)}, bf16[128,1024]{1,0:T(8,128)(2,1)}, u32[]{:S(2)}) copy-start(bf16[128,1024]{1,0:T(8,128)(2,1)} %param.17) | copy-start | bytes 786436
  4.2 4.8 %collective-permute-start = (f32[96,256]{1,0:T(8,128)S(1)}, f32[96,256]{1,0:T(8,128)S(1)}, u32[]{:S(2)}, u32[]{:S(2)}) collective-permute-start(f32[96,256]{1,0:T(8,128)S(1)} %get-tuple-element.15), channel_id=1, source_target_pairs={{0,2},{2,0},{4,6},{6,4},{1,3},{3,1},{5,7},{7,5},{8,10},{10,8},{12,... | collective-permute-start | bytes 294920 | tf_op jit(solution)/shard_map/ppermute | solution.py:31
  6.4 4.7 %collective-permute-start.1 = (f32[96,256]{1,0:T(8,128)S(1)}, f32[96,256]{1,0:T(8,128)S(1)}, u32[]{:S(2)}, u32[]{:S(2)}) collective-permute-start(f32[96,256]{1,0:T(8,128)S(1)} %get-tuple-element.13), channel_id=1, source_target_pairs={{0,6},{2,4},{4,2},{6,0},{1,7},{3,5},{5,3},{7,1},{8,14},{10,12},{12... | collective-permute-start | bytes 294920 | tf_op jit(solution)/shard_map/ppermute | solution.py:31
  8.3 5.1 %collective-permute-start.2 = (f32[96,256]{1,0:T(8,128)S(1)}, f32[96,256]{1,0:T(8,128)S(1)}, u32[]{:S(2)}, u32[]{:S(2)}) collective-permute-start(f32[96,256]{1,0:T(8,128)S(1)} %get-tuple-element.14), channel_id=1, source_target_pairs={{0,4},{2,6},{4,0},{6,2},{1,5},{3,7},{5,1},{7,3},{8,12},{10,14},{12... | collective-permute-start | bytes 294920 | tf_op jit(solution)/shard_map/ppermute | solution.py:31
  13.4 9.1 %collective-permute-start.3 = (f32[96,256]{1,0:T(8,128)S(1)}, f32[96,256]{1,0:T(8,128)S(1)}, u32[]{:S(2)}, u32[]{:S(2)}) collective-permute-start(f32[96,256]{1,0:T(8,128)S(1)} %bitcast_add_fusion), channel_id=1, source_target_pairs={{0,1},{1,0},{2,3},{3,2},{4,5},{5,4},{6,7},{7,6},{8,9},{9,8},{10,11... | collective-permute-start | bytes 294920 | tf_op jit(solution)/shard_map/ppermute | solution.py:31
  20.4 23.5 %collective-permute-start.5 = (bf16[128,1024]{1,0:T(8,128)(2,1)S(1)}, bf16[128,1024]{1,0:T(8,128)(2,1)S(1)}, u32[]{:S(2)}, u32[]{:S(2)}) collective-permute-start(bf16[128,1024]{1,0:T(8,128)(2,1)S(1)} %copy-done.4), channel_id=1, source_target_pairs={{0,1},{1,0},{2,3},{3,2},{4,5},{5,4},{6,7},{7,6},{8,9},{9,8},{10,11... | collective-permute-start | bytes 786440 | tf_op jit(solution)/shard_map/ppermute | solution.py:31
  23.7 15.7 %all-to-all-start = ((bf16[16,16,128]{2,1,0:T(8,128)(2,1)}), bf16[16,16,128]{2,1,0:T(8,128)(2,1)S(1)}, u32[]{:S(2)}, u32[]{:S(2)}) async-start(bf16[16,16,128]{2,1,0:T(8,128)(2,1)} %broadcast_in_dim.3), calls=%async_computation | async-start | bytes 131072 | tf_op jit(solution)/shard_map/all_to_all | solution.py:26
  39.3 5.5 %collective-permute-start.4 = (bf16[16,16,128]{2,1,0:T(8,128)(2,1)S(1)}, bf16[16,16,128]{2,1,0:T(8,128)(2,1)S(1)}, u32[]{:S(2)}, u32[]{:S(2)}) collective-permute-start(bf16[16,16,128]{2,1,0:T(8,128)(2,1)S(1)} %all-to-all-done), channel_id=1, source_target_pairs={{0,8},{8,0},{1,9},{9,1},{2,10},{10,2},{3,11},{11,3},{4,12},{12,4},... | collective-permute-start | bytes 196616 | tf_op jit(solution)/shard_map/ppermute | solution.py:31
  45.2 4.1 %collective-permute-start.6 = (f32[32,128]{1,0:T(8,128)S(1)}, f32[32,128]{1,0:T(8,128)S(1)}, u32[]{:S(2)}, u32[]{:S(2)}) collective-permute-start(f32[32,128]{1,0:T(8,128)S(1)} %fusion.4), channel_id=1, source_target_pairs={{0,4},{2,6},{4,0},{6,2},{1,5},{3,7},{5,1},{7,3},{8,12},{10,14},{12... | collective-permute-start | bytes 49160 | tf_op jit(solution)/shard_map/ppermute | solution.py:31
  46.5 3.9 %collective-permute-start.7 = (f32[32,128]{1,0:T(8,128)S(1)}, f32[32,128]{1,0:T(8,128)S(1)}, u32[]{:S(2)}, u32[]{:S(2)}) collective-permute-start(f32[32,128]{1,0:T(8,128)S(1)} %fusion.4), channel_id=1, source_target_pairs={{0,6},{2,4},{4,2},{6,0},{1,7},{3,5},{5,3},{7,1},{8,14},{10,12},{12... | collective-permute-start | bytes 49160 | tf_op jit(solution)/shard_map/ppermute | solution.py:31
  48.1 2.6 %collective-permute-start.8 = (f32[32,128]{1,0:T(8,128)S(1)}, f32[32,128]{1,0:T(8,128)S(1)}, u32[]{:S(2)}, u32[]{:S(2)}) collective-permute-start(f32[32,128]{1,0:T(8,128)S(1)} %fusion.4), channel_id=1, source_target_pairs={{0,2},{2,0},{4,6},{6,4},{1,3},{3,1},{5,7},{7,5},{8,10},{10,8},{12,... | collective-permute-start | bytes 49160 | tf_op jit(solution)/shard_map/ppermute | solution.py:31

commit v5 on v1

--- a/solution.py
+++ b/solution.py
@@ -49,7 +49,8 @@
     zls, xs, cores, ys, zhs = SIZES
     rank = up_in_proj.shape[1]
     rows = 2 * rank // ys // zhs
-    other = swap(queries, "zh", 1)
+    part = queries.shape[0] // 2
+    early, late = swap(queries[:part], "zh", 1), swap(queries[part:], "zh", 1)
     up_in = project_columns(up_inputs, up_in_proj)
     down_out = project_columns(down_grads, down_out_proj)
     wide_proj = jnp.concatenate([up_out_proj, down_in_proj], axis=1)
@@ -65,6 +66,8 @@
     piece = lambda k: lax.dynamic_index_in_dim(pieces, k, 0, keepdims=False)
     half = piece(y) + sum(swap(piece(y ^ mask), "y", mask) for mask in (1, 3, 2))
     sums = half + swap(half, "zh", 1)
+    sums, early = lax.optimization_barrier((sums, early))
+    other = jnp.concatenate([early, late], axis=0)
     outer = zhs * rows
     outs, ins = sums[:outer], sums[outer:]
     own = jnp.concatenate([outer_rows(outs[0::2], ins), outer_rows(outs[1::2], ins)], axis=1)

time: 50.8 us -> 54.2 us (1.067)
  starting transfers between devices: 26.8 us -> 33.2 us
  waiting for transfers between devices: 17.4 us -> 14.3 us
    ppermute x8 -> x9, starting transfers between devices: 14.9 us -> 22.5 us  [swap(): return lax.ppermute(values, axis, [(k, k ^ mask) for k in range(size)])]
    ppermute x8 -> x9, waiting for transfers between devices: 8.94 us -> 5.9 us  [swap(): return lax.ppermute(values, axis, [(k, k ^ mask) for k in range(size)])]
    all_to_all x1, starting transfers between devices: 11.9 us -> 10.7 us  [exchange(): return lax.all_to_all(pieces, axes, split_axis=0, concat_axis=0, tiled=True)]
  transfers between devices with their start and end apart: 9 -> 10, of which waited for: 7 -> 4; matrix products, arithmetic and copies ran while one was open for 2% -> 2% of each run, Pallas kernels for 0% -> 0%
where the time goes in v5:
time: 54.2 us; the launch traced here: 54 us
  starting transfers between devices  33.2 us (61%)
  waiting for transfers between devices  14.3 us (26%)
  matrix products  2.49 us (5%)
  other arithmetic  2.23 us (4%)
  local copies, waits for them, and re-layouts  1.51 us (3%)
    ppermute x9, starting transfers between devices, swap(): return lax.ppermute(values, axis, [(k, k ^ mask) for k in range(size)])  22.5 us
    all_to_all x1, starting transfers between devices, exchange(): return lax.all_to_all(pieces, axes, split_axis=0, concat_axis=0, tiled=True)  10.7 us
    all_to_all x1, waiting for transfers between devices, exchange(): return lax.all_to_all(pieces, axes, split_axis=0, concat_axis=0, tiled=True)  8.45 us
    ppermute x9, waiting for transfers between devices, swap(): return lax.ppermute(values, axis, [(k, k ^ mask) for k in range(size)])  5.9 us
    dot_general x4, matrix products, project_columns(): lax.dot_general(proj, acts[0], (((0,), (1,)), ((), ())), preferred_elemen...  1.9 us
    concatenate x1, other arithmetic, per_device(): wide_proj = jnp.concatenate([up_out_proj, down_in_proj], axis=1)  1.37 us
  transfers between devices with their start and end apart: 10, of which 4 were waited for; matrix products, arithmetic and copies ran while one was open for 2% of the time, Pallas kernels for 0%

profile of v5, /device:TPU:1, one launch (start us, length us, event | category | flops | bytes accessed | tf_op | source)
XLA Modules:
  0.0 54.0 jit_solution(10588565408736588102)
XLA Ops:
  0.0 1.4 %pad_maximum_fusion = bf16[3584,128]{0,1:T(8,128)(2,1)S(1)} fusion(bf16[3584,64]{0,1:T(8,128)(2,1)} %param.15, bf16[3584,64]{0,1:T(8,128)(2,1)} %param.14), kind=kLoop, calls=%fused_computation.6 | loop fusion | flops 1835008 | bytes 1835008 | tf_op jit(solution)/shard_map/concatenate | solution.py:56
  1.5 0.3 fusion.10
  1.8 0.3 fusion.8
  2.2 0.7 %fusion.2 = f32[64,256]{1,0:T(8,128)S(1)} fusion(bf16[1,256,3584]{2,1,0:T(8,128)(2,1)S(1)} %copy-done, bf16[3584,128]{0,1:T(8,128)(2,1)S(1)} %pad_maximum_fusion), kind=kOutput, calls=%fused_computation.2 | convolution fusion | flops 117440512 | bytes 2359296 | tf_op jit(solution)/shard_map/dot_general | solution.py:13
  2.9 0.5 copy-done.1
  3.4 0.7 %fusion = f32[64,256]{1,0:T(8,128)S(1)} fusion(bf16[1,256,3584]{2,1,0:T(8,128)(2,1)S(1)} %copy-done.1, bf16[3584,128]{0,1:T(8,128)(2,1)S(1)} %pad_maximum_fusion), kind=kOutput, calls=%fused_computation | convolution fusion | flops 117440512 | bytes 2359296 | tf_op jit(solution)/shard_map/dot_general | solution.py:13
  4.2 2.2 %collective-permute-start = (f32[96,256]{1,0:T(8,128)S(1)}, f32[96,256]{1,0:T(8,128)S(1)}, u32[]{:S(2)}, u32[]{:S(2)}) collective-permute-start(f32[96,256]{1,0:T(8,128)S(1)} %get-tuple-element.19), channel_id=1, source_target_pairs={{0,2},{2,0},{4,6},{6,4},{1,3},{3,1},{5,7},{7,5},{8,10},{10,8},{12,... | collective-permute-start | bytes 294920 | tf_op jit(solution)/shard_map/ppermute | solution.py:31
  6.4 1.9 %collective-permute-start.1 = (f32[96,256]{1,0:T(8,128)S(1)}, f32[96,256]{1,0:T(8,128)S(1)}, u32[]{:S(2)}, u32[]{:S(2)}) collective-permute-start(f32[96,256]{1,0:T(8,128)S(1)} %get-tuple-element.17), channel_id=1, source_target_pairs={{0,6},{2,4},{4,2},{6,0},{1,7},{3,5},{5,3},{7,1},{8,14},{10,12},{12... | collective-permute-start | bytes 294920 | tf_op jit(solution)/shard_map/ppermute | solution.py:31
  8.3 0.7 %collective-permute-start.2 = (f32[96,256]{1,0:T(8,128)S(1)}, f32[96,256]{1,0:T(8,128)S(1)}, u32[]{:S(2)}, u32[]{:S(2)}) collective-permute-start(f32[96,256]{1,0:T(8,128)S(1)} %get-tuple-element.18), channel_id=1, source_target_pairs={{0,4},{2,6},{4,0},{6,2},{1,5},{3,7},{5,1},{7,3},{8,12},{10,14},{12... | collective-permute-start | bytes 294920 | tf_op jit(solution)/shard_map/ppermute | solution.py:31
  9.1 7.0 %collective-permute-start.4 = (bf16[64,1024]{1,0:T(8,128)(2,1)S(1)}, bf16[64,1024]{1,0:T(8,128)(2,1)S(1)}, u32[]{:S(2)}, u32[]{:S(2)}) collective-permute-start(bf16[64,1024]{1,0:T(8,128)(2,1)S(1)} %get-tuple-element.21), channel_id=1, source_target_pairs={{0,1},{1,0},{2,3},{3,2},{4,5},{5,4},{6,7},{7,6},{8,9},{9,8},{10,11... | collective-permute-start | bytes 393224 | tf_op jit(solution)/shard_map/ppermute | solution.py:31
  16.1 4.3 %collective-permute-start.3 = (f32[96,256]{1,0:T(8,128)S(1)}, f32[96,256]{1,0:T(8,128)S(1)}, u32[]{:S(2)}, u32[]{:S(2)}) collective-permute-start(f32[96,256]{1,0:T(8,128)S(1)} %bitcast_add_fusion), channel_id=1, source_target_pairs={{0,1},{1,0},{2,3},{3,2},{4,5},{5,4},{6,7},{7,6},{8,9},{9,8},{10,11... | collective-permute-start | bytes 294920 | tf_op jit(solution)/shard_map/ppermute | solution.py:31
  20.4 1.1 %collective-permute-start.5 = (bf16[64,1024]{1,0:T(8,128)(2,1)S(1)}, bf16[64,1024]{1,0:T(8,128)(2,1)S(1)}, u32[]{:S(2)}, u32[]{:S(2)}) collective-permute-start(bf16[64,1024]{1,0:T(8,128)(2,1)S(1)} %get-tuple-element.20), channel_id=1, source_target_pairs={{0,1},{1,0},{2,3},{3,2},{4,5},{5,4},{6,7},{7,6},{8,9},{9,8},{10,11... | collective-permute-start | bytes 393224 | tf_op jit(solution)/shard_map/ppermute | solution.py:31
  21.6 2.9 %collective-permute-done.3 = f32[96,256]{1,0:T(8,128)S(1)} collective-permute-done((f32[96,256]{1,0:T(8,128)S(1)}, f32[96,256]{1,0:T(8,128)S(1)}, u32[]{:S(2)}, u32[]{:S(2)}) %collective-permute-start.3) | collective-permute-done | bytes 98336 | tf_op jit(solution)/shard_map/ppermute | solution.py:31
  24.5 0.1 convolution_convert_fusion.1
  24.7 0.2 convolution_convert_fusion
  25.0 0.7 %broadcast_in_dim.3 = bf16[32,16,128]{2,1,0:T(8,128)(2,1)} broadcast(bf16[16,128]{1,0:T(8,128)(2,1)S(1)} %pad_maximum_fusion.6), dimensions={1,2} | broadcast | bytes 135168 | tf_op jit(solution)/shard_map/broadcast_in_dim | solution.py:35
  25.6 10.7 %all-to-all-start = ((bf16[32,16,128]{2,1,0:T(8,128)(2,1)}), bf16[32,16,128]{2,1,0:T(8,128)(2,1)S(1)}, u32[]{:S(2)}, u32[]{:S(2)}) async-start(bf16[32,16,128]{2,1,0:T(8,128)(2,1)} %broadcast_in_dim.3), calls=%async_computation | async-start | bytes 262144 | tf_op jit(solution)/shard_map/all_to_all | solution.py:26
  36.5 8.4 %all-to-all-done = bf16[32,16,128]{2,1,0:T(8,128)(2,1)S(1)} async-done(((bf16[32,16,128]{2,1,0:T(8,128)(2,1)}), bf16[32,16,128]{2,1,0:T(8,128)(2,1)S(1)}, u32[]{:S(2)}, u32[]{:S(2)}) %all-to-all-start) | async-done | bytes 131104 | tf_op jit(solution)/shard_map/all_to_all | solution.py:26
  44.9 0.3 fusion.4
  45.2 4.4 %collective-permute-start.6 = (f32[32,128]{1,0:T(8,128)S(1)}, f32[32,128]{1,0:T(8,128)S(1)}, u32[]{:S(2)}, u32[]{:S(2)}) collective-permute-start(f32[32,128]{1,0:T(8,128)S(1)} %fusion.4), channel_id=1, source_target_pairs={{0,4},{2,6},{4,0},{6,2},{1,5},{3,7},{5,1},{7,3},{8,12},{10,14},{12... | collective-permute-start | bytes 49160 | tf_op jit(solution)/shard_map/ppermute | solution.py:31
  49.6 0.8 %collective-permute-start.7 = (f32[32,128]{1,0:T(8,128)S(1)}, f32[32,128]{1,0:T(8,128)S(1)}, u32[]{:S(2)}, u32[]{:S(2)}) collective-permute-start(f32[32,128]{1,0:T(8,128)S(1)} %fusion.4), channel_id=1, source_target_pairs={{0,6},{2,4},{4,2},{6,0},{1,7},{3,5},{5,3},{7,1},{8,14},{10,12},{12... | collective-permute-start | bytes 49160 | tf_op jit(solution)/shard_map/ppermute | solution.py:31
  50.4 0.3 collective-permute-done.6
  50.7 2.7 %collective-permute-done.7 = f32[32,128]{1,0:T(8,128)S(1)} collective-permute-done((f32[32,128]{1,0:T(8,128)S(1)}, f32[32,128]{1,0:T(8,128)S(1)}, u32[]{:S(2)}, u32[]{:S(2)}) %collective-permute-start.7) | collective-permute-done | bytes 16416 | tf_op jit(solution)/shard_map/ppermute | solution.py:31
  53.4 0.6 %add_add_fusion = f32[32,128]{1,0:T(8,128)} fusion(f32[32,128]{1,0:T(8,128)S(1)} %collective-permute-done.8, f32[32,128]{1,0:T(8,128)S(1)} %fusion.4, f32[32,128]{1,0:T(8,128)S(1)} %collective-permute-done.6, f32[32,128]{1,0:T(8,128)S(1)} %collective-permute-done.7), kind=kLoop, calls=%fused_computation.36 | loop fusion | flops 12288 | bytes 81920 | tf_op jit(solution)/shard_map/add | solution.py:82
  (35 shorter events, 0.6 us)
Async XLA Ops:
  0.0 2.2 %copy-start = (bf16[1,256,3584]{2,1,0:T(8,128)(2,1)S(1)}, bf16[1,256,3584]{2,1,0:T(8,128)(2,1)}, u32[]{:S(2)}) copy-start(bf16[1,256,3584]{2,1,0:T(8,128)(2,1)} %param.10) | copy-start | bytes 5505028
  0.0 1.4 %copy-start.5 = (bf16[1024,64]{0,1:T(8,128)(2,1)S(1)}, bf16[1024,64]{0,1:T(8,128)(2,1)}, u32[]{:S(2)}) copy-start(bf16[1024,64]{0,1:T(8,128)(2,1)} %param.13) | copy-start | bytes 393220
  0.0 1.5 %copy-start.3 = (bf16[1,256,1024]{2,1,0:T(8,128)(2,1)S(1)}, bf16[1,256,1024]{2,1,0:T(8,128)(2,1)}, u32[]{:S(2)}) copy-start(bf16[1,256,1024]{2,1,0:T(8,128)(2,1)} %param.9) | copy-start | bytes 1572868
  0.0 1.8 %copy-start.4 = (bf16[1,256,1024]{2,1,0:T(8,128)(2,1)S(1)}, bf16[1,256,1024]{2,1,0:T(8,128)(2,1)}, u32[]{:S(2)}) copy-start(bf16[1,256,1024]{2,1,0:T(8,128)(2,1)} %param.12) | copy-start | bytes 1572868
  0.0 1.8 %copy-start.6 = (bf16[1024,64]{0,1:T(8,128)(2,1)S(1)}, bf16[1024,64]{0,1:T(8,128)(2,1)}, u32[]{:S(2)}) copy-start(bf16[1024,64]{0,1:T(8,128)(2,1)} %param.16) | copy-start | bytes 393220
  1.8 1.6 %copy-start.1 = (bf16[1,256,3584]{2,1,0:T(8,128)(2,1)S(1)}, bf16[1,256,3584]{2,1,0:T(8,128)(2,1)}, u32[]{:S(2)}) copy-start(bf16[1,256,3584]{2,1,0:T(8,128)(2,1)} %param.11) | copy-start | bytes 5505028
  3.4 5.6 %copy-start.2 = (bf16[128,1024]{1,0:T(8,128)(2,1)S(1)}, bf16[128,1024]{1,0:T(8,128)(2,1)}, u32[]{:S(2)}) copy-start(bf16[128,1024]{1,0:T(8,128)(2,1)} %param.17) | copy-start | bytes 786436
  4.2 11.9 %collective-permute-start = (f32[96,256]{1,0:T(8,128)S(1)}, f32[96,256]{1,0:T(8,128)S(1)}, u32[]{:S(2)}, u32[]{:S(2)}) collective-permute-start(f32[96,256]{1,0:T(8,128)S(1)} %get-tuple-element.19), channel_id=1, source_target_pairs={{0,2},{2,0},{4,6},{6,4},{1,3},{3,1},{5,7},{7,5},{8,10},{10,8},{12,... | collective-permute-start | bytes 294920 | tf_op jit(solution)/shard_map/ppermute | solution.py:31
  6.4 9.7 %collective-permute-start.1 = (f32[96,256]{1,0:T(8,128)S(1)}, f32[96,256]{1,0:T(8,128)S(1)}, u32[]{:S(2)}, u32[]{:S(2)}) collective-permute-start(f32[96,256]{1,0:T(8,128)S(1)} %get-tuple-element.17), channel_id=1, source_target_pairs={{0,6},{2,4},{4,2},{6,0},{1,7},{3,5},{5,3},{7,1},{8,14},{10,12},{12... | collective-permute-start | bytes 294920 | tf_op jit(solution)/shard_map/ppermute | solution.py:31
  8.3 7.8 %collective-permute-start.2 = (f32[96,256]{1,0:T(8,128)S(1)}, f32[96,256]{1,0:T(8,128)S(1)}, u32[]{:S(2)}, u32[]{:S(2)}) collective-permute-start(f32[96,256]{1,0:T(8,128)S(1)} %get-tuple-element.18), channel_id=1, source_target_pairs={{0,4},{2,6},{4,0},{6,2},{1,5},{3,7},{5,1},{7,3},{8,12},{10,14},{12... | collective-permute-start | bytes 294920 | tf_op jit(solution)/shard_map/ppermute | solution.py:31
  9.1 15.4 %collective-permute-start.4 = (bf16[64,1024]{1,0:T(8,128)(2,1)S(1)}, bf16[64,1024]{1,0:T(8,128)(2,1)S(1)}, u32[]{:S(2)}, u32[]{:S(2)}) collective-permute-start(bf16[64,1024]{1,0:T(8,128)(2,1)S(1)} %get-tuple-element.21), channel_id=1, source_target_pairs={{0,1},{1,0},{2,3},{3,2},{4,5},{5,4},{6,7},{7,6},{8,9},{9,8},{10,11... | collective-permute-start | bytes 393224 | tf_op jit(solution)/shard_map/ppermute | solution.py:31
  16.1 8.3 %collective-permute-start.3 = (f32[96,256]{1,0:T(8,128)S(1)}, f32[96,256]{1,0:T(8,128)S(1)}, u32[]{:S(2)}, u32[]{:S(2)}) collective-permute-start(f32[96,256]{1,0:T(8,128)S(1)} %bitcast_add_fusion), channel_id=1, source_target_pairs={{0,1},{1,0},{2,3},{3,2},{4,5},{5,4},{6,7},{7,6},{8,9},{9,8},{10,11... | collective-permute-start | bytes 294920 | tf_op jit(solution)/shard_map/ppermute | solution.py:31
  20.4 16.0 %collective-permute-start.5 = (bf16[64,1024]{1,0:T(8,128)(2,1)S(1)}, bf16[64,1024]{1,0:T(8,128)(2,1)S(1)}, u32[]{:S(2)}, u32[]{:S(2)}) collective-permute-start(bf16[64,1024]{1,0:T(8,128)(2,1)S(1)} %get-tuple-element.20), channel_id=1, source_target_pairs={{0,1},{1,0},{2,3},{3,2},{4,5},{5,4},{6,7},{7,6},{8,9},{9,8},{10,11... | collective-permute-start | bytes 393224 | tf_op jit(solution)/shard_map/ppermute | solution.py:31
  25.6 19.3 %all-to-all-start = ((bf16[32,16,128]{2,1,0:T(8,128)(2,1)}), bf16[32,16,128]{2,1,0:T(8,128)(2,1)S(1)}, u32[]{:S(2)}, u32[]{:S(2)}) async-start(bf16[32,16,128]{2,1,0:T(8,128)(2,1)} %broadcast_in_dim.3), calls=%async_computation | async-start | bytes 262144 | tf_op jit(solution)/shard_map/all_to_all | solution.py:26
  45.2 5.5 %collective-permute-start.6 = (f32[32,128]{1,0:T(8,128)S(1)}, f32[32,128]{1,0:T(8,128)S(1)}, u32[]{:S(2)}, u32[]{:S(2)}) collective-permute-start(f32[32,128]{1,0:T(8,128)S(1)} %fusion.4), channel_id=1, source_target_pairs={{0,4},{2,6},{4,0},{6,2},{1,5},{3,7},{5,1},{7,3},{8,12},{10,14},{12... | collective-permute-start | bytes 49160 | tf_op jit(solution)/shard_map/ppermute | solution.py:31
  49.6 3.8 %collective-permute-start.7 = (f32[32,128]{1,0:T(8,128)S(1)}, f32[32,128]{1,0:T(8,128)S(1)}, u32[]{:S(2)}, u32[]{:S(2)}) collective-permute-start(f32[32,128]{1,0:T(8,128)S(1)} %fusion.4), channel_id=1, source_target_pairs={{0,6},{2,4},{4,2},{6,0},{1,7},{3,5},{5,3},{7,1},{8,14},{10,12},{12... | collective-permute-start | bytes 49160 | tf_op jit(solution)/shard_map/ppermute | solution.py:31
  50.4 3.0 %collective-permute-start.8 = (f32[32,128]{1,0:T(8,128)S(1)}, f32[32,128]{1,0:T(8,128)S(1)}, u32[]{:S(2)}, u32[]{:S(2)}) collective-permute-start(f32[32,128]{1,0:T(8,128)S(1)} %fusion.4), channel_id=1, source_target_pairs={{0,2},{2,0},{4,6},{6,4},{1,3},{3,1},{5,7},{7,5},{8,10},{10,8},{12,... | collective-permute-start | bytes 49160 | tf_op jit(solution)/shard_map/ppermute | solution.py:31

commit v6 on v1

--- a/solution.py
+++ b/solution.py
@@ -13,6 +13,16 @@
     return lax.dot_general(
         proj, acts[0], (((0,), (1,)), ((), ())), preferred_element_type=jnp.float32
     )
+
+
+def to_send(sums, outer):
+    high = lax.reduce_precision(sums[:outer], 8, 7)
+    return jnp.concatenate([high, sums[:outer] - high, sums[outer:]], axis=0).astype(jnp.bfloat16)
+
+
+def from_sent(sent, outer):
+    sums = sent.astype(jnp.float32)
+    return jnp.concatenate([sums[:outer] + sums[outer : 2 * outer], sums[2 * outer :]], axis=0)
 
 
 def outer_rows(outs, ins):
@@ -50,12 +60,11 @@
     rank = up_in_proj.shape[1]
     rows = 2 * rank // ys // zhs
     other = swap(queries, "zh", 1)
+    wide_proj = lax.optimization_barrier(jnp.concatenate([up_out_proj, down_in_proj], axis=1))
     up_in = project_columns(up_inputs, up_in_proj)
-    down_out = project_columns(down_grads, down_out_proj)
-    wide_proj = jnp.concatenate([up_out_proj, down_in_proj], axis=1)
-    wide_proj, up_in, down_out = lax.optimization_barrier((wide_proj, up_in, down_out))
     up_out = project_columns(up_grads, wide_proj[:, :rank])
     down_in = project_columns(down_inputs, wide_proj[:, rank:])
+    down_out = project_columns(down_grads, down_out_proj)
     pieces = []
     for outs, ins in ((up_out, up_in), (down_out, down_in)):
         for k in range(rank // (zhs * rows)):
@@ -63,9 +72,11 @@
     pieces = jnp.stack(pieces)
     y = lax.axis_index("y")
     piece = lambda k: lax.dynamic_index_in_dim(pieces, k, 0, keepdims=False)
-    half = piece(y) + sum(swap(piece(y ^ mask), "y", mask) for mask in (1, 3, 2))
+    outer = zhs * rows
+    half = piece(y) + sum(
+        from_sent(swap(to_send(piece(y ^ mask), outer), "y", mask), outer) for mask in (1, 3, 2)
+    )
     sums = half + swap(half, "zh", 1)
-    outer = zhs * rows
     outs, ins = sums[:outer], sums[outer:]
     own = jnp.concatenate([outer_rows(outs[0::2], ins), outer_rows(outs[1::2], ins)], axis=1)
     every = to_all(own.astype(jnp.bfloat16), DP, zls * xs * cores)

time: 50.8 us -> 49.2 us (0.969)
  starting transfers between devices: 26.8 us -> 25.3 us
    ppermute x8, starting transfers between devices: 14.9 us -> 13.7 us  [swap(): return lax.ppermute(values, axis, [(k, k ^ mask) for k in range(size)])]
    concatenate x1 -> x4, other arithmetic: 1.37 us -> 1.38 us  [the longest x1 1.37 us: per_device(): jnp.concatenate([up_out_proj, down_in_proj], axis=1)]
  transfers between devices with their start and end apart: 9 -> 9, of which waited for: 7 -> 6; matrix products, arithmetic and copies ran while one was open for 2% -> 3% of each run, Pallas kernels for 0% -> 0%
where the time goes in v6:
time: 49.2 us; the launch traced here: 48.9 us
  starting transfers between devices  25.3 us (51%)
  waiting for transfers between devices  17.3 us (35%)
  matrix products  2.49 us (5%)
  other arithmetic  2.32 us (5%)
  local copies, waits for them, and re-layouts  1.28 us (3%)
    ppermute x8, starting transfers between devices, swap(): return lax.ppermute(values, axis, [(k, k ^ mask) for k in range(size)])  13.7 us
    all_to_all x1, starting transfers between devices, exchange(): return lax.all_to_all(pieces, axes, split_axis=0, concat_axis=0, tiled=True)  11.6 us
    ppermute x8, waiting for transfers between devices, swap(): return lax.ppermute(values, axis, [(k, k ^ mask) for k in range(size)])  8.69 us
    all_to_all x1, waiting for transfers between devices, exchange(): return lax.all_to_all(pieces, axes, split_axis=0, concat_axis=0, tiled=True)  8.59 us
    dot_general x4, matrix products, project_columns(): lax.dot_general(proj, acts[0], (((0,), (1,)), ((), ())), preferred_elemen...  1.9 us
    concatenate x1, other arithmetic, per_device(): jnp.concatenate([up_out_proj, down_in_proj], axis=1)  1.37 us
  transfers between devices with their start and end apart: 9, of which 6 were waited for; matrix products, arithmetic and copies ran while one was open for 3% of the time, Pallas kernels for 0%

profile of v6, /device:TPU:1, one launch (start us, length us, event | category | flops | bytes accessed | tf_op | source)
XLA Modules:
  0.0 48.9 jit_solution(1553045049418971928)
XLA Ops:
  0.0 1.4 %pad_maximum_fusion = bf16[3584,128]{0,1:T(8,128)(2,1)S(1)} fusion(bf16[3584,64]{0,1:T(8,128)(2,1)} %param.15, bf16[3584,64]{0,1:T(8,128)(2,1)} %param.14), kind=kLoop, calls=%fused_computation.6 | loop fusion | flops 1835008 | bytes 1835008 | tf_op jit(solution)/shard_map/concatenate | solution.py:63
  1.4 0.4 copy-done
  1.8 0.7 %fusion.2 = f32[64,256]{1,0:T(8,128)S(1)} fusion(bf16[1,256,3584]{2,1,0:T(8,128)(2,1)S(1)} %copy-done, bf16[3584,128]{0,1:T(8,128)(2,1)S(1)} %pad_maximum_fusion), kind=kOutput, calls=%fused_computation.2 | convolution fusion | flops 117440512 | bytes 2359296 | tf_op jit(solution)/shard_map/dot_general | solution.py:13
  2.5 0.7 %fusion = f32[64,256]{1,0:T(8,128)S(1)} fusion(bf16[1,256,3584]{2,1,0:T(8,128)(2,1)S(1)} %copy-done.1, bf16[3584,128]{0,1:T(8,128)(2,1)S(1)} %pad_maximum_fusion), kind=kOutput, calls=%fused_computation | convolution fusion | flops 117440512 | bytes 2359296 | tf_op jit(solution)/shard_map/dot_general | solution.py:13
  3.2 0.3 fusion.8
  3.6 0.3 fusion.10
  4.0 3.8 %collective-permute-start.2 = (bf16[128,256]{1,0:T(8,128)(2,1)S(1)}, bf16[128,256]{1,0:T(8,128)(2,1)S(1)}, u32[]{:S(2)}, u32[]{:S(2)}) collective-permute-start(bf16[128,256]{1,0:T(8,128)(2,1)S(1)} %pad_maximum_fusion.8), channel_id=1, source_target_pairs={{0,4},{2,6},{4,0},{6,2},{1,5},{3,7},{5,1},{7,3},{8,12},{10,14},{12... | collective-permute-start | bytes 196616 | tf_op jit(solution)/shard_map/ppermute | solution.py:41
  7.9 0.8 %collective-permute-start.1 = (bf16[128,256]{1,0:T(8,128)(2,1)S(1)}, bf16[128,256]{1,0:T(8,128)(2,1)S(1)}, u32[]{:S(2)}, u32[]{:S(2)}) collective-permute-start(bf16[128,256]{1,0:T(8,128)(2,1)S(1)} %pad_maximum_fusion.7), channel_id=1, source_target_pairs={{0,6},{2,4},{4,2},{6,0},{1,7},{3,5},{5,3},{7,1},{8,14},{10,12},{12... | collective-permute-start | bytes 196616 | tf_op jit(solution)/shard_map/ppermute | solution.py:41
  8.7 0.9 %collective-permute-done.2 = bf16[128,256]{1,0:T(8,128)(2,1)S(1)} collective-permute-done((bf16[128,256]{1,0:T(8,128)(2,1)S(1)}, bf16[128,256]{1,0:T(8,128)(2,1)S(1)}, u32[]{:S(2)}, u32[]{:S(2)}) %collective-permute-start.2) | collective-permute-done | bytes 65568 | tf_op jit(solution)/shard_map/ppermute | solution.py:41
  9.5 3.4 %collective-permute-done.1 = bf16[128,256]{1,0:T(8,128)(2,1)S(1)} collective-permute-done((bf16[128,256]{1,0:T(8,128)(2,1)S(1)}, bf16[128,256]{1,0:T(8,128)(2,1)S(1)}, u32[]{:S(2)}, u32[]{:S(2)}) %collective-permute-start.1) | collective-permute-done | bytes 65568 | tf_op jit(solution)/shard_map/ppermute | solution.py:41
  13.1 6.3 %collective-permute-start.3 = (f32[96,256]{1,0:T(8,128)S(1)}, f32[96,256]{1,0:T(8,128)S(1)}, u32[]{:S(2)}, u32[]{:S(2)}) collective-permute-start(f32[96,256]{1,0:T(8,128)S(1)} %fusion.21), channel_id=1, source_target_pairs={{0,1},{1,0},{2,3},{3,2},{4,5},{5,4},{6,7},{7,6},{8,9},{9,8},{10,11... | collective-permute-start | bytes 294920 | tf_op jit(solution)/shard_map/ppermute | solution.py:41
  19.5 2.0 %collective-permute-done.3 = f32[96,256]{1,0:T(8,128)S(1)} collective-permute-done((f32[96,256]{1,0:T(8,128)S(1)}, f32[96,256]{1,0:T(8,128)S(1)}, u32[]{:S(2)}, u32[]{:S(2)}) %collective-permute-start.3) | collective-permute-done | bytes 98336 | tf_op jit(solution)/shard_map/ppermute | solution.py:41
  21.5 0.1 convolution_convert_fusion.1
  21.7 0.2 convolution_convert_fusion
  21.9 0.7 %broadcast_in_dim.3 = bf16[32,16,128]{2,1,0:T(8,128)(2,1)} broadcast(bf16[16,128]{1,0:T(8,128)(2,1)S(1)} %pad_maximum_fusion.9), dimensions={1,2} | broadcast | bytes 135168 | tf_op jit(solution)/shard_map/broadcast_in_dim | solution.py:45
  22.6 11.6 %all-to-all-start = ((bf16[32,16,128]{2,1,0:T(8,128)(2,1)}), bf16[32,16,128]{2,1,0:T(8,128)(2,1)S(1)}, u32[]{:S(2)}, u32[]{:S(2)}) async-start(bf16[32,16,128]{2,1,0:T(8,128)(2,1)} %broadcast_in_dim.3), calls=%async_computation | async-start | bytes 262144 | tf_op jit(solution)/shard_map/all_to_all | solution.py:36
  34.3 8.6 %all-to-all-done = bf16[32,16,128]{2,1,0:T(8,128)(2,1)S(1)} async-done(((bf16[32,16,128]{2,1,0:T(8,128)(2,1)}), bf16[32,16,128]{2,1,0:T(8,128)(2,1)S(1)}, u32[]{:S(2)}, u32[]{:S(2)}) %all-to-all-start) | async-done | bytes 131104 | tf_op jit(solution)/shard_map/all_to_all | solution.py:36
  42.9 0.3 fusion.4
  43.2 1.3 %collective-permute-start.5 = (f32[32,128]{1,0:T(8,128)S(1)}, f32[32,128]{1,0:T(8,128)S(1)}, u32[]{:S(2)}, u32[]{:S(2)}) collective-permute-start(f32[32,128]{1,0:T(8,128)S(1)} %fusion.4), channel_id=1, source_target_pairs={{0,4},{2,6},{4,0},{6,2},{1,5},{3,7},{5,1},{7,3},{8,12},{10,14},{12... | collective-permute-start | bytes 49160 | tf_op jit(solution)/shard_map/ppermute | solution.py:41
  44.4 1.2 %collective-permute-start.6 = (f32[32,128]{1,0:T(8,128)S(1)}, f32[32,128]{1,0:T(8,128)S(1)}, u32[]{:S(2)}, u32[]{:S(2)}) collective-permute-start(f32[32,128]{1,0:T(8,128)S(1)} %fusion.4), channel_id=1, source_target_pairs={{0,6},{2,4},{4,2},{6,0},{1,7},{3,5},{5,3},{7,1},{8,14},{10,12},{12... | collective-permute-start | bytes 49160 | tf_op jit(solution)/shard_map/ppermute | solution.py:41
  45.6 0.2 collective-permute-start.7
  45.8 1.4 %collective-permute-done.5 = f32[32,128]{1,0:T(8,128)S(1)} collective-permute-done((f32[32,128]{1,0:T(8,128)S(1)}, f32[32,128]{1,0:T(8,128)S(1)}, u32[]{:S(2)}, u32[]{:S(2)}) %collective-permute-start.5) | collective-permute-done | bytes 16416 | tf_op jit(solution)/shard_map/ppermute | solution.py:41
  47.3 1.0 %collective-permute-done.6 = f32[32,128]{1,0:T(8,128)S(1)} collective-permute-done((f32[32,128]{1,0:T(8,128)S(1)}, f32[32,128]{1,0:T(8,128)S(1)}, u32[]{:S(2)}, u32[]{:S(2)}) %collective-permute-start.6) | collective-permute-done | bytes 16416 | tf_op jit(solution)/shard_map/ppermute | solution.py:41
  48.3 0.6 %add_add_fusion = f32[32,128]{1,0:T(8,128)} fusion(f32[32,128]{1,0:T(8,128)S(1)} %collective-permute-done.7, f32[32,128]{1,0:T(8,128)S(1)} %fusion.4, f32[32,128]{1,0:T(8,128)S(1)} %collective-permute-done.5, f32[32,128]{1,0:T(8,128)S(1)} %collective-permute-done.6), kind=kLoop, calls=%fused_computation.59 | loop fusion | flops 12288 | bytes 81920 | tf_op jit(solution)/shard_map/add | solution.py:90
  (43 shorter events, 0.7 us)
Async XLA Ops:
  0.0 1.8 %copy-start = (bf16[1,256,3584]{2,1,0:T(8,128)(2,1)S(1)}, bf16[1,256,3584]{2,1,0:T(8,128)(2,1)}, u32[]{:S(2)}) copy-start(bf16[1,256,3584]{2,1,0:T(8,128)(2,1)} %param.10) | copy-start | bytes 5505028
  0.0 2.5 %copy-start.1 = (bf16[1,256,3584]{2,1,0:T(8,128)(2,1)S(1)}, bf16[1,256,3584]{2,1,0:T(8,128)(2,1)}, u32[]{:S(2)}) copy-start(bf16[1,256,3584]{2,1,0:T(8,128)(2,1)} %param.11) | copy-start | bytes 5505028
  1.8 1.4 %copy-start.2 = (bf16[1,256,1024]{2,1,0:T(8,128)(2,1)S(1)}, bf16[1,256,1024]{2,1,0:T(8,128)(2,1)}, u32[]{:S(2)}) copy-start(bf16[1,256,1024]{2,1,0:T(8,128)(2,1)} %param.12) | copy-start | bytes 1572868
  1.8 1.4 %copy-start.5 = (bf16[1024,64]{0,1:T(8,128)(2,1)S(1)}, bf16[1024,64]{0,1:T(8,128)(2,1)}, u32[]{:S(2)}) copy-start(bf16[1024,64]{0,1:T(8,128)(2,1)} %param.16) | copy-start | bytes 393220
  2.5 1.1 %copy-start.3 = (bf16[1,256,1024]{2,1,0:T(8,128)(2,1)S(1)}, bf16[1,256,1024]{2,1,0:T(8,128)(2,1)}, u32[]{:S(2)}) copy-start(bf16[1,256,1024]{2,1,0:T(8,128)(2,1)} %param.9) | copy-start | bytes 1572868
  2.5 1.1 %copy-start.6 = (bf16[1024,64]{0,1:T(8,128)(2,1)S(1)}, bf16[1024,64]{0,1:T(8,128)(2,1)}, u32[]{:S(2)}) copy-start(bf16[1024,64]{0,1:T(8,128)(2,1)} %param.13) | copy-start | bytes 393220
  3.9 15.4 %copy-start.4 = (bf16[128,1024]{1,0:T(8,128)(2,1)S(1)}, bf16[128,1024]{1,0:T(8,128)(2,1)}, u32[]{:S(2)}) copy-start(bf16[128,1024]{1,0:T(8,128)(2,1)} %param.17) | copy-start | bytes 786436
  4.0 5.5 %collective-permute-start.2 = (bf16[128,256]{1,0:T(8,128)(2,1)S(1)}, bf16[128,256]{1,0:T(8,128)(2,1)S(1)}, u32[]{:S(2)}, u32[]{:S(2)}) collective-permute-start(bf16[128,256]{1,0:T(8,128)(2,1)S(1)} %pad_maximum_fusion.8), channel_id=1, source_target_pairs={{0,4},{2,6},{4,0},{6,2},{1,5},{3,7},{5,1},{7,3},{8,12},{10,14},{12... | collective-permute-start | bytes 196616 | tf_op jit(solution)/shard_map/ppermute | solution.py:41
  7.9 5.0 %collective-permute-start.1 = (bf16[128,256]{1,0:T(8,128)(2,1)S(1)}, bf16[128,256]{1,0:T(8,128)(2,1)S(1)}, u32[]{:S(2)}, u32[]{:S(2)}) collective-permute-start(bf16[128,256]{1,0:T(8,128)(2,1)S(1)} %pad_maximum_fusion.7), channel_id=1, source_target_pairs={{0,6},{2,4},{4,2},{6,0},{1,7},{3,5},{5,3},{7,1},{8,14},{10,12},{12... | collective-permute-start | bytes 196616 | tf_op jit(solution)/shard_map/ppermute | solution.py:41
  8.6 4.3 %collective-permute-start = (bf16[128,256]{1,0:T(8,128)(2,1)S(1)}, bf16[128,256]{1,0:T(8,128)(2,1)S(1)}, u32[]{:S(2)}, u32[]{:S(2)}) collective-permute-start(bf16[128,256]{1,0:T(8,128)(2,1)S(1)} %pad_maximum_fusion.6), channel_id=1, source_target_pairs={{0,2},{2,0},{4,6},{6,4},{1,3},{3,1},{5,7},{7,5},{8,10},{10,8},{12,... | collective-permute-start | bytes 196616 | tf_op jit(solution)/shard_map/ppermute | solution.py:41
  13.1 8.4 %collective-permute-start.3 = (f32[96,256]{1,0:T(8,128)S(1)}, f32[96,256]{1,0:T(8,128)S(1)}, u32[]{:S(2)}, u32[]{:S(2)}) collective-permute-start(f32[96,256]{1,0:T(8,128)S(1)} %fusion.21), channel_id=1, source_target_pairs={{0,1},{1,0},{2,3},{3,2},{4,5},{5,4},{6,7},{7,6},{8,9},{9,8},{10,11... | collective-permute-start | bytes 294920 | tf_op jit(solution)/shard_map/ppermute | solution.py:41
  19.4 14.9 %collective-permute-start.4 = (bf16[128,1024]{1,0:T(8,128)(2,1)S(1)}, bf16[128,1024]{1,0:T(8,128)(2,1)S(1)}, u32[]{:S(2)}, u32[]{:S(2)}) collective-permute-start(bf16[128,1024]{1,0:T(8,128)(2,1)S(1)} %copy-done.4), channel_id=1, source_target_pairs={{0,1},{1,0},{2,3},{3,2},{4,5},{5,4},{6,7},{7,6},{8,9},{9,8},{10,11... | collective-permute-start | bytes 786440 | tf_op jit(solution)/shard_map/ppermute | solution.py:41
  22.6 20.3 %all-to-all-start = ((bf16[32,16,128]{2,1,0:T(8,128)(2,1)}), bf16[32,16,128]{2,1,0:T(8,128)(2,1)S(1)}, u32[]{:S(2)}, u32[]{:S(2)}) async-start(bf16[32,16,128]{2,1,0:T(8,128)(2,1)} %broadcast_in_dim.3), calls=%async_computation | async-start | bytes 262144 | tf_op jit(solution)/shard_map/all_to_all | solution.py:36
  43.2 4.1 %collective-permute-start.5 = (f32[32,128]{1,0:T(8,128)S(1)}, f32[32,128]{1,0:T(8,128)S(1)}, u32[]{:S(2)}, u32[]{:S(2)}) collective-permute-start(f32[32,128]{1,0:T(8,128)S(1)} %fusion.4), channel_id=1, source_target_pairs={{0,4},{2,6},{4,0},{6,2},{1,5},{3,7},{5,1},{7,3},{8,12},{10,14},{12... | collective-permute-start | bytes 49160 | tf_op jit(solution)/shard_map/ppermute | solution.py:41
  44.4 3.9 %collective-permute-start.6 = (f32[32,128]{1,0:T(8,128)S(1)}, f32[32,128]{1,0:T(8,128)S(1)}, u32[]{:S(2)}, u32[]{:S(2)}) collective-permute-start(f32[32,128]{1,0:T(8,128)S(1)} %fusion.4), channel_id=1, source_target_pairs={{0,6},{2,4},{4,2},{6,0},{1,7},{3,5},{5,3},{7,1},{8,14},{10,12},{12... | collective-permute-start | bytes 49160 | tf_op jit(solution)/shard_map/ppermute | solution.py:41
  45.6 2.7 %collective-permute-start.7 = (f32[32,128]{1,0:T(8,128)S(1)}, f32[32,128]{1,0:T(8,128)S(1)}, u32[]{:S(2)}, u32[]{:S(2)}) collective-permute-start(f32[32,128]{1,0:T(8,128)S(1)} %fusion.4), channel_id=1, source_target_pairs={{0,2},{2,0},{4,6},{6,4},{1,3},{3,1},{5,7},{7,5},{8,10},{10,8},{12,... | collective-permute-start | bytes 49160 | tf_op jit(solution)/shard_map/ppermute | solution.py:41

commit v7 on v6

--- a/solution.py
+++ b/solution.py
@@ -60,8 +60,9 @@
     rank = up_in_proj.shape[1]
     rows = 2 * rank // ys // zhs
     other = swap(queries, "zh", 1)
-    wide_proj = lax.optimization_barrier(jnp.concatenate([up_out_proj, down_in_proj], axis=1))
     up_in = project_columns(up_inputs, up_in_proj)
+    wide_proj = jnp.concatenate([up_out_proj, down_in_proj], axis=1)
+    wide_proj, up_in = lax.optimization_barrier((wide_proj, up_in))
     up_out = project_columns(up_grads, wide_proj[:, :rank])
     down_in = project_columns(down_inputs, wide_proj[:, rank:])
     down_out = project_columns(down_grads, down_out_proj)

time: 49.2 us -> 49.5 us (level)
  no operation moved by 1% of the time
where the time goes in v7:
time: 49.5 us; the launch traced here: 49.2 us
  starting transfers between devices  25.3 us (51%)
  waiting for transfers between devices  17.3 us (35%)
  matrix products  2.48 us (5%)
  other arithmetic  2.32 us (5%)
  local copies, waits for them, and re-layouts  1.57 us (3%)
    ppermute x8, starting transfers between devices, swap(): return lax.ppermute(values, axis, [(k, k ^ mask) for k in range(size)])  13.7 us
    all_to_all x1, starting transfers between devices, exchange(): return lax.all_to_all(pieces, axes, split_axis=0, concat_axis=0, tiled=True)  11.6 us
    ppermute x8, waiting for transfers between devices, swap(): return lax.ppermute(values, axis, [(k, k ^ mask) for k in range(size)])  8.68 us
    all_to_all x1, waiting for transfers between devices, exchange(): return lax.all_to_all(pieces, axes, split_axis=0, concat_axis=0, tiled=True)  8.61 us
    dot_general x4, matrix products, project_columns(): lax.dot_general(proj, acts[0], (((0,), (1,)), ((), ())), preferred_elemen...  1.89 us
    concatenate x1, other arithmetic, per_device(): wide_proj = jnp.concatenate([up_out_proj, down_in_proj], axis=1)  1.37 us
  transfers between devices with their start and end apart: 9, of which 6 were waited for; matrix products, arithmetic and copies ran while one was open for 3% of the time, Pallas kernels for 0%

profile of v7, /device:TPU:1, one launch (start us, length us, event | category | flops | bytes accessed | tf_op | source)
XLA Modules:
  0.0 49.2 jit_solution(687921662298555927)
XLA Ops:
  0.0 1.4 %pad_maximum_fusion = bf16[3584,128]{0,1:T(8,128)(2,1)S(1)} fusion(bf16[3584,64]{0,1:T(8,128)(2,1)} %param.15, bf16[3584,64]{0,1:T(8,128)(2,1)} %param.14), kind=kLoop, calls=%fused_computation.6 | loop fusion | flops 1835008 | bytes 1835008 | tf_op jit(solution)/shard_map/concatenate | solution.py:64
  1.5 0.3 fusion.10
  1.8 0.2 copy-done
  2.0 0.7 %fusion.2 = f32[64,256]{1,0:T(8,128)S(1)} fusion(bf16[1,256,3584]{2,1,0:T(8,128)(2,1)S(1)} %copy-done, bf16[3584,128]{0,1:T(8,128)(2,1)S(1)} %pad_maximum_fusion), kind=kOutput, calls=%fused_computation.2 | convolution fusion | flops 117440512 | bytes 2359296 | tf_op jit(solution)/shard_map/dot_general | solution.py:13
  2.7 0.4 copy-done.1
  3.1 0.7 %fusion = f32[64,256]{1,0:T(8,128)S(1)} fusion(bf16[1,256,3584]{2,1,0:T(8,128)(2,1)S(1)} %copy-done.1, bf16[3584,128]{0,1:T(8,128)(2,1)S(1)} %pad_maximum_fusion), kind=kOutput, calls=%fused_computation | convolution fusion | flops 117440512 | bytes 2359296 | tf_op jit(solution)/shard_map/dot_general | solution.py:13
  3.8 0.3 fusion.8
  4.3 3.8 %collective-permute-start.2 = (bf16[128,256]{1,0:T(8,128)(2,1)S(1)}, bf16[128,256]{1,0:T(8,128)(2,1)S(1)}, u32[]{:S(2)}, u32[]{:S(2)}) collective-permute-start(bf16[128,256]{1,0:T(8,128)(2,1)S(1)} %pad_maximum_fusion.8), channel_id=1, source_target_pairs={{0,4},{2,6},{4,0},{6,2},{1,5},{3,7},{5,1},{7,3},{8,12},{10,14},{12... | collective-permute-start | bytes 196616 | tf_op jit(solution)/shard_map/ppermute | solution.py:41
  8.2 0.8 %collective-permute-start.1 = (bf16[128,256]{1,0:T(8,128)(2,1)S(1)}, bf16[128,256]{1,0:T(8,128)(2,1)S(1)}, u32[]{:S(2)}, u32[]{:S(2)}) collective-permute-start(bf16[128,256]{1,0:T(8,128)(2,1)S(1)} %pad_maximum_fusion.7), channel_id=1, source_target_pairs={{0,6},{2,4},{4,2},{6,0},{1,7},{3,5},{5,3},{7,1},{8,14},{10,12},{12... | collective-permute-start | bytes 196616 | tf_op jit(solution)/shard_map/ppermute | solution.py:41
  9.0 0.9 %collective-permute-done.2 = bf16[128,256]{1,0:T(8,128)(2,1)S(1)} collective-permute-done((bf16[128,256]{1,0:T(8,128)(2,1)S(1)}, bf16[128,256]{1,0:T(8,128)(2,1)S(1)}, u32[]{:S(2)}, u32[]{:S(2)}) %collective-permute-start.2) | collective-permute-done | bytes 65568 | tf_op jit(solution)/shard_map/ppermute | solution.py:41
  9.8 3.4 %collective-permute-done.1 = bf16[128,256]{1,0:T(8,128)(2,1)S(1)} collective-permute-done((bf16[128,256]{1,0:T(8,128)(2,1)S(1)}, bf16[128,256]{1,0:T(8,128)(2,1)S(1)}, u32[]{:S(2)}, u32[]{:S(2)}) %collective-permute-start.1) | collective-permute-done | bytes 65568 | tf_op jit(solution)/shard_map/ppermute | solution.py:41
  13.3 6.3 %collective-permute-start.3 = (f32[96,256]{1,0:T(8,128)S(1)}, f32[96,256]{1,0:T(8,128)S(1)}, u32[]{:S(2)}, u32[]{:S(2)}) collective-permute-start(f32[96,256]{1,0:T(8,128)S(1)} %fusion.21), channel_id=1, source_target_pairs={{0,1},{1,0},{2,3},{3,2},{4,5},{5,4},{6,7},{7,6},{8,9},{9,8},{10,11... | collective-permute-start | bytes 294920 | tf_op jit(solution)/shard_map/ppermute | solution.py:41
  19.8 2.0 %collective-permute-done.3 = f32[96,256]{1,0:T(8,128)S(1)} collective-permute-done((f32[96,256]{1,0:T(8,128)S(1)}, f32[96,256]{1,0:T(8,128)S(1)}, u32[]{:S(2)}, u32[]{:S(2)}) %collective-permute-start.3) | collective-permute-done | bytes 98336 | tf_op jit(solution)/shard_map/ppermute | solution.py:41
  22.0 0.2 convolution_convert_fusion
  22.2 0.7 %broadcast_in_dim.3 = bf16[32,16,128]{2,1,0:T(8,128)(2,1)} broadcast(bf16[16,128]{1,0:T(8,128)(2,1)S(1)} %pad_maximum_fusion.9), dimensions={1,2} | broadcast | bytes 135168 | tf_op jit(solution)/shard_map/broadcast_in_dim | solution.py:45
  22.9 11.6 %all-to-all-start = ((bf16[32,16,128]{2,1,0:T(8,128)(2,1)}), bf16[32,16,128]{2,1,0:T(8,128)(2,1)S(1)}, u32[]{:S(2)}, u32[]{:S(2)}) async-start(bf16[32,16,128]{2,1,0:T(8,128)(2,1)} %broadcast_in_dim.3), calls=%async_computation | async-start | bytes 262144 | tf_op jit(solution)/shard_map/all_to_all | solution.py:36
  34.6 8.6 %all-to-all-done = bf16[32,16,128]{2,1,0:T(8,128)(2,1)S(1)} async-done(((bf16[32,16,128]{2,1,0:T(8,128)(2,1)}), bf16[32,16,128]{2,1,0:T(8,128)(2,1)S(1)}, u32[]{:S(2)}, u32[]{:S(2)}) %all-to-all-start) | async-done | bytes 131104 | tf_op jit(solution)/shard_map/all_to_all | solution.py:36
  43.2 0.3 fusion.4
  43.4 1.3 %collective-permute-start.5 = (f32[32,128]{1,0:T(8,128)S(1)}, f32[32,128]{1,0:T(8,128)S(1)}, u32[]{:S(2)}, u32[]{:S(2)}) collective-permute-start(f32[32,128]{1,0:T(8,128)S(1)} %fusion.4), channel_id=1, source_target_pairs={{0,4},{2,6},{4,0},{6,2},{1,5},{3,7},{5,1},{7,3},{8,12},{10,14},{12... | collective-permute-start | bytes 49160 | tf_op jit(solution)/shard_map/ppermute | solution.py:41
  44.7 1.2 %collective-permute-start.6 = (f32[32,128]{1,0:T(8,128)S(1)}, f32[32,128]{1,0:T(8,128)S(1)}, u32[]{:S(2)}, u32[]{:S(2)}) collective-permute-start(f32[32,128]{1,0:T(8,128)S(1)} %fusion.4), channel_id=1, source_target_pairs={{0,6},{2,4},{4,2},{6,0},{1,7},{3,5},{5,3},{7,1},{8,14},{10,12},{12... | collective-permute-start | bytes 49160 | tf_op jit(solution)/shard_map/ppermute | solution.py:41
  45.9 0.2 collective-permute-start.7
  46.1 1.4 %collective-permute-done.5 = f32[32,128]{1,0:T(8,128)S(1)} collective-permute-done((f32[32,128]{1,0:T(8,128)S(1)}, f32[32,128]{1,0:T(8,128)S(1)}, u32[]{:S(2)}, u32[]{:S(2)}) %collective-permute-start.5) | collective-permute-done | bytes 16416 | tf_op jit(solution)/shard_map/ppermute | solution.py:41
  47.6 1.0 %collective-permute-done.6 = f32[32,128]{1,0:T(8,128)S(1)} collective-permute-done((f32[32,128]{1,0:T(8,128)S(1)}, f32[32,128]{1,0:T(8,128)S(1)}, u32[]{:S(2)}, u32[]{:S(2)}) %collective-permute-start.6) | collective-permute-done | bytes 16416 | tf_op jit(solution)/shard_map/ppermute | solution.py:41
  48.6 0.6 %add_add_fusion = f32[32,128]{1,0:T(8,128)} fusion(f32[32,128]{1,0:T(8,128)S(1)} %collective-permute-done.7, f32[32,128]{1,0:T(8,128)S(1)} %fusion.4, f32[32,128]{1,0:T(8,128)S(1)} %collective-permute-done.5, f32[32,128]{1,0:T(8,128)S(1)} %collective-permute-done.6), kind=kLoop, calls=%fused_computation.59 | loop fusion | flops 12288 | bytes 81920 | tf_op jit(solution)/shard_map/add | solution.py:91
  (43 shorter events, 0.9 us)
Async XLA Ops:
  0.0 2.0 %copy-start = (bf16[1,256,3584]{2,1,0:T(8,128)(2,1)S(1)}, bf16[1,256,3584]{2,1,0:T(8,128)(2,1)}, u32[]{:S(2)}) copy-start(bf16[1,256,3584]{2,1,0:T(8,128)(2,1)} %param.10) | copy-start | bytes 5505028
  0.0 1.4 %copy-start.5 = (bf16[1024,64]{0,1:T(8,128)(2,1)S(1)}, bf16[1024,64]{0,1:T(8,128)(2,1)}, u32[]{:S(2)}) copy-start(bf16[1024,64]{0,1:T(8,128)(2,1)} %param.13) | copy-start | bytes 393220
  0.0 1.5 %copy-start.2 = (bf16[1,256,1024]{2,1,0:T(8,128)(2,1)S(1)}, bf16[1,256,1024]{2,1,0:T(8,128)(2,1)}, u32[]{:S(2)}) copy-start(bf16[1,256,1024]{2,1,0:T(8,128)(2,1)} %param.9) | copy-start | bytes 1572868
  1.5 1.6 %copy-start.1 = (bf16[1,256,3584]{2,1,0:T(8,128)(2,1)S(1)}, bf16[1,256,3584]{2,1,0:T(8,128)(2,1)}, u32[]{:S(2)}) copy-start(bf16[1,256,3584]{2,1,0:T(8,128)(2,1)} %param.11) | copy-start | bytes 5505028
  2.7 1.2 %copy-start.3 = (bf16[1,256,1024]{2,1,0:T(8,128)(2,1)S(1)}, bf16[1,256,1024]{2,1,0:T(8,128)(2,1)}, u32[]{:S(2)}) copy-start(bf16[1,256,1024]{2,1,0:T(8,128)(2,1)} %param.12) | copy-start | bytes 1572868
  2.7 1.2 %copy-start.6 = (bf16[1024,64]{0,1:T(8,128)(2,1)S(1)}, bf16[1024,64]{0,1:T(8,128)(2,1)}, u32[]{:S(2)}) copy-start(bf16[1024,64]{0,1:T(8,128)(2,1)} %param.16) | copy-start | bytes 393220
  4.2 15.4 %copy-start.4 = (bf16[128,1024]{1,0:T(8,128)(2,1)S(1)}, bf16[128,1024]{1,0:T(8,128)(2,1)}, u32[]{:S(2)}) copy-start(bf16[128,1024]{1,0:T(8,128)(2,1)} %param.17) | copy-start | bytes 786436
  4.3 5.5 %collective-permute-start.2 = (bf16[128,256]{1,0:T(8,128)(2,1)S(1)}, bf16[128,256]{1,0:T(8,128)(2,1)S(1)}, u32[]{:S(2)}, u32[]{:S(2)}) collective-permute-start(bf16[128,256]{1,0:T(8,128)(2,1)S(1)} %pad_maximum_fusion.8), channel_id=1, source_target_pairs={{0,4},{2,6},{4,0},{6,2},{1,5},{3,7},{5,1},{7,3},{8,12},{10,14},{12... | collective-permute-start | bytes 196616 | tf_op jit(solution)/shard_map/ppermute | solution.py:41
  8.2 5.0 %collective-permute-start.1 = (bf16[128,256]{1,0:T(8,128)(2,1)S(1)}, bf16[128,256]{1,0:T(8,128)(2,1)S(1)}, u32[]{:S(2)}, u32[]{:S(2)}) collective-permute-start(bf16[128,256]{1,0:T(8,128)(2,1)S(1)} %pad_maximum_fusion.7), channel_id=1, source_target_pairs={{0,6},{2,4},{4,2},{6,0},{1,7},{3,5},{5,3},{7,1},{8,14},{10,12},{12... | collective-permute-start | bytes 196616 | tf_op jit(solution)/shard_map/ppermute | solution.py:41
  8.9 4.3 %collective-permute-start = (bf16[128,256]{1,0:T(8,128)(2,1)S(1)}, bf16[128,256]{1,0:T(8,128)(2,1)S(1)}, u32[]{:S(2)}, u32[]{:S(2)}) collective-permute-start(bf16[128,256]{1,0:T(8,128)(2,1)S(1)} %pad_maximum_fusion.6), channel_id=1, source_target_pairs={{0,2},{2,0},{4,6},{6,4},{1,3},{3,1},{5,7},{7,5},{8,10},{10,8},{12,... | collective-permute-start | bytes 196616 | tf_op jit(solution)/shard_map/ppermute | solution.py:41
  13.3 8.4 %collective-permute-start.3 = (f32[96,256]{1,0:T(8,128)S(1)}, f32[96,256]{1,0:T(8,128)S(1)}, u32[]{:S(2)}, u32[]{:S(2)}) collective-permute-start(f32[96,256]{1,0:T(8,128)S(1)} %fusion.21), channel_id=1, source_target_pairs={{0,1},{1,0},{2,3},{3,2},{4,5},{5,4},{6,7},{7,6},{8,9},{9,8},{10,11... | collective-permute-start | bytes 294920 | tf_op jit(solution)/shard_map/ppermute | solution.py:41
  19.6 14.9 %collective-permute-start.4 = (bf16[128,1024]{1,0:T(8,128)(2,1)S(1)}, bf16[128,1024]{1,0:T(8,128)(2,1)S(1)}, u32[]{:S(2)}, u32[]{:S(2)}) collective-permute-start(bf16[128,1024]{1,0:T(8,128)(2,1)S(1)} %copy-done.4), channel_id=1, source_target_pairs={{0,1},{1,0},{2,3},{3,2},{4,5},{5,4},{6,7},{7,6},{8,9},{9,8},{10,11... | collective-permute-start | bytes 786440 | tf_op jit(solution)/shard_map/ppermute | solution.py:41
  22.9 20.3 %all-to-all-start = ((bf16[32,16,128]{2,1,0:T(8,128)(2,1)}), bf16[32,16,128]{2,1,0:T(8,128)(2,1)S(1)}, u32[]{:S(2)}, u32[]{:S(2)}) async-start(bf16[32,16,128]{2,1,0:T(8,128)(2,1)} %broadcast_in_dim.3), calls=%async_computation | async-start | bytes 262144 | tf_op jit(solution)/shard_map/all_to_all | solution.py:36
  43.4 4.1 %collective-permute-start.5 = (f32[32,128]{1,0:T(8,128)S(1)}, f32[32,128]{1,0:T(8,128)S(1)}, u32[]{:S(2)}, u32[]{:S(2)}) collective-permute-start(f32[32,128]{1,0:T(8,128)S(1)} %fusion.4), channel_id=1, source_target_pairs={{0,4},{2,6},{4,0},{6,2},{1,5},{3,7},{5,1},{7,3},{8,12},{10,14},{12... | collective-permute-start | bytes 49160 | tf_op jit(solution)/shard_map/ppermute | solution.py:41
  44.7 3.9 %collective-permute-start.6 = (f32[32,128]{1,0:T(8,128)S(1)}, f32[32,128]{1,0:T(8,128)S(1)}, u32[]{:S(2)}, u32[]{:S(2)}) collective-permute-start(f32[32,128]{1,0:T(8,128)S(1)} %fusion.4), channel_id=1, source_target_pairs={{0,6},{2,4},{4,2},{6,0},{1,7},{3,5},{5,3},{7,1},{8,14},{10,12},{12... | collective-permute-start | bytes 49160 | tf_op jit(solution)/shard_map/ppermute | solution.py:41
  45.9 2.7 %collective-permute-start.7 = (f32[32,128]{1,0:T(8,128)S(1)}, f32[32,128]{1,0:T(8,128)S(1)}, u32[]{:S(2)}, u32[]{:S(2)}) collective-permute-start(f32[32,128]{1,0:T(8,128)S(1)} %fusion.4), channel_id=1, source_target_pairs={{0,2},{2,0},{4,6},{6,4},{1,3},{3,1},{5,7},{7,5},{8,10},{10,8},{12,... | collective-permute-start | bytes 49160 | tf_op jit(solution)/shard_map/ppermute | solution.py:41

commit v8 on v6

--- a/solution.py
+++ b/solution.py
@@ -79,7 +79,8 @@
     sums = half + swap(half, "zh", 1)
     outs, ins = sums[:outer], sums[outer:]
     own = jnp.concatenate([outer_rows(outs[0::2], ins), outer_rows(outs[1::2], ins)], axis=1)
-    every = to_all(own.astype(jnp.bfloat16), DP, zls * xs * cores)
+    every = to_all(own.astype(jnp.bfloat16), DP[::-1], zls * xs * cores)
+    every = every.reshape((cores, xs, zls) + own.shape).transpose(2, 1, 0, 3, 4).reshape(every.shape)
     first_half = lax.axis_index("zh") == 0
     low, high = jnp.where(first_half, queries, other), jnp.where(first_half, other, queries)
     scores = lax.dot_general(

time: 49.2 us -> 49.7 us (1.010)
  no operation moved by 1% of the time
where the time goes in v8:
time: 49.7 us; the launch traced here: 49.1 us
  starting transfers between devices  25.3 us (51%)
  waiting for transfers between devices  17.4 us (35%)
  matrix products  2.49 us (5%)
  other arithmetic  2.32 us (5%)
  local copies, waits for them, and re-layouts  1.29 us (3%)
    ppermute x8, starting transfers between devices, swap(): return lax.ppermute(values, axis, [(k, k ^ mask) for k in range(size)])  13.7 us
    all_to_all x1, starting transfers between devices, exchange(): return lax.all_to_all(pieces, axes, split_axis=0, concat_axis=0, tiled=True)  11.6 us
    ppermute x8, waiting for transfers between devices, swap(): return lax.ppermute(values, axis, [(k, k ^ mask) for k in range(size)])  8.96 us
    all_to_all x1, waiting for transfers between devices, exchange(): return lax.all_to_all(pieces, axes, split_axis=0, concat_axis=0, tiled=True)  8.47 us
    dot_general x4, matrix products, project_columns(): lax.dot_general(proj, acts[0], (((0,), (1,)), ((), ())), preferred_elemen...  1.9 us
    concatenate x1, other arithmetic, per_device(): jnp.concatenate([up_out_proj, down_in_proj], axis=1)  1.37 us
  transfers between devices with their start and end apart: 9, of which 6 were waited for; matrix products, arithmetic and copies ran while one was open for 3% of the time, Pallas kernels for 0%

profile of v8, /device:TPU:1, one launch (start us, length us, event | category | flops | bytes accessed | tf_op | source)
XLA Modules:
  0.0 49.1 jit_solution(18437091428961051794)
XLA Ops:
  0.0 1.4 %pad_maximum_fusion = bf16[3584,128]{0,1:T(8,128)(2,1)S(1)} fusion(bf16[3584,64]{0,1:T(8,128)(2,1)} %param.15, bf16[3584,64]{0,1:T(8,128)(2,1)} %param.14), kind=kLoop, calls=%fused_computation.6 | loop fusion | flops 1835008 | bytes 1835008 | tf_op jit(solution)/shard_map/concatenate | solution.py:63
  1.4 0.4 copy-done
  1.8 0.7 %fusion.2 = f32[64,256]{1,0:T(8,128)S(1)} fusion(bf16[1,256,3584]{2,1,0:T(8,128)(2,1)S(1)} %copy-done, bf16[3584,128]{0,1:T(8,128)(2,1)S(1)} %pad_maximum_fusion), kind=kOutput, calls=%fused_computation.2 | convolution fusion | flops 117440512 | bytes 2359296 | tf_op jit(solution)/shard_map/dot_general | solution.py:13
  2.5 0.7 %fusion = f32[64,256]{1,0:T(8,128)S(1)} fusion(bf16[1,256,3584]{2,1,0:T(8,128)(2,1)S(1)} %copy-done.1, bf16[3584,128]{0,1:T(8,128)(2,1)S(1)} %pad_maximum_fusion), kind=kOutput, calls=%fused_computation | convolution fusion | flops 117440512 | bytes 2359296 | tf_op jit(solution)/shard_map/dot_general | solution.py:13
  3.2 0.3 fusion.8
  3.6 0.3 fusion.10
  4.0 3.8 %collective-permute-start.2 = (bf16[128,256]{1,0:T(8,128)(2,1)S(1)}, bf16[128,256]{1,0:T(8,128)(2,1)S(1)}, u32[]{:S(2)}, u32[]{:S(2)}) collective-permute-start(bf16[128,256]{1,0:T(8,128)(2,1)S(1)} %pad_maximum_fusion.8), channel_id=1, source_target_pairs={{0,4},{2,6},{4,0},{6,2},{1,5},{3,7},{5,1},{7,3},{8,12},{10,14},{12... | collective-permute-start | bytes 196616 | tf_op jit(solution)/shard_map/ppermute | solution.py:41
  7.9 0.8 %collective-permute-start.1 = (bf16[128,256]{1,0:T(8,128)(2,1)S(1)}, bf16[128,256]{1,0:T(8,128)(2,1)S(1)}, u32[]{:S(2)}, u32[]{:S(2)}) collective-permute-start(bf16[128,256]{1,0:T(8,128)(2,1)S(1)} %pad_maximum_fusion.7), channel_id=1, source_target_pairs={{0,6},{2,4},{4,2},{6,0},{1,7},{3,5},{5,3},{7,1},{8,14},{10,12},{12... | collective-permute-start | bytes 196616 | tf_op jit(solution)/shard_map/ppermute | solution.py:41
  8.7 0.9 %collective-permute-done.2 = bf16[128,256]{1,0:T(8,128)(2,1)S(1)} collective-permute-done((bf16[128,256]{1,0:T(8,128)(2,1)S(1)}, bf16[128,256]{1,0:T(8,128)(2,1)S(1)}, u32[]{:S(2)}, u32[]{:S(2)}) %collective-permute-start.2) | collective-permute-done | bytes 65568 | tf_op jit(solution)/shard_map/ppermute | solution.py:41
  9.5 3.4 %collective-permute-done.1 = bf16[128,256]{1,0:T(8,128)(2,1)S(1)} collective-permute-done((bf16[128,256]{1,0:T(8,128)(2,1)S(1)}, bf16[128,256]{1,0:T(8,128)(2,1)S(1)}, u32[]{:S(2)}, u32[]{:S(2)}) %collective-permute-start.1) | collective-permute-done | bytes 65568 | tf_op jit(solution)/shard_map/ppermute | solution.py:41
  13.1 6.3 %collective-permute-start.3 = (f32[96,256]{1,0:T(8,128)S(1)}, f32[96,256]{1,0:T(8,128)S(1)}, u32[]{:S(2)}, u32[]{:S(2)}) collective-permute-start(f32[96,256]{1,0:T(8,128)S(1)} %fusion.21), channel_id=1, source_target_pairs={{0,1},{1,0},{2,3},{3,2},{4,5},{5,4},{6,7},{7,6},{8,9},{9,8},{10,11... | collective-permute-start | bytes 294920 | tf_op jit(solution)/shard_map/ppermute | solution.py:41
  19.5 2.0 %collective-permute-done.3 = f32[96,256]{1,0:T(8,128)S(1)} collective-permute-done((f32[96,256]{1,0:T(8,128)S(1)}, f32[96,256]{1,0:T(8,128)S(1)}, u32[]{:S(2)}, u32[]{:S(2)}) %collective-permute-start.3) | collective-permute-done | bytes 98336 | tf_op jit(solution)/shard_map/ppermute | solution.py:41
  21.5 0.1 convolution_convert_fusion.1
  21.7 0.2 convolution_convert_fusion
  21.9 0.7 %broadcast_in_dim.3 = bf16[32,16,128]{2,1,0:T(8,128)(2,1)} broadcast(bf16[16,128]{1,0:T(8,128)(2,1)S(1)} %pad_maximum_fusion.9), dimensions={1,2} | broadcast | bytes 135168 | tf_op jit(solution)/shard_map/broadcast_in_dim | solution.py:45
  22.6 11.6 %all-to-all-start = ((bf16[32,16,128]{2,1,0:T(8,128)(2,1)}), bf16[32,16,128]{2,1,0:T(8,128)(2,1)S(1)}, u32[]{:S(2)}, u32[]{:S(2)}) async-start(bf16[32,16,128]{2,1,0:T(8,128)(2,1)} %broadcast_in_dim.3), calls=%async_computation | async-start | bytes 262144 | tf_op jit(solution)/shard_map/all_to_all | solution.py:36
  34.3 8.5 %all-to-all-done = bf16[32,16,128]{2,1,0:T(8,128)(2,1)S(1)} async-done(((bf16[32,16,128]{2,1,0:T(8,128)(2,1)}), bf16[32,16,128]{2,1,0:T(8,128)(2,1)S(1)}, u32[]{:S(2)}, u32[]{:S(2)}) %all-to-all-start) | async-done | bytes 131104 | tf_op jit(solution)/shard_map/all_to_all | solution.py:36
  42.8 0.3 fusion.4
  43.1 1.3 %collective-permute-start.5 = (f32[32,128]{1,0:T(8,128)S(1)}, f32[32,128]{1,0:T(8,128)S(1)}, u32[]{:S(2)}, u32[]{:S(2)}) collective-permute-start(f32[32,128]{1,0:T(8,128)S(1)} %fusion.4), channel_id=1, source_target_pairs={{0,4},{2,6},{4,0},{6,2},{1,5},{3,7},{5,1},{7,3},{8,12},{10,14},{12... | collective-permute-start | bytes 49160 | tf_op jit(solution)/shard_map/ppermute | solution.py:41
  44.4 1.0 %collective-permute-start.6 = (f32[32,128]{1,0:T(8,128)S(1)}, f32[32,128]{1,0:T(8,128)S(1)}, u32[]{:S(2)}, u32[]{:S(2)}) collective-permute-start(f32[32,128]{1,0:T(8,128)S(1)} %fusion.4), channel_id=1, source_target_pairs={{0,6},{2,4},{4,2},{6,0},{1,7},{3,5},{5,3},{7,1},{8,14},{10,12},{12... | collective-permute-start | bytes 49160 | tf_op jit(solution)/shard_map/ppermute | solution.py:41
  45.4 0.4 collective-permute-start.7
  45.7 1.4 %collective-permute-done.5 = f32[32,128]{1,0:T(8,128)S(1)} collective-permute-done((f32[32,128]{1,0:T(8,128)S(1)}, f32[32,128]{1,0:T(8,128)S(1)}, u32[]{:S(2)}, u32[]{:S(2)}) %collective-permute-start.5) | collective-permute-done | bytes 16416 | tf_op jit(solution)/shard_map/ppermute | solution.py:41
  47.2 1.3 %collective-permute-done.6 = f32[32,128]{1,0:T(8,128)S(1)} collective-permute-done((f32[32,128]{1,0:T(8,128)S(1)}, f32[32,128]{1,0:T(8,128)S(1)}, u32[]{:S(2)}, u32[]{:S(2)}) %collective-permute-start.6) | collective-permute-done | bytes 16416 | tf_op jit(solution)/shard_map/ppermute | solution.py:41
  48.5 0.6 %add_add_fusion = f32[32,128]{1,0:T(8,128)} fusion(f32[32,128]{1,0:T(8,128)S(1)} %collective-permute-done.7, f32[32,128]{1,0:T(8,128)S(1)} %fusion.4, f32[32,128]{1,0:T(8,128)S(1)} %collective-permute-done.5, f32[32,128]{1,0:T(8,128)S(1)} %collective-permute-done.6), kind=kLoop, calls=%fused_computation.59 | loop fusion | flops 12288 | bytes 81920 | tf_op jit(solution)/shard_map/add | solution.py:91
  (44 shorter events, 0.7 us)
Async XLA Ops:
  0.0 1.8 %copy-start = (bf16[1,256,3584]{2,1,0:T(8,128)(2,1)S(1)}, bf16[1,256,3584]{2,1,0:T(8,128)(2,1)}, u32[]{:S(2)}) copy-start(bf16[1,256,3584]{2,1,0:T(8,128)(2,1)} %param.10) | copy-start | bytes 5505028
  0.0 2.5 %copy-start.1 = (bf16[1,256,3584]{2,1,0:T(8,128)(2,1)S(1)}, bf16[1,256,3584]{2,1,0:T(8,128)(2,1)}, u32[]{:S(2)}) copy-start(bf16[1,256,3584]{2,1,0:T(8,128)(2,1)} %param.11) | copy-start | bytes 5505028
  1.8 1.4 %copy-start.2 = (bf16[1,256,1024]{2,1,0:T(8,128)(2,1)S(1)}, bf16[1,256,1024]{2,1,0:T(8,128)(2,1)}, u32[]{:S(2)}) copy-start(bf16[1,256,1024]{2,1,0:T(8,128)(2,1)} %param.12) | copy-start | bytes 1572868
  1.8 1.4 %copy-start.5 = (bf16[1024,64]{0,1:T(8,128)(2,1)S(1)}, bf16[1024,64]{0,1:T(8,128)(2,1)}, u32[]{:S(2)}) copy-start(bf16[1024,64]{0,1:T(8,128)(2,1)} %param.16) | copy-start | bytes 393220
  2.5 1.1 %copy-start.3 = (bf16[1,256,1024]{2,1,0:T(8,128)(2,1)S(1)}, bf16[1,256,1024]{2,1,0:T(8,128)(2,1)}, u32[]{:S(2)}) copy-start(bf16[1,256,1024]{2,1,0:T(8,128)(2,1)} %param.9) | copy-start | bytes 1572868
  2.5 1.1 %copy-start.6 = (bf16[1024,64]{0,1:T(8,128)(2,1)S(1)}, bf16[1024,64]{0,1:T(8,128)(2,1)}, u32[]{:S(2)}) copy-start(bf16[1024,64]{0,1:T(8,128)(2,1)} %param.13) | copy-start | bytes 393220
  3.9 15.4 %copy-start.4 = (bf16[128,1024]{1,0:T(8,128)(2,1)S(1)}, bf16[128,1024]{1,0:T(8,128)(2,1)}, u32[]{:S(2)}) copy-start(bf16[128,1024]{1,0:T(8,128)(2,1)} %param.17) | copy-start | bytes 786436
  4.0 5.5 %collective-permute-start.2 = (bf16[128,256]{1,0:T(8,128)(2,1)S(1)}, bf16[128,256]{1,0:T(8,128)(2,1)S(1)}, u32[]{:S(2)}, u32[]{:S(2)}) collective-permute-start(bf16[128,256]{1,0:T(8,128)(2,1)S(1)} %pad_maximum_fusion.8), channel_id=1, source_target_pairs={{0,4},{2,6},{4,0},{6,2},{1,5},{3,7},{5,1},{7,3},{8,12},{10,14},{12... | collective-permute-start | bytes 196616 | tf_op jit(solution)/shard_map/ppermute | solution.py:41
  7.9 5.0 %collective-permute-start.1 = (bf16[128,256]{1,0:T(8,128)(2,1)S(1)}, bf16[128,256]{1,0:T(8,128)(2,1)S(1)}, u32[]{:S(2)}, u32[]{:S(2)}) collective-permute-start(bf16[128,256]{1,0:T(8,128)(2,1)S(1)} %pad_maximum_fusion.7), channel_id=1, source_target_pairs={{0,6},{2,4},{4,2},{6,0},{1,7},{3,5},{5,3},{7,1},{8,14},{10,12},{12... | collective-permute-start | bytes 196616 | tf_op jit(solution)/shard_map/ppermute | solution.py:41
  8.6 4.3 %collective-permute-start = (bf16[128,256]{1,0:T(8,128)(2,1)S(1)}, bf16[128,256]{1,0:T(8,128)(2,1)S(1)}, u32[]{:S(2)}, u32[]{:S(2)}) collective-permute-start(bf16[128,256]{1,0:T(8,128)(2,1)S(1)} %pad_maximum_fusion.6), channel_id=1, source_target_pairs={{0,2},{2,0},{4,6},{6,4},{1,3},{3,1},{5,7},{7,5},{8,10},{10,8},{12,... | collective-permute-start | bytes 196616 | tf_op jit(solution)/shard_map/ppermute | solution.py:41
  13.1 8.4 %collective-permute-start.3 = (f32[96,256]{1,0:T(8,128)S(1)}, f32[96,256]{1,0:T(8,128)S(1)}, u32[]{:S(2)}, u32[]{:S(2)}) collective-permute-start(f32[96,256]{1,0:T(8,128)S(1)} %fusion.21), channel_id=1, source_target_pairs={{0,1},{1,0},{2,3},{3,2},{4,5},{5,4},{6,7},{7,6},{8,9},{9,8},{10,11... | collective-permute-start | bytes 294920 | tf_op jit(solution)/shard_map/ppermute | solution.py:41
  19.4 14.9 %collective-permute-start.4 = (bf16[128,1024]{1,0:T(8,128)(2,1)S(1)}, bf16[128,1024]{1,0:T(8,128)(2,1)S(1)}, u32[]{:S(2)}, u32[]{:S(2)}) collective-permute-start(bf16[128,1024]{1,0:T(8,128)(2,1)S(1)} %copy-done.4), channel_id=1, source_target_pairs={{0,1},{1,0},{2,3},{3,2},{4,5},{5,4},{6,7},{7,6},{8,9},{9,8},{10,11... | collective-permute-start | bytes 786440 | tf_op jit(solution)/shard_map/ppermute | solution.py:41
  22.6 20.1 %all-to-all-start = ((bf16[32,16,128]{2,1,0:T(8,128)(2,1)}), bf16[32,16,128]{2,1,0:T(8,128)(2,1)S(1)}, u32[]{:S(2)}, u32[]{:S(2)}) async-start(bf16[32,16,128]{2,1,0:T(8,128)(2,1)} %broadcast_in_dim.3), calls=%async_computation | async-start | bytes 262144 | tf_op jit(solution)/shard_map/all_to_all | solution.py:36
  43.1 4.1 %collective-permute-start.5 = (f32[32,128]{1,0:T(8,128)S(1)}, f32[32,128]{1,0:T(8,128)S(1)}, u32[]{:S(2)}, u32[]{:S(2)}) collective-permute-start(f32[32,128]{1,0:T(8,128)S(1)} %fusion.4), channel_id=1, source_target_pairs={{0,4},{2,6},{4,0},{6,2},{1,5},{3,7},{5,1},{7,3},{8,12},{10,14},{12... | collective-permute-start | bytes 49160 | tf_op jit(solution)/shard_map/ppermute | solution.py:41
  44.4 4.1 %collective-permute-start.6 = (f32[32,128]{1,0:T(8,128)S(1)}, f32[32,128]{1,0:T(8,128)S(1)}, u32[]{:S(2)}, u32[]{:S(2)}) collective-permute-start(f32[32,128]{1,0:T(8,128)S(1)} %fusion.4), channel_id=1, source_target_pairs={{0,6},{2,4},{4,2},{6,0},{1,7},{3,5},{5,3},{7,1},{8,14},{10,12},{12... | collective-permute-start | bytes 49160 | tf_op jit(solution)/shard_map/ppermute | solution.py:41
  45.4 3.1 %collective-permute-start.7 = (f32[32,128]{1,0:T(8,128)S(1)}, f32[32,128]{1,0:T(8,128)S(1)}, u32[]{:S(2)}, u32[]{:S(2)}) collective-permute-start(f32[32,128]{1,0:T(8,128)S(1)} %fusion.4), channel_id=1, source_target_pairs={{0,2},{2,0},{4,6},{6,4},{1,3},{3,1},{5,7},{7,5},{8,10},{10,8},{12,... | collective-permute-start | bytes 49160 | tf_op jit(solution)/shard_map/ppermute | solution.py:41

commit v9 on v6

--- a/solution.py
+++ b/solution.py
@@ -78,7 +78,8 @@
     )
     sums = half + swap(half, "zh", 1)
     outs, ins = sums[:outer], sums[outer:]
-    own = jnp.concatenate([outer_rows(outs[0::2], ins), outer_rows(outs[1::2], ins)], axis=1)
+    own = outer_rows(jnp.concatenate([outs[0::2], outs[1::2]], axis=0), ins)
+    own = jnp.concatenate([own[:rows], own[rows:]], axis=1)
     every = to_all(own.astype(jnp.bfloat16), DP, zls * xs * cores)
     first_half = lax.axis_index("zh") == 0
     low, high = jnp.where(first_half, queries, other), jnp.where(first_half, other, queries)

time: 49.2 us -> 49.1 us (level)
  transfers between devices with their start and end apart: 9 -> 9, of which waited for: 6 -> 6; matrix products, arithmetic and copies ran while one was open for 3% -> 2% of each run, Pallas kernels for 0% -> 0%
where the time goes in v9:
time: 49.1 us; the launch traced here: 48.8 us
  starting transfers between devices  25.3 us (52%)
  waiting for transfers between devices  17.4 us (35%)
  matrix products  2.35 us (5%)
  other arithmetic  2.3 us (5%)
  local copies, waits for them, and re-layouts  1.27 us (3%)
    ppermute x8, starting transfers between devices, swap(): return lax.ppermute(values, axis, [(k, k ^ mask) for k in range(size)])  13.7 us
    all_to_all x1, starting transfers between devices, exchange(): return lax.all_to_all(pieces, axes, split_axis=0, concat_axis=0, tiled=True)  11.6 us
    all_to_all x1, waiting for transfers between devices, exchange(): return lax.all_to_all(pieces, axes, split_axis=0, concat_axis=0, tiled=True)  8.75 us
    ppermute x8, waiting for transfers between devices, swap(): return lax.ppermute(values, axis, [(k, k ^ mask) for k in range(size)])  8.61 us
    dot_general x4, matrix products, project_columns(): lax.dot_general(proj, acts[0], (((0,), (1,)), ((), ())), preferred_elemen...  1.9 us
    concatenate x1, other arithmetic, per_device(): jnp.concatenate([up_out_proj, down_in_proj], axis=1)  1.37 us
  transfers between devices with their start and end apart: 9, of which 6 were waited for; matrix products, arithmetic and copies ran while one was open for 2% of the time, Pallas kernels for 0%

profile of v9, /device:TPU:1, one launch (start us, length us, event | category | flops | bytes accessed | tf_op | source)
XLA Modules:
  0.0 48.8 jit_solution(15367829854518880337)
XLA Ops:
  0.0 1.4 %pad_maximum_fusion = bf16[3584,128]{0,1:T(8,128)(2,1)S(1)} fusion(bf16[3584,64]{0,1:T(8,128)(2,1)} %param.15, bf16[3584,64]{0,1:T(8,128)(2,1)} %param.14), kind=kLoop, calls=%fused_computation.5 | loop fusion | flops 1835008 | bytes 1835008 | tf_op jit(solution)/shard_map/concatenate | solution.py:63
  1.4 0.4 copy-done
  1.8 0.7 %fusion.2 = f32[64,256]{1,0:T(8,128)S(1)} fusion(bf16[1,256,3584]{2,1,0:T(8,128)(2,1)S(1)} %copy-done, bf16[3584,128]{0,1:T(8,128)(2,1)S(1)} %pad_maximum_fusion), kind=kOutput, calls=%fused_computation.2 | convolution fusion | flops 117440512 | bytes 2359296 | tf_op jit(solution)/shard_map/dot_general | solution.py:13
  2.5 0.7 %fusion = f32[64,256]{1,0:T(8,128)S(1)} fusion(bf16[1,256,3584]{2,1,0:T(8,128)(2,1)S(1)} %copy-done.1, bf16[3584,128]{0,1:T(8,128)(2,1)S(1)} %pad_maximum_fusion), kind=kOutput, calls=%fused_computation | convolution fusion | flops 117440512 | bytes 2359296 | tf_op jit(solution)/shard_map/dot_general | solution.py:13
  3.2 0.3 fusion.8
  3.6 0.3 fusion.10
  4.0 3.8 %collective-permute-start.2 = (bf16[128,256]{1,0:T(8,128)(2,1)S(1)}, bf16[128,256]{1,0:T(8,128)(2,1)S(1)}, u32[]{:S(2)}, u32[]{:S(2)}) collective-permute-start(bf16[128,256]{1,0:T(8,128)(2,1)S(1)} %pad_maximum_fusion.8), channel_id=1, source_target_pairs={{0,4},{2,6},{4,0},{6,2},{1,5},{3,7},{5,1},{7,3},{8,12},{10,14},{12... | collective-permute-start | bytes 196616 | tf_op jit(solution)/shard_map/ppermute | solution.py:41
  7.9 0.8 %collective-permute-start.1 = (bf16[128,256]{1,0:T(8,128)(2,1)S(1)}, bf16[128,256]{1,0:T(8,128)(2,1)S(1)}, u32[]{:S(2)}, u32[]{:S(2)}) collective-permute-start(bf16[128,256]{1,0:T(8,128)(2,1)S(1)} %pad_maximum_fusion.7), channel_id=1, source_target_pairs={{0,6},{2,4},{4,2},{6,0},{1,7},{3,5},{5,3},{7,1},{8,14},{10,12},{12... | collective-permute-start | bytes 196616 | tf_op jit(solution)/shard_map/ppermute | solution.py:41
  8.7 0.9 %collective-permute-done.2 = bf16[128,256]{1,0:T(8,128)(2,1)S(1)} collective-permute-done((bf16[128,256]{1,0:T(8,128)(2,1)S(1)}, bf16[128,256]{1,0:T(8,128)(2,1)S(1)}, u32[]{:S(2)}, u32[]{:S(2)}) %collective-permute-start.2) | collective-permute-done | bytes 65568 | tf_op jit(solution)/shard_map/ppermute | solution.py:41
  9.5 3.4 %collective-permute-done.1 = bf16[128,256]{1,0:T(8,128)(2,1)S(1)} collective-permute-done((bf16[128,256]{1,0:T(8,128)(2,1)S(1)}, bf16[128,256]{1,0:T(8,128)(2,1)S(1)}, u32[]{:S(2)}, u32[]{:S(2)}) %collective-permute-start.1) | collective-permute-done | bytes 65568 | tf_op jit(solution)/shard_map/ppermute | solution.py:41
  13.1 6.3 %collective-permute-start.3 = (f32[96,256]{1,0:T(8,128)S(1)}, f32[96,256]{1,0:T(8,128)S(1)}, u32[]{:S(2)}, u32[]{:S(2)}) collective-permute-start(f32[96,256]{1,0:T(8,128)S(1)} %fusion.21), channel_id=1, source_target_pairs={{0,1},{1,0},{2,3},{3,2},{4,5},{5,4},{6,7},{7,6},{8,9},{9,8},{10,11... | collective-permute-start | bytes 294920 | tf_op jit(solution)/shard_map/ppermute | solution.py:41
  19.4 0.1 collective-permute-start.4
  19.5 2.0 %collective-permute-done.3 = f32[96,256]{1,0:T(8,128)S(1)} collective-permute-done((f32[96,256]{1,0:T(8,128)S(1)}, f32[96,256]{1,0:T(8,128)S(1)}, u32[]{:S(2)}, u32[]{:S(2)}) %collective-permute-start.3) | collective-permute-done | bytes 98336 | tf_op jit(solution)/shard_map/ppermute | solution.py:41
  21.5 0.2 convolution_convert_fusion
  21.8 0.7 %broadcast_in_dim.3 = bf16[32,16,128]{2,1,0:T(8,128)(2,1)} broadcast(bf16[16,128]{1,0:T(8,128)(2,1)S(1)} %pad_maximum_fusion.9), dimensions={1,2} | broadcast | bytes 135168 | tf_op jit(solution)/shard_map/broadcast_in_dim | solution.py:45
  22.5 11.6 %all-to-all-start = ((bf16[32,16,128]{2,1,0:T(8,128)(2,1)}), bf16[32,16,128]{2,1,0:T(8,128)(2,1)S(1)}, u32[]{:S(2)}, u32[]{:S(2)}) async-start(bf16[32,16,128]{2,1,0:T(8,128)(2,1)} %broadcast_in_dim.3), calls=%async_computation | async-start | bytes 262144 | tf_op jit(solution)/shard_map/all_to_all | solution.py:36
  34.1 8.8 %all-to-all-done = bf16[32,16,128]{2,1,0:T(8,128)(2,1)S(1)} async-done(((bf16[32,16,128]{2,1,0:T(8,128)(2,1)}), bf16[32,16,128]{2,1,0:T(8,128)(2,1)S(1)}, u32[]{:S(2)}, u32[]{:S(2)}) %all-to-all-start) | async-done | bytes 131104 | tf_op jit(solution)/shard_map/all_to_all | solution.py:36
  42.9 0.3 fusion.4
  43.2 1.3 %collective-permute-start.5 = (f32[32,128]{1,0:T(8,128)S(1)}, f32[32,128]{1,0:T(8,128)S(1)}, u32[]{:S(2)}, u32[]{:S(2)}) collective-permute-start(f32[32,128]{1,0:T(8,128)S(1)} %fusion.4), channel_id=1, source_target_pairs={{0,4},{2,6},{4,0},{6,2},{1,5},{3,7},{5,1},{7,3},{8,12},{10,14},{12... | collective-permute-start | bytes 49160 | tf_op jit(solution)/shard_map/ppermute | solution.py:41
  44.4 1.2 %collective-permute-start.6 = (f32[32,128]{1,0:T(8,128)S(1)}, f32[32,128]{1,0:T(8,128)S(1)}, u32[]{:S(2)}, u32[]{:S(2)}) collective-permute-start(f32[32,128]{1,0:T(8,128)S(1)} %fusion.4), channel_id=1, source_target_pairs={{0,6},{2,4},{4,2},{6,0},{1,7},{3,5},{5,3},{7,1},{8,14},{10,12},{12... | collective-permute-start | bytes 49160 | tf_op jit(solution)/shard_map/ppermute | solution.py:41
  45.6 0.3 collective-permute-start.7
  45.8 1.4 %collective-permute-done.5 = f32[32,128]{1,0:T(8,128)S(1)} collective-permute-done((f32[32,128]{1,0:T(8,128)S(1)}, f32[32,128]{1,0:T(8,128)S(1)}, u32[]{:S(2)}, u32[]{:S(2)}) %collective-permute-start.5) | collective-permute-done | bytes 16416 | tf_op jit(solution)/shard_map/ppermute | solution.py:41
  47.3 0.9 %collective-permute-done.6 = f32[32,128]{1,0:T(8,128)S(1)} collective-permute-done((f32[32,128]{1,0:T(8,128)S(1)}, f32[32,128]{1,0:T(8,128)S(1)}, u32[]{:S(2)}, u32[]{:S(2)}) %collective-permute-start.6) | collective-permute-done | bytes 16416 | tf_op jit(solution)/shard_map/ppermute | solution.py:41
  48.2 0.6 %add_add_fusion = f32[32,128]{1,0:T(8,128)} fusion(f32[32,128]{1,0:T(8,128)S(1)} %collective-permute-done.7, f32[32,128]{1,0:T(8,128)S(1)} %fusion.4, f32[32,128]{1,0:T(8,128)S(1)} %collective-permute-done.5, f32[32,128]{1,0:T(8,128)S(1)} %collective-permute-done.6), kind=kLoop, calls=%fused_computation.60 | loop fusion | flops 12288 | bytes 81920 | tf_op jit(solution)/shard_map/add | solution.py:91
  (43 shorter events, 0.5 us)
Async XLA Ops:
  0.0 1.8 %copy-start = (bf16[1,256,3584]{2,1,0:T(8,128)(2,1)S(1)}, bf16[1,256,3584]{2,1,0:T(8,128)(2,1)}, u32[]{:S(2)}) copy-start(bf16[1,256,3584]{2,1,0:T(8,128)(2,1)} %param.10) | copy-start | bytes 5505028
  0.0 2.5 %copy-start.1 = (bf16[1,256,3584]{2,1,0:T(8,128)(2,1)S(1)}, bf16[1,256,3584]{2,1,0:T(8,128)(2,1)}, u32[]{:S(2)}) copy-start(bf16[1,256,3584]{2,1,0:T(8,128)(2,1)} %param.11) | copy-start | bytes 5505028
  1.8 1.4 %copy-start.2 = (bf16[1,256,1024]{2,1,0:T(8,128)(2,1)S(1)}, bf16[1,256,1024]{2,1,0:T(8,128)(2,1)}, u32[]{:S(2)}) copy-start(bf16[1,256,1024]{2,1,0:T(8,128)(2,1)} %param.12) | copy-start | bytes 1572868
  1.8 1.4 %copy-start.5 = (bf16[1024,64]{0,1:T(8,128)(2,1)S(1)}, bf16[1024,64]{0,1:T(8,128)(2,1)}, u32[]{:S(2)}) copy-start(bf16[1024,64]{0,1:T(8,128)(2,1)} %param.16) | copy-start | bytes 393220
  2.5 1.1 %copy-start.3 = (bf16[1,256,1024]{2,1,0:T(8,128)(2,1)S(1)}, bf16[1,256,1024]{2,1,0:T(8,128)(2,1)}, u32[]{:S(2)}) copy-start(bf16[1,256,1024]{2,1,0:T(8,128)(2,1)} %param.9) | copy-start | bytes 1572868
  2.5 1.1 %copy-start.6 = (bf16[1024,64]{0,1:T(8,128)(2,1)S(1)}, bf16[1024,64]{0,1:T(8,128)(2,1)}, u32[]{:S(2)}) copy-start(bf16[1024,64]{0,1:T(8,128)(2,1)} %param.13) | copy-start | bytes 393220
  3.9 15.4 %copy-start.4 = (bf16[128,1024]{1,0:T(8,128)(2,1)S(1)}, bf16[128,1024]{1,0:T(8,128)(2,1)}, u32[]{:S(2)}) copy-start(bf16[128,1024]{1,0:T(8,128)(2,1)} %param.17) | copy-start | bytes 786436
  4.0 5.5 %collective-permute-start.2 = (bf16[128,256]{1,0:T(8,128)(2,1)S(1)}, bf16[128,256]{1,0:T(8,128)(2,1)S(1)}, u32[]{:S(2)}, u32[]{:S(2)}) collective-permute-start(bf16[128,256]{1,0:T(8,128)(2,1)S(1)} %pad_maximum_fusion.8), channel_id=1, source_target_pairs={{0,4},{2,6},{4,0},{6,2},{1,5},{3,7},{5,1},{7,3},{8,12},{10,14},{12... | collective-permute-start | bytes 196616 | tf_op jit(solution)/shard_map/ppermute | solution.py:41
  7.9 5.0 %collective-permute-start.1 = (bf16[128,256]{1,0:T(8,128)(2,1)S(1)}, bf16[128,256]{1,0:T(8,128)(2,1)S(1)}, u32[]{:S(2)}, u32[]{:S(2)}) collective-permute-start(bf16[128,256]{1,0:T(8,128)(2,1)S(1)} %pad_maximum_fusion.7), channel_id=1, source_target_pairs={{0,6},{2,4},{4,2},{6,0},{1,7},{3,5},{5,3},{7,1},{8,14},{10,12},{12... | collective-permute-start | bytes 196616 | tf_op jit(solution)/shard_map/ppermute | solution.py:41
  8.6 4.3 %collective-permute-start = (bf16[128,256]{1,0:T(8,128)(2,1)S(1)}, bf16[128,256]{1,0:T(8,128)(2,1)S(1)}, u32[]{:S(2)}, u32[]{:S(2)}) collective-permute-start(bf16[128,256]{1,0:T(8,128)(2,1)S(1)} %pad_maximum_fusion.6), channel_id=1, source_target_pairs={{0,2},{2,0},{4,6},{6,4},{1,3},{3,1},{5,7},{7,5},{8,10},{10,8},{12,... | collective-permute-start | bytes 196616 | tf_op jit(solution)/shard_map/ppermute | solution.py:41
  13.1 8.4 %collective-permute-start.3 = (f32[96,256]{1,0:T(8,128)S(1)}, f32[96,256]{1,0:T(8,128)S(1)}, u32[]{:S(2)}, u32[]{:S(2)}) collective-permute-start(f32[96,256]{1,0:T(8,128)S(1)} %fusion.21), channel_id=1, source_target_pairs={{0,1},{1,0},{2,3},{3,2},{4,5},{5,4},{6,7},{7,6},{8,9},{9,8},{10,11... | collective-permute-start | bytes 294920 | tf_op jit(solution)/shard_map/ppermute | solution.py:41
  19.4 14.7 %collective-permute-start.4 = (bf16[128,1024]{1,0:T(8,128)(2,1)S(1)}, bf16[128,1024]{1,0:T(8,128)(2,1)S(1)}, u32[]{:S(2)}, u32[]{:S(2)}) collective-permute-start(bf16[128,1024]{1,0:T(8,128)(2,1)S(1)} %copy-done.4), channel_id=1, source_target_pairs={{0,1},{1,0},{2,3},{3,2},{4,5},{5,4},{6,7},{7,6},{8,9},{9,8},{10,11... | collective-permute-start | bytes 786440 | tf_op jit(solution)/shard_map/ppermute | solution.py:41
  22.5 20.4 %all-to-all-start = ((bf16[32,16,128]{2,1,0:T(8,128)(2,1)}), bf16[32,16,128]{2,1,0:T(8,128)(2,1)S(1)}, u32[]{:S(2)}, u32[]{:S(2)}) async-start(bf16[32,16,128]{2,1,0:T(8,128)(2,1)} %broadcast_in_dim.3), calls=%async_computation | async-start | bytes 262144 | tf_op jit(solution)/shard_map/all_to_all | solution.py:36
  43.2 4.1 %collective-permute-start.5 = (f32[32,128]{1,0:T(8,128)S(1)}, f32[32,128]{1,0:T(8,128)S(1)}, u32[]{:S(2)}, u32[]{:S(2)}) collective-permute-start(f32[32,128]{1,0:T(8,128)S(1)} %fusion.4), channel_id=1, source_target_pairs={{0,4},{2,6},{4,0},{6,2},{1,5},{3,7},{5,1},{7,3},{8,12},{10,14},{12... | collective-permute-start | bytes 49160 | tf_op jit(solution)/shard_map/ppermute | solution.py:41
  44.4 3.8 %collective-permute-start.6 = (f32[32,128]{1,0:T(8,128)S(1)}, f32[32,128]{1,0:T(8,128)S(1)}, u32[]{:S(2)}, u32[]{:S(2)}) collective-permute-start(f32[32,128]{1,0:T(8,128)S(1)} %fusion.4), channel_id=1, source_target_pairs={{0,6},{2,4},{4,2},{6,0},{1,7},{3,5},{5,3},{7,1},{8,14},{10,12},{12... | collective-permute-start | bytes 49160 | tf_op jit(solution)/shard_map/ppermute | solution.py:41
  45.6 2.6 %collective-permute-start.7 = (f32[32,128]{1,0:T(8,128)S(1)}, f32[32,128]{1,0:T(8,128)S(1)}, u32[]{:S(2)}, u32[]{:S(2)}) collective-permute-start(f32[32,128]{1,0:T(8,128)S(1)} %fusion.4), channel_id=1, source_target_pairs={{0,2},{2,0},{4,6},{6,4},{1,3},{3,1},{5,7},{7,5},{8,10},{10,8},{12,... | collective-permute-start | bytes 49160 | tf_op jit(solution)/shard_map/ppermute | solution.py:41

commit v10 on v9

--- a/solution.py
+++ b/solution.py
@@ -28,7 +28,7 @@
 def outer_rows(outs, ins):
     return lax.dot_general(
         outs, ins, (((1,), (1,)), ((), ())),
-        precision=lax.Precision.HIGHEST, preferred_element_type=jnp.float32,
+        precision=lax.Precision.HIGH, preferred_element_type=jnp.float32,
     )
 
 
@@ -74,7 +74,7 @@
     piece = lambda k: lax.dynamic_index_in_dim(pieces, k, 0, keepdims=False)
     outer = zhs * rows
     half = piece(y) + sum(
-        from_sent(swap(to_send(piece(y ^ mask), outer), "y", mask), outer) for mask in (1, 3, 2)
+        from_sent(swap(to_send(piece(y ^ mask), outer), "y", mask), outer) for mask in (1, 2, 3)
     )
     sums = half + swap(half, "zh", 1)
     outs, ins = sums[:outer], sums[outer:]

time: 49.1 us -> 49.7 us (1.012)
  no operation moved by 1% of the time
where the time goes in v10:
time: 49.7 us; the launch traced here: 49.4 us
  starting transfers between devices  25.6 us (52%)
  waiting for transfers between devices  17.6 us (35%)
  matrix products  2.32 us (5%)
  other arithmetic  2.3 us (5%)
  local copies, waits for them, and re-layouts  1.28 us (3%)
    ppermute x8, starting transfers between devices, swap(): return lax.ppermute(values, axis, [(k, k ^ mask) for k in range(size)])  14 us
    all_to_all x1, starting transfers between devices, exchange(): return lax.all_to_all(pieces, axes, split_axis=0, concat_axis=0, tiled=True)  11.6 us
    ppermute x8, waiting for transfers between devices, swap(): return lax.ppermute(values, axis, [(k, k ^ mask) for k in range(size)])  8.87 us
    all_to_all x1, waiting for transfers between devices, exchange(): return lax.all_to_all(pieces, axes, split_axis=0, concat_axis=0, tiled=True)  8.77 us
    dot_general x4, matrix products, project_columns(): lax.dot_general(proj, acts[0], (((0,), (1,)), ((), ())), preferred_elemen...  1.9 us
    concatenate x1, other arithmetic, per_device(): jnp.concatenate([up_out_proj, down_in_proj], axis=1)  1.37 us
  transfers between devices with their start and end apart: 9, of which 6 were waited for; matrix products, arithmetic and copies ran while one was open for 2% of the time, Pallas kernels for 0%

profile of v10, /device:TPU:1, one launch (start us, length us, event | category | flops | bytes accessed | tf_op | source)
XLA Modules:
  0.0 49.4 jit_solution(11526095698921248280)
XLA Ops:
  0.0 1.4 %pad_maximum_fusion = bf16[3584,128]{0,1:T(8,128)(2,1)S(1)} fusion(bf16[3584,64]{0,1:T(8,128)(2,1)} %param.15, bf16[3584,64]{0,1:T(8,128)(2,1)} %param.14), kind=kLoop, calls=%fused_computation.5 | loop fusion | flops 1835008 | bytes 1835008 | tf_op jit(solution)/shard_map/concatenate | solution.py:63
  1.4 0.4 copy-done
  1.8 0.7 %fusion.2 = f32[64,256]{1,0:T(8,128)S(1)} fusion(bf16[1,256,3584]{2,1,0:T(8,128)(2,1)S(1)} %copy-done, bf16[3584,128]{0,1:T(8,128)(2,1)S(1)} %pad_maximum_fusion), kind=kOutput, calls=%fused_computation.2 | convolution fusion | flops 117440512 | bytes 2359296 | tf_op jit(solution)/shard_map/dot_general | solution.py:13
  2.5 0.7 %fusion = f32[64,256]{1,0:T(8,128)S(1)} fusion(bf16[1,256,3584]{2,1,0:T(8,128)(2,1)S(1)} %copy-done.1, bf16[3584,128]{0,1:T(8,128)(2,1)S(1)} %pad_maximum_fusion), kind=kOutput, calls=%fused_computation | convolution fusion | flops 117440512 | bytes 2359296 | tf_op jit(solution)/shard_map/dot_general | solution.py:13
  3.2 0.3 fusion.8
  3.6 0.3 fusion.10
  4.0 3.6 %collective-permute-start.2 = (bf16[128,256]{1,0:T(8,128)(2,1)S(1)}, bf16[128,256]{1,0:T(8,128)(2,1)S(1)}, u32[]{:S(2)}, u32[]{:S(2)}) collective-permute-start(bf16[128,256]{1,0:T(8,128)(2,1)S(1)} %pad_maximum_fusion.8), channel_id=1, source_target_pairs={{0,6},{2,4},{4,2},{6,0},{1,7},{3,5},{5,3},{7,1},{8,14},{10,12},{12... | collective-permute-start | bytes 196616 | tf_op jit(solution)/shard_map/ppermute | solution.py:41
  7.7 0.3 collective-permute-start.1
  8.0 0.3 collective-permute-start
  8.4 1.0 %collective-permute-done.2 = bf16[128,256]{1,0:T(8,128)(2,1)S(1)} collective-permute-done((bf16[128,256]{1,0:T(8,128)(2,1)S(1)}, bf16[128,256]{1,0:T(8,128)(2,1)S(1)}, u32[]{:S(2)}, u32[]{:S(2)}) %collective-permute-start.2) | collective-permute-done | bytes 65568 | tf_op jit(solution)/shard_map/ppermute | solution.py:41
  9.4 3.1 %collective-permute-done.1 = bf16[128,256]{1,0:T(8,128)(2,1)S(1)} collective-permute-done((bf16[128,256]{1,0:T(8,128)(2,1)S(1)}, bf16[128,256]{1,0:T(8,128)(2,1)S(1)}, u32[]{:S(2)}, u32[]{:S(2)}) %collective-permute-start.1) | collective-permute-done | bytes 65568 | tf_op jit(solution)/shard_map/ppermute | solution.py:41
  12.6 6.9 %collective-permute-start.3 = (f32[96,256]{1,0:T(8,128)S(1)}, f32[96,256]{1,0:T(8,128)S(1)}, u32[]{:S(2)}, u32[]{:S(2)}) collective-permute-start(f32[96,256]{1,0:T(8,128)S(1)} %fusion.21), channel_id=1, source_target_pairs={{0,1},{1,0},{2,3},{3,2},{4,5},{5,4},{6,7},{7,6},{8,9},{9,8},{10,11... | collective-permute-start | bytes 294920 | tf_op jit(solution)/shard_map/ppermute | solution.py:41
  19.5 0.1 collective-permute-start.4
  19.6 2.0 %collective-permute-done.3 = f32[96,256]{1,0:T(8,128)S(1)} collective-permute-done((f32[96,256]{1,0:T(8,128)S(1)}, f32[96,256]{1,0:T(8,128)S(1)}, u32[]{:S(2)}, u32[]{:S(2)}) %collective-permute-start.3) | collective-permute-done | bytes 98336 | tf_op jit(solution)/shard_map/ppermute | solution.py:41
  21.6 0.1 convolution_convert_fusion
  21.9 0.7 %broadcast_in_dim.3 = bf16[32,16,128]{2,1,0:T(8,128)(2,1)} broadcast(bf16[16,128]{1,0:T(8,128)(2,1)S(1)} %pad_maximum_fusion.9), dimensions={1,2} | broadcast | bytes 135168 | tf_op jit(solution)/shard_map/broadcast_in_dim | solution.py:45
  22.6 11.6 %all-to-all-start = ((bf16[32,16,128]{2,1,0:T(8,128)(2,1)}), bf16[32,16,128]{2,1,0:T(8,128)(2,1)S(1)}, u32[]{:S(2)}, u32[]{:S(2)}) async-start(bf16[32,16,128]{2,1,0:T(8,128)(2,1)} %broadcast_in_dim.3), calls=%async_computation | async-start | bytes 262144 | tf_op jit(solution)/shard_map/all_to_all | solution.py:36
  34.2 8.8 %all-to-all-done = bf16[32,16,128]{2,1,0:T(8,128)(2,1)S(1)} async-done(((bf16[32,16,128]{2,1,0:T(8,128)(2,1)}), bf16[32,16,128]{2,1,0:T(8,128)(2,1)S(1)}, u32[]{:S(2)}, u32[]{:S(2)}) %all-to-all-start) | async-done | bytes 131104 | tf_op jit(solution)/shard_map/all_to_all | solution.py:36
  43.0 0.3 fusion.4
  43.3 1.8 %collective-permute-start.5 = (f32[32,128]{1,0:T(8,128)S(1)}, f32[32,128]{1,0:T(8,128)S(1)}, u32[]{:S(2)}, u32[]{:S(2)}) collective-permute-start(f32[32,128]{1,0:T(8,128)S(1)} %fusion.4), channel_id=1, source_target_pairs={{0,4},{2,6},{4,0},{6,2},{1,5},{3,7},{5,1},{7,3},{8,12},{10,14},{12... | collective-permute-start | bytes 49160 | tf_op jit(solution)/shard_map/ppermute | solution.py:41
  45.0 0.9 %collective-permute-start.6 = (f32[32,128]{1,0:T(8,128)S(1)}, f32[32,128]{1,0:T(8,128)S(1)}, u32[]{:S(2)}, u32[]{:S(2)}) collective-permute-start(f32[32,128]{1,0:T(8,128)S(1)} %fusion.4), channel_id=1, source_target_pairs={{0,6},{2,4},{4,2},{6,0},{1,7},{3,5},{5,3},{7,1},{8,14},{10,12},{12... | collective-permute-start | bytes 49160 | tf_op jit(solution)/shard_map/ppermute | solution.py:41
  46.0 1.4 %collective-permute-done.5 = f32[32,128]{1,0:T(8,128)S(1)} collective-permute-done((f32[32,128]{1,0:T(8,128)S(1)}, f32[32,128]{1,0:T(8,128)S(1)}, u32[]{:S(2)}, u32[]{:S(2)}) %collective-permute-start.5) | collective-permute-done | bytes 16416 | tf_op jit(solution)/shard_map/ppermute | solution.py:41
  47.4 1.4 %collective-permute-done.6 = f32[32,128]{1,0:T(8,128)S(1)} collective-permute-done((f32[32,128]{1,0:T(8,128)S(1)}, f32[32,128]{1,0:T(8,128)S(1)}, u32[]{:S(2)}, u32[]{:S(2)}) %collective-permute-start.6) | collective-permute-done | bytes 16416 | tf_op jit(solution)/shard_map/ppermute | solution.py:41
  48.8 0.6 %add_add_fusion = f32[32,128]{1,0:T(8,128)} fusion(f32[32,128]{1,0:T(8,128)S(1)} %collective-permute-done.7, f32[32,128]{1,0:T(8,128)S(1)} %fusion.4, f32[32,128]{1,0:T(8,128)S(1)} %collective-permute-done.5, f32[32,128]{1,0:T(8,128)S(1)} %collective-permute-done.6), kind=kLoop, calls=%fused_computation.60 | loop fusion | flops 12288 | bytes 81920 | tf_op jit(solution)/shard_map/add | solution.py:91
  (43 shorter events, 0.6 us)
Async XLA Ops:
  0.0 1.8 %copy-start = (bf16[1,256,3584]{2,1,0:T(8,128)(2,1)S(1)}, bf16[1,256,3584]{2,1,0:T(8,128)(2,1)}, u32[]{:S(2)}) copy-start(bf16[1,256,3584]{2,1,0:T(8,128)(2,1)} %param.10) | copy-start | bytes 5505028
  0.0 2.5 %copy-start.1 = (bf16[1,256,3584]{2,1,0:T(8,128)(2,1)S(1)}, bf16[1,256,3584]{2,1,0:T(8,128)(2,1)}, u32[]{:S(2)}) copy-start(bf16[1,256,3584]{2,1,0:T(8,128)(2,1)} %param.11) | copy-start | bytes 5505028
  1.8 1.4 %copy-start.2 = (bf16[1,256,1024]{2,1,0:T(8,128)(2,1)S(1)}, bf16[1,256,1024]{2,1,0:T(8,128)(2,1)}, u32[]{:S(2)}) copy-start(bf16[1,256,1024]{2,1,0:T(8,128)(2,1)} %param.12) | copy-start | bytes 1572868
  1.8 1.4 %copy-start.5 = (bf16[1024,64]{0,1:T(8,128)(2,1)S(1)}, bf16[1024,64]{0,1:T(8,128)(2,1)}, u32[]{:S(2)}) copy-start(bf16[1024,64]{0,1:T(8,128)(2,1)} %param.16) | copy-start | bytes 393220
  2.5 1.1 %copy-start.3 = (bf16[1,256,1024]{2,1,0:T(8,128)(2,1)S(1)}, bf16[1,256,1024]{2,1,0:T(8,128)(2,1)}, u32[]{:S(2)}) copy-start(bf16[1,256,1024]{2,1,0:T(8,128)(2,1)} %param.9) | copy-start | bytes 1572868
  2.5 1.1 %copy-start.6 = (bf16[1024,64]{0,1:T(8,128)(2,1)S(1)}, bf16[1024,64]{0,1:T(8,128)(2,1)}, u32[]{:S(2)}) copy-start(bf16[1024,64]{0,1:T(8,128)(2,1)} %param.13) | copy-start | bytes 393220
  3.9 15.6 %copy-start.4 = (bf16[128,1024]{1,0:T(8,128)(2,1)S(1)}, bf16[128,1024]{1,0:T(8,128)(2,1)}, u32[]{:S(2)}) copy-start(bf16[128,1024]{1,0:T(8,128)(2,1)} %param.17) | copy-start | bytes 786436
  4.0 5.3 %collective-permute-start.2 = (bf16[128,256]{1,0:T(8,128)(2,1)S(1)}, bf16[128,256]{1,0:T(8,128)(2,1)S(1)}, u32[]{:S(2)}, u32[]{:S(2)}) collective-permute-start(bf16[128,256]{1,0:T(8,128)(2,1)S(1)} %pad_maximum_fusion.8), channel_id=1, source_target_pairs={{0,6},{2,4},{4,2},{6,0},{1,7},{3,5},{5,3},{7,1},{8,14},{10,12},{12... | collective-permute-start | bytes 196616 | tf_op jit(solution)/shard_map/ppermute | solution.py:41
  7.7 4.7 %collective-permute-start.1 = (bf16[128,256]{1,0:T(8,128)(2,1)S(1)}, bf16[128,256]{1,0:T(8,128)(2,1)S(1)}, u32[]{:S(2)}, u32[]{:S(2)}) collective-permute-start(bf16[128,256]{1,0:T(8,128)(2,1)S(1)} %pad_maximum_fusion.7), channel_id=1, source_target_pairs={{0,4},{2,6},{4,0},{6,2},{1,5},{3,7},{5,1},{7,3},{8,12},{10,14},{12... | collective-permute-start | bytes 196616 | tf_op jit(solution)/shard_map/ppermute | solution.py:41
  8.0 4.4 %collective-permute-start = (bf16[128,256]{1,0:T(8,128)(2,1)S(1)}, bf16[128,256]{1,0:T(8,128)(2,1)S(1)}, u32[]{:S(2)}, u32[]{:S(2)}) collective-permute-start(bf16[128,256]{1,0:T(8,128)(2,1)S(1)} %pad_maximum_fusion.6), channel_id=1, source_target_pairs={{0,2},{2,0},{4,6},{6,4},{1,3},{3,1},{5,7},{7,5},{8,10},{10,8},{12,... | collective-permute-start | bytes 196616 | tf_op jit(solution)/shard_map/ppermute | solution.py:41
  12.6 9.0 %collective-permute-start.3 = (f32[96,256]{1,0:T(8,128)S(1)}, f32[96,256]{1,0:T(8,128)S(1)}, u32[]{:S(2)}, u32[]{:S(2)}) collective-permute-start(f32[96,256]{1,0:T(8,128)S(1)} %fusion.21), channel_id=1, source_target_pairs={{0,1},{1,0},{2,3},{3,2},{4,5},{5,4},{6,7},{7,6},{8,9},{9,8},{10,11... | collective-permute-start | bytes 294920 | tf_op jit(solution)/shard_map/ppermute | solution.py:41
  19.5 14.7 %collective-permute-start.4 = (bf16[128,1024]{1,0:T(8,128)(2,1)S(1)}, bf16[128,1024]{1,0:T(8,128)(2,1)S(1)}, u32[]{:S(2)}, u32[]{:S(2)}) collective-permute-start(bf16[128,1024]{1,0:T(8,128)(2,1)S(1)} %copy-done.4), channel_id=1, source_target_pairs={{0,1},{1,0},{2,3},{3,2},{4,5},{5,4},{6,7},{7,6},{8,9},{9,8},{10,11... | collective-permute-start | bytes 786440 | tf_op jit(solution)/shard_map/ppermute | solution.py:41
  22.6 20.4 %all-to-all-start = ((bf16[32,16,128]{2,1,0:T(8,128)(2,1)}), bf16[32,16,128]{2,1,0:T(8,128)(2,1)S(1)}, u32[]{:S(2)}, u32[]{:S(2)}) async-start(bf16[32,16,128]{2,1,0:T(8,128)(2,1)} %broadcast_in_dim.3), calls=%async_computation | async-start | bytes 262144 | tf_op jit(solution)/shard_map/all_to_all | solution.py:36
  43.3 4.1 %collective-permute-start.5 = (f32[32,128]{1,0:T(8,128)S(1)}, f32[32,128]{1,0:T(8,128)S(1)}, u32[]{:S(2)}, u32[]{:S(2)}) collective-permute-start(f32[32,128]{1,0:T(8,128)S(1)} %fusion.4), channel_id=1, source_target_pairs={{0,4},{2,6},{4,0},{6,2},{1,5},{3,7},{5,1},{7,3},{8,12},{10,14},{12... | collective-permute-start | bytes 49160 | tf_op jit(solution)/shard_map/ppermute | solution.py:41
  45.0 3.8 %collective-permute-start.6 = (f32[32,128]{1,0:T(8,128)S(1)}, f32[32,128]{1,0:T(8,128)S(1)}, u32[]{:S(2)}, u32[]{:S(2)}) collective-permute-start(f32[32,128]{1,0:T(8,128)S(1)} %fusion.4), channel_id=1, source_target_pairs={{0,6},{2,4},{4,2},{6,0},{1,7},{3,5},{5,3},{7,1},{8,14},{10,12},{12... | collective-permute-start | bytes 49160 | tf_op jit(solution)/shard_map/ppermute | solution.py:41
  45.9 2.9 %collective-permute-start.7 = (f32[32,128]{1,0:T(8,128)S(1)}, f32[32,128]{1,0:T(8,128)S(1)}, u32[]{:S(2)}, u32[]{:S(2)}) collective-permute-start(f32[32,128]{1,0:T(8,128)S(1)} %fusion.4), channel_id=1, source_target_pairs={{0,2},{2,0},{4,6},{6,4},{1,3},{3,1},{5,7},{7,5},{8,10},{10,8},{12,... | collective-permute-start | bytes 49160 | tf_op jit(solution)/shard_map/ppermute | solution.py:41

commit v11 on v9

--- a/solution.py
+++ b/solution.py
@@ -69,12 +69,12 @@
     for outs, ins in ((up_out, up_in), (down_out, down_in)):
         for k in range(rank // (zhs * rows)):
             pieces.append(jnp.concatenate([outs[k * zhs * rows : (k + 1) * zhs * rows], ins], axis=0))
-    pieces = jnp.stack(pieces)
     y = lax.axis_index("y")
-    piece = lambda k: lax.dynamic_index_in_dim(pieces, k, 0, keepdims=False)
+    pick = lambda table, k: lax.dynamic_index_in_dim(table, k, 0, keepdims=False)
     outer = zhs * rows
-    half = piece(y) + sum(
-        from_sent(swap(to_send(piece(y ^ mask), outer), "y", mask), outer) for mask in (1, 3, 2)
+    sent = jnp.stack([to_send(piece, outer) for piece in pieces])
+    half = pick(jnp.stack(pieces), y) + sum(
+        from_sent(swap(pick(sent, y ^ mask), "y", mask), outer) for mask in (1, 3, 2)
     )
     sums = half + swap(half, "zh", 1)
     outs, ins = sums[:outer], sums[outer:]

time: 49.1 us -> 49 us (level)
  no operation moved by 1% of the time
where the time goes in v11:
time: 49 us; the launch traced here: 48.8 us
  starting transfers between devices  25.3 us (52%)
  waiting for transfers between devices  17.3 us (35%)
  matrix products  2.36 us (5%)
  other arithmetic  2.31 us (5%)
  local copies, waits for them, and re-layouts  1.26 us (3%)
    ppermute x8, starting transfers between devices, swap(): return lax.ppermute(values, axis, [(k, k ^ mask) for k in range(size)])  13.7 us
    all_to_all x1, starting transfers between devices, exchange(): return lax.all_to_all(pieces, axes, split_axis=0, concat_axis=0, tiled=True)  11.6 us
    all_to_all x1, waiting for transfers between devices, exchange(): return lax.all_to_all(pieces, axes, split_axis=0, concat_axis=0, tiled=True)  8.77 us
    ppermute x8, waiting for transfers between devices, swap(): return lax.ppermute(values, axis, [(k, k ^ mask) for k in range(size)])  8.55 us
    dot_general x4, matrix products, project_columns(): lax.dot_general(proj, acts[0], (((0,), (1,)), ((), ())), preferred_elemen...  1.9 us
    concatenate x1, other arithmetic, per_device(): jnp.concatenate([up_out_proj, down_in_proj], axis=1)  1.37 us
  transfers between devices with their start and end apart: 9, of which 6 were waited for; matrix products, arithmetic and copies ran while one was open for 2% of the time, Pallas kernels for 0%

profile of v11, /device:TPU:1, one launch (start us, length us, event | category | flops | bytes accessed | tf_op | source)
XLA Modules:
  0.0 48.8 jit_solution(9471628746573952762)
XLA Ops:
  0.0 1.4 %pad_maximum_fusion = bf16[3584,128]{0,1:T(8,128)(2,1)S(1)} fusion(bf16[3584,64]{0,1:T(8,128)(2,1)} %param.15, bf16[3584,64]{0,1:T(8,128)(2,1)} %param.14), kind=kLoop, calls=%fused_computation.5 | loop fusion | flops 1835008 | bytes 1835008 | tf_op jit(solution)/shard_map/concatenate | solution.py:63
  1.4 0.4 copy-done
  1.8 0.7 %fusion.2 = f32[64,256]{1,0:T(8,128)S(1)} fusion(bf16[1,256,3584]{2,1,0:T(8,128)(2,1)S(1)} %copy-done, bf16[3584,128]{0,1:T(8,128)(2,1)S(1)} %pad_maximum_fusion), kind=kOutput, calls=%fused_computation.2 | convolution fusion | flops 117440512 | bytes 2359296 | tf_op jit(solution)/shard_map/dot_general | solution.py:13
  2.5 0.7 %fusion = f32[64,256]{1,0:T(8,128)S(1)} fusion(bf16[1,256,3584]{2,1,0:T(8,128)(2,1)S(1)} %copy-done.1, bf16[3584,128]{0,1:T(8,128)(2,1)S(1)} %pad_maximum_fusion), kind=kOutput, calls=%fused_computation | convolution fusion | flops 117440512 | bytes 2359296 | tf_op jit(solution)/shard_map/dot_general | solution.py:13
  3.2 0.3 fusion.8
  3.6 0.3 fusion.10
  4.0 3.8 %collective-permute-start.2 = (bf16[128,256]{1,0:T(8,128)(2,1)S(1)}, bf16[128,256]{1,0:T(8,128)(2,1)S(1)}, u32[]{:S(2)}, u32[]{:S(2)}) collective-permute-start(bf16[128,256]{1,0:T(8,128)(2,1)S(1)} %get-tuple-element.7), channel_id=1, source_target_pairs={{0,4},{2,6},{4,0},{6,2},{1,5},{3,7},{5,1},{7,3},{8,12},{10,14},{12... | collective-permute-start | bytes 196616 | tf_op jit(solution)/shard_map/ppermute | solution.py:41
  7.8 0.8 %collective-permute-start.1 = (bf16[128,256]{1,0:T(8,128)(2,1)S(1)}, bf16[128,256]{1,0:T(8,128)(2,1)S(1)}, u32[]{:S(2)}, u32[]{:S(2)}) collective-permute-start(bf16[128,256]{1,0:T(8,128)(2,1)S(1)} %get-tuple-element.8), channel_id=1, source_target_pairs={{0,6},{2,4},{4,2},{6,0},{1,7},{3,5},{5,3},{7,1},{8,14},{10,12},{12... | collective-permute-start | bytes 196616 | tf_op jit(solution)/shard_map/ppermute | solution.py:41
  8.6 0.8 %collective-permute-done.2 = bf16[128,256]{1,0:T(8,128)(2,1)S(1)} collective-permute-done((bf16[128,256]{1,0:T(8,128)(2,1)S(1)}, bf16[128,256]{1,0:T(8,128)(2,1)S(1)}, u32[]{:S(2)}, u32[]{:S(2)}) %collective-permute-start.2) | collective-permute-done | bytes 65568 | tf_op jit(solution)/shard_map/ppermute | solution.py:41
  9.5 3.3 %collective-permute-done.1 = bf16[128,256]{1,0:T(8,128)(2,1)S(1)} collective-permute-done((bf16[128,256]{1,0:T(8,128)(2,1)S(1)}, bf16[128,256]{1,0:T(8,128)(2,1)S(1)}, u32[]{:S(2)}, u32[]{:S(2)}) %collective-permute-start.1) | collective-permute-done | bytes 65568 | tf_op jit(solution)/shard_map/ppermute | solution.py:41
  13.0 6.3 %collective-permute-start.3 = (f32[96,256]{1,0:T(8,128)S(1)}, f32[96,256]{1,0:T(8,128)S(1)}, u32[]{:S(2)}, u32[]{:S(2)}) collective-permute-start(f32[96,256]{1,0:T(8,128)S(1)} %fusion.24), channel_id=1, source_target_pairs={{0,1},{1,0},{2,3},{3,2},{4,5},{5,4},{6,7},{7,6},{8,9},{9,8},{10,11... | collective-permute-start | bytes 294920 | tf_op jit(solution)/shard_map/ppermute | solution.py:41
  19.3 0.1 collective-permute-start.4
  19.4 2.0 %collective-permute-done.3 = f32[96,256]{1,0:T(8,128)S(1)} collective-permute-done((f32[96,256]{1,0:T(8,128)S(1)}, f32[96,256]{1,0:T(8,128)S(1)}, u32[]{:S(2)}, u32[]{:S(2)}) %collective-permute-start.3) | collective-permute-done | bytes 98336 | tf_op jit(solution)/shard_map/ppermute | solution.py:41
  21.5 0.2 convolution_convert_fusion
  21.8 0.7 %broadcast_in_dim.3 = bf16[32,16,128]{2,1,0:T(8,128)(2,1)} broadcast(bf16[16,128]{1,0:T(8,128)(2,1)S(1)} %pad_maximum_fusion.5), dimensions={1,2} | broadcast | bytes 135168 | tf_op jit(solution)/shard_map/broadcast_in_dim | solution.py:45
  22.4 11.6 %all-to-all-start = ((bf16[32,16,128]{2,1,0:T(8,128)(2,1)}), bf16[32,16,128]{2,1,0:T(8,128)(2,1)S(1)}, u32[]{:S(2)}, u32[]{:S(2)}) async-start(bf16[32,16,128]{2,1,0:T(8,128)(2,1)} %broadcast_in_dim.3), calls=%async_computation | async-start | bytes 262144 | tf_op jit(solution)/shard_map/all_to_all | solution.py:36
  34.1 8.8 %all-to-all-done = bf16[32,16,128]{2,1,0:T(8,128)(2,1)S(1)} async-done(((bf16[32,16,128]{2,1,0:T(8,128)(2,1)}), bf16[32,16,128]{2,1,0:T(8,128)(2,1)S(1)}, u32[]{:S(2)}, u32[]{:S(2)}) %all-to-all-start) | async-done | bytes 131104 | tf_op jit(solution)/shard_map/all_to_all | solution.py:36
  42.8 0.3 fusion.4
  43.1 1.2 %collective-permute-start.5 = (f32[32,128]{1,0:T(8,128)S(1)}, f32[32,128]{1,0:T(8,128)S(1)}, u32[]{:S(2)}, u32[]{:S(2)}) collective-permute-start(f32[32,128]{1,0:T(8,128)S(1)} %fusion.4), channel_id=1, source_target_pairs={{0,4},{2,6},{4,0},{6,2},{1,5},{3,7},{5,1},{7,3},{8,12},{10,14},{12... | collective-permute-start | bytes 49160 | tf_op jit(solution)/shard_map/ppermute | solution.py:41
  44.4 1.2 %collective-permute-start.6 = (f32[32,128]{1,0:T(8,128)S(1)}, f32[32,128]{1,0:T(8,128)S(1)}, u32[]{:S(2)}, u32[]{:S(2)}) collective-permute-start(f32[32,128]{1,0:T(8,128)S(1)} %fusion.4), channel_id=1, source_target_pairs={{0,6},{2,4},{4,2},{6,0},{1,7},{3,5},{5,3},{7,1},{8,14},{10,12},{12... | collective-permute-start | bytes 49160 | tf_op jit(solution)/shard_map/ppermute | solution.py:41
  45.5 0.3 collective-permute-start.7
  45.8 1.4 %collective-permute-done.5 = f32[32,128]{1,0:T(8,128)S(1)} collective-permute-done((f32[32,128]{1,0:T(8,128)S(1)}, f32[32,128]{1,0:T(8,128)S(1)}, u32[]{:S(2)}, u32[]{:S(2)}) %collective-permute-start.5) | collective-permute-done | bytes 16416 | tf_op jit(solution)/shard_map/ppermute | solution.py:41
  47.2 0.9 %collective-permute-done.6 = f32[32,128]{1,0:T(8,128)S(1)} collective-permute-done((f32[32,128]{1,0:T(8,128)S(1)}, f32[32,128]{1,0:T(8,128)S(1)}, u32[]{:S(2)}, u32[]{:S(2)}) %collective-permute-start.6) | collective-permute-done | bytes 16416 | tf_op jit(solution)/shard_map/ppermute | solution.py:41
  48.2 0.6 %add_add_fusion = f32[32,128]{1,0:T(8,128)} fusion(f32[32,128]{1,0:T(8,128)S(1)} %collective-permute-done.7, f32[32,128]{1,0:T(8,128)S(1)} %fusion.4, f32[32,128]{1,0:T(8,128)S(1)} %collective-permute-done.5, f32[32,128]{1,0:T(8,128)S(1)} %collective-permute-done.6), kind=kLoop, calls=%fused_computation.72 | loop fusion | flops 12288 | bytes 81920 | tf_op jit(solution)/shard_map/add | solution.py:91
  (40 shorter events, 0.5 us)
Async XLA Ops:
  0.0 1.8 %copy-start = (bf16[1,256,3584]{2,1,0:T(8,128)(2,1)S(1)}, bf16[1,256,3584]{2,1,0:T(8,128)(2,1)}, u32[]{:S(2)}) copy-start(bf16[1,256,3584]{2,1,0:T(8,128)(2,1)} %param.10) | copy-start | bytes 5505028
  0.0 2.5 %copy-start.1 = (bf16[1,256,3584]{2,1,0:T(8,128)(2,1)S(1)}, bf16[1,256,3584]{2,1,0:T(8,128)(2,1)}, u32[]{:S(2)}) copy-start(bf16[1,256,3584]{2,1,0:T(8,128)(2,1)} %param.11) | copy-start | bytes 5505028
  1.8 1.4 %copy-start.2 = (bf16[1,256,1024]{2,1,0:T(8,128)(2,1)S(1)}, bf16[1,256,1024]{2,1,0:T(8,128)(2,1)}, u32[]{:S(2)}) copy-start(bf16[1,256,1024]{2,1,0:T(8,128)(2,1)} %param.12) | copy-start | bytes 1572868
  1.8 1.4 %copy-start.5 = (bf16[1024,64]{0,1:T(8,128)(2,1)S(1)}, bf16[1024,64]{0,1:T(8,128)(2,1)}, u32[]{:S(2)}) copy-start(bf16[1024,64]{0,1:T(8,128)(2,1)} %param.16) | copy-start | bytes 393220
  2.5 1.1 %copy-start.3 = (bf16[1,256,1024]{2,1,0:T(8,128)(2,1)S(1)}, bf16[1,256,1024]{2,1,0:T(8,128)(2,1)}, u32[]{:S(2)}) copy-start(bf16[1,256,1024]{2,1,0:T(8,128)(2,1)} %param.9) | copy-start | bytes 1572868
  2.5 1.1 %copy-start.6 = (bf16[1024,64]{0,1:T(8,128)(2,1)S(1)}, bf16[1024,64]{0,1:T(8,128)(2,1)}, u32[]{:S(2)}) copy-start(bf16[1024,64]{0,1:T(8,128)(2,1)} %param.13) | copy-start | bytes 393220
  3.9 15.4 %copy-start.4 = (bf16[128,1024]{1,0:T(8,128)(2,1)S(1)}, bf16[128,1024]{1,0:T(8,128)(2,1)}, u32[]{:S(2)}) copy-start(bf16[128,1024]{1,0:T(8,128)(2,1)} %param.17) | copy-start | bytes 786436
  4.0 5.5 %collective-permute-start.2 = (bf16[128,256]{1,0:T(8,128)(2,1)S(1)}, bf16[128,256]{1,0:T(8,128)(2,1)S(1)}, u32[]{:S(2)}, u32[]{:S(2)}) collective-permute-start(bf16[128,256]{1,0:T(8,128)(2,1)S(1)} %get-tuple-element.7), channel_id=1, source_target_pairs={{0,4},{2,6},{4,0},{6,2},{1,5},{3,7},{5,1},{7,3},{8,12},{10,14},{12... | collective-permute-start | bytes 196616 | tf_op jit(solution)/shard_map/ppermute | solution.py:41
  7.8 5.0 %collective-permute-start.1 = (bf16[128,256]{1,0:T(8,128)(2,1)S(1)}, bf16[128,256]{1,0:T(8,128)(2,1)S(1)}, u32[]{:S(2)}, u32[]{:S(2)}) collective-permute-start(bf16[128,256]{1,0:T(8,128)(2,1)S(1)} %get-tuple-element.8), channel_id=1, source_target_pairs={{0,6},{2,4},{4,2},{6,0},{1,7},{3,5},{5,3},{7,1},{8,14},{10,12},{12... | collective-permute-start | bytes 196616 | tf_op jit(solution)/shard_map/ppermute | solution.py:41
  8.6 4.3 %collective-permute-start = (bf16[128,256]{1,0:T(8,128)(2,1)S(1)}, bf16[128,256]{1,0:T(8,128)(2,1)S(1)}, u32[]{:S(2)}, u32[]{:S(2)}) collective-permute-start(bf16[128,256]{1,0:T(8,128)(2,1)S(1)} %get-tuple-element.9), channel_id=1, source_target_pairs={{0,2},{2,0},{4,6},{6,4},{1,3},{3,1},{5,7},{7,5},{8,10},{10,8},{12,... | collective-permute-start | bytes 196616 | tf_op jit(solution)/shard_map/ppermute | solution.py:41
  13.0 8.4 %collective-permute-start.3 = (f32[96,256]{1,0:T(8,128)S(1)}, f32[96,256]{1,0:T(8,128)S(1)}, u32[]{:S(2)}, u32[]{:S(2)}) collective-permute-start(f32[96,256]{1,0:T(8,128)S(1)} %fusion.24), channel_id=1, source_target_pairs={{0,1},{1,0},{2,3},{3,2},{4,5},{5,4},{6,7},{7,6},{8,9},{9,8},{10,11... | collective-permute-start | bytes 294920 | tf_op jit(solution)/shard_map/ppermute | solution.py:41
  19.3 14.7 %collective-permute-start.4 = (bf16[128,1024]{1,0:T(8,128)(2,1)S(1)}, bf16[128,1024]{1,0:T(8,128)(2,1)S(1)}, u32[]{:S(2)}, u32[]{:S(2)}) collective-permute-start(bf16[128,1024]{1,0:T(8,128)(2,1)S(1)} %copy-done.4), channel_id=1, source_target_pairs={{0,1},{1,0},{2,3},{3,2},{4,5},{5,4},{6,7},{7,6},{8,9},{9,8},{10,11... | collective-permute-start | bytes 786440 | tf_op jit(solution)/shard_map/ppermute | solution.py:41
  22.4 20.4 %all-to-all-start = ((bf16[32,16,128]{2,1,0:T(8,128)(2,1)}), bf16[32,16,128]{2,1,0:T(8,128)(2,1)S(1)}, u32[]{:S(2)}, u32[]{:S(2)}) async-start(bf16[32,16,128]{2,1,0:T(8,128)(2,1)} %broadcast_in_dim.3), calls=%async_computation | async-start | bytes 262144 | tf_op jit(solution)/shard_map/all_to_all | solution.py:36
  43.1 4.1 %collective-permute-start.5 = (f32[32,128]{1,0:T(8,128)S(1)}, f32[32,128]{1,0:T(8,128)S(1)}, u32[]{:S(2)}, u32[]{:S(2)}) collective-permute-start(f32[32,128]{1,0:T(8,128)S(1)} %fusion.4), channel_id=1, source_target_pairs={{0,4},{2,6},{4,0},{6,2},{1,5},{3,7},{5,1},{7,3},{8,12},{10,14},{12... | collective-permute-start | bytes 49160 | tf_op jit(solution)/shard_map/ppermute | solution.py:41
  44.4 3.8 %collective-permute-start.6 = (f32[32,128]{1,0:T(8,128)S(1)}, f32[32,128]{1,0:T(8,128)S(1)}, u32[]{:S(2)}, u32[]{:S(2)}) collective-permute-start(f32[32,128]{1,0:T(8,128)S(1)} %fusion.4), channel_id=1, source_target_pairs={{0,6},{2,4},{4,2},{6,0},{1,7},{3,5},{5,3},{7,1},{8,14},{10,12},{12... | collective-permute-start | bytes 49160 | tf_op jit(solution)/shard_map/ppermute | solution.py:41
  45.5 2.6 %collective-permute-start.7 = (f32[32,128]{1,0:T(8,128)S(1)}, f32[32,128]{1,0:T(8,128)S(1)}, u32[]{:S(2)}, u32[]{:S(2)}) collective-permute-start(f32[32,128]{1,0:T(8,128)S(1)} %fusion.4), channel_id=1, source_target_pairs={{0,2},{2,0},{4,6},{6,4},{1,3},{3,1},{5,7},{7,5},{8,10},{10,8},{12,... | collective-permute-start | bytes 49160 | tf_op jit(solution)/shard_map/ppermute | solution.py:41
